TPU v7x, 128 devices: a whole 4x4x4 slice. The times are simulated.
128 devices in a mesh: batch: 8 (over x, core), seq: 16 (over z, y).
Axes of the slice: x: 4, y: 4, z: 4, core: 2. Of those that a mesh axis runs over, the one named last changes fastest.
Arguments:
- latents: bfloat16 [8, 64, 1024], P('batch'), may hold values from -16 to 16
- frames: bfloat16 [512, 128, 1152], P(('batch', 'seq')), may hold values from -40 to 40
- counts: int32 [512], P(('batch', 'seq')), may hold values from 1 to 128, as said below
- groups: int32 [512], P(('batch', 'seq')), may hold values from 0 to 7, as said below
- w_query: bfloat16 [1024, 1024], replicated, may hold values from -0.5 to 0.5
- w_kv: bfloat16 [1152, 2048], replicated, may hold values from -0.5 to 0.5
- w_out: bfloat16 [1024, 1024], replicated, may hold values from -0.1875 to 0.1875
- d_out: bfloat16 [8, 64, 1024], P('batch'), may hold values from -6 to 6
Outputs:
- out: bfloat16 [8, 64, 1024], P('batch')
- d_latents: bfloat16 [8, 64, 1024], P('batch')
- grad_query: float32 [1024, 1024], P('seq')
- grad_outproj: float32 [1024, 1024], P('seq')
- grad_kv: float32 [1152, 2048], P(('batch', 'seq'))
Inputs may be any that keep to these rules, and one draw needn't show every extreme that they name: Rows 0 to counts[i] - 1 of block i hold tokens, the rest is padding; the first block of every source device is full. `groups`: the blocks of one source device name no group more than 2 times. At every seq index one group is named exactly 2 times by every source device at that seq index, and every group is that group at some seq index.
All inputs are finite; a program needn't handle non-finite values.
Results may differ from a plain program's by a relative error of at most 0.0055.
The roundings to bfloat16 on the way count: a program that leaves them out, or rounds other values in their place, can miss the bound.
Values may be sent and summed in bfloat16 or wider, within the bound.
No kernel may reach another device: no remote copies, remote signals or barrier semaphores. Data moves between devices by JAX's collectives and lax.ppermute only.
A program may use at most 128 MiB of HBM per device.

v0:
```python
import jax
import jax.numpy as jnp
from jax import lax
from jax.sharding import PartitionSpec as P

H = 16
CAP = 2


epsilon = 1e-06


def rms_rows(values):
    return values * lax.rsqrt(jnp.mean(values * values, axis=-1, keepdims=True) + epsilon)


def rms_back(values, grads):
    factor = lax.rsqrt(jnp.mean(values * values, axis=-1, keepdims=True) + epsilon)
    normed = values * factor
    return factor * (grads - normed * jnp.mean(grads * normed, axis=-1, keepdims=True))


def normalize(values):
    return rms_rows(values.astype(jnp.float32)).astype(jnp.bfloat16)


def local(latents, frames, counts, groups, w_query, w_kv, w_out, d_out):
    group_count = lax.axis_size("batch")
    seq_count = lax.axis_size("seq")
    blocks = frames.shape[0]
    block_rows = frames.shape[1]
    feature = frames.shape[2]
    model_width = w_query.shape[0]
    head_dim = model_width // H
    score_scale = head_dim ** (-0.5)
    block_order = jnp.arange(blocks, dtype=jnp.int32)
    same_group = (groups[None, :] == groups[:, None]) & (
        block_order[None, :] < block_order[:, None]
    )
    slot_index = jnp.sum(same_group.astype(jnp.int32), axis=1)
    placed = (groups[None, None, :] == jnp.arange(group_count, dtype=jnp.int32)[:, None, None]) & (
        slot_index[None, None, :] == jnp.arange(CAP, dtype=jnp.int32)[None, :, None]
    )
    placing = placed.astype(jnp.bfloat16)
    send_counts = jnp.sum(jnp.where(placed, counts[None, None, :], 0), axis=2)
    outgoing = jnp.einsum(
        "gci,ird->gcrd", placing, frames, preferred_element_type=jnp.float32
    ).astype(jnp.bfloat16)
    arrived = lax.all_to_all(outgoing, "batch", split_axis=0, concat_axis=0, tiled=True)
    arrived_counts = lax.all_to_all(send_counts, "batch", split_axis=0, concat_axis=0, tiled=True)
    normed_here = normalize(arrived)
    projected_here = jnp.einsum(
        "gcrf,fe->gcre", normed_here, w_kv, preferred_element_type=jnp.float32
    ).astype(jnp.bfloat16)
    slot_rows = projected_here.shape[0] * projected_here.shape[1] * block_rows
    flat_pairs = projected_here.reshape(slot_rows, 2 * model_width)
    usable = (
        jnp.arange(block_rows, dtype=jnp.int32)[None, None, :] < arrived_counts[:, :, None]
    ).reshape(slot_rows)
    key_heads = flat_pairs[:, :model_width].reshape(slot_rows, H, head_dim)
    value_heads = flat_pairs[:, model_width:].reshape(slot_rows, H, head_dim)
    latent = latents[0].astype(jnp.float32)
    latent_count = latent.shape[0]
    normed_latent = rms_rows(latent).astype(jnp.bfloat16)
    queries = jnp.dot(normed_latent, w_query, preferred_element_type=jnp.float32).astype(
        jnp.bfloat16
    )
    query_heads = queries.reshape(latent_count, H, head_dim)
    scores = (
        jnp.einsum("lhd,thd->hlt", query_heads, key_heads, preferred_element_type=jnp.float32)
        * score_scale
    )
    masked = jnp.where(usable[None, None, :], scores, -1e30)
    row_top = lax.pmax(jnp.max(masked, axis=2), "seq")
    raw_weights = jnp.where(usable[None, None, :], jnp.exp(masked - row_top[:, :, None]), 0.0)
    totals = lax.psum(jnp.sum(raw_weights, axis=2), "seq")
    weights = raw_weights / totals[:, :, None]
    weights_b = weights.astype(jnp.bfloat16)
    partial_value = jnp.einsum(
        "hlt,thd->lhd", weights_b, value_heads, preferred_element_type=jnp.float32
    ).reshape(latent_count, model_width)
    attended = lax.psum(partial_value, "seq")
    mixed_b = attended.astype(jnp.bfloat16)
    result = (latent + jnp.dot(mixed_b, w_out, preferred_element_type=jnp.float32)).astype(
        jnp.bfloat16
    )
    cotangent = d_out[0]
    d_mixed = jnp.dot(cotangent, w_out.T, preferred_element_type=jnp.float32).astype(jnp.bfloat16)
    d_heads = d_mixed.reshape(latent_count, H, head_dim)
    d_weights = jnp.einsum("lhd,thd->hlt", d_heads, value_heads, preferred_element_type=jnp.float32)
    row_delta = jnp.einsum(
        "lhd,lhd->hl", d_heads.astype(jnp.float32), attended.reshape(latent_count, H, head_dim)
    )
    d_scores = (weights * (d_weights - row_delta[:, :, None]) * score_scale).astype(jnp.bfloat16)
    query_term = jnp.einsum(
        "hlt,thd->lhd", d_scores, key_heads, preferred_element_type=jnp.float32
    ).reshape(latent_count, model_width)
    d_query = lax.psum(query_term, "seq").astype(jnp.bfloat16)
    d_keys = jnp.einsum(
        "hlt,lhd->thd", d_scores, query_heads, preferred_element_type=jnp.float32
    ).reshape(slot_rows, model_width)
    d_values = jnp.einsum(
        "hlt,lhd->thd", weights_b, d_heads, preferred_element_type=jnp.float32
    ).reshape(slot_rows, model_width)
    d_pairs = jnp.concatenate([d_keys, d_values], axis=1).astype(jnp.bfloat16)
    col_share = model_width // seq_count
    offset = lax.axis_index("seq") * col_share
    latent_cols = lax.dynamic_slice_in_dim(normed_latent, offset, col_share, 1)
    mixed_cols = lax.dynamic_slice_in_dim(mixed_b, offset, col_share, 1)
    query_part = jnp.dot(latent_cols.T, d_query, preferred_element_type=jnp.float32)
    outproj_part = jnp.dot(mixed_cols.T, cotangent, preferred_element_type=jnp.float32)
    grad_query, grad_outproj = lax.psum((query_part, outproj_part), "batch")
    d_normed = jnp.dot(d_query, w_query.T, preferred_element_type=jnp.float32)
    d_latent = (cotangent.astype(jnp.float32) + rms_back(latent, d_normed)).astype(jnp.bfloat16)
    source_rows = normed_here.reshape(slot_rows, feature)
    grad_kv = lax.psum_scatter(
        lax.dot_general(
            source_rows, d_pairs, (((0,), (0,)), ((), ())), preferred_element_type=jnp.float32
        ),
        ("batch", "seq"),
        scatter_dimension=0,
        tiled=True,
    )
    return (result[None], d_latent[None], grad_query, grad_outproj, grad_kv)


def solution(mesh):
    in_specs = (
        P("batch", None, None),
        P(("batch", "seq"), None, None),
        P(("batch", "seq")),
        P(("batch", "seq")),
        P(),
        P(),
        P(),
        P("batch", None, None),
    )
    out_specs = (
        P("batch", None, None),
        P("batch", None, None),
        P("seq", None),
        P("seq", None),
        P(("batch", "seq"), None),
    )
    return jax.shard_map(local, mesh=mesh, in_specs=in_specs, out_specs=out_specs, check_vma=False)
```

profile of v0, /device:TPU:1, one launch (start us, length us, event | category | flops | bytes accessed | tf_op | source)
XLA Modules:
  0.0 563.4 jit_solution(13254946425386572525)
XLA Ops:
  10.4 5.8 %all-to-all-start.1 = ((s32[8,1,2]{2,1,0:T(1,128)}), s32[8,1,2]{2,1,0:T(1,128)S(1)}, u32[]{:S(2)}, u32[]{:S(2)}) async-start(s32[8,1,2]{2,1,0:T(1,128)} %copy.46), calls=%async_computation.1 | async-start | bytes 8192 | tf_op jit(solution)/shard_map/all_to_all | solution.py:50
  16.2 2.9 convolution_convert_fusion.1
  19.2 3.0 copy.44
  22.1 4.9 all-to-all-start
  33.8 47.9 %all-to-all-done = bf16[8,2,128,1152]{3,2,1,0:T(8,128)(2,1)} async-done(((bf16[8,2,128,1152]{3,2,1,0:T(8,128)(2,1)}), bf16[8,2,128,1152]{3,2,1,0:T(8,128)(2,1)}, u32[]{:S(2)}, u32[]{:S(2)}) %all-to-all-start) | async-done | bytes 4718624 | tf_op jit(solution)/shard_map/all_to_all | solution.py:49
  81.6 3.3 fusion
  85.0 3.2 fusion.1
  88.2 14.8 %convolution_convert_fusion = bf16[8,2,128,2048]{3,2,1,0:T(8,128)(2,1)S(1)} fusion(bf16[8,2,128,1152]{3,2,1,0:T(8,128)(2,1)S(1)} %fusion.1, bf16[1152,2048]{1,0:T(8,128)(2,1)} %param.13), kind=kOutput, calls=%fused_computation.14 | convolution fusion | flops 9667870720 | bytes 17825792 | tf_op jit(solution)/shard_map/gcrf,fe->gcre/dot_general | solution.py:52
  103.0 3.7 fusion.45
  106.7 6.5 %copy.49 = bf16[2048,1024]{0,1:T(8,128)(2,1)} copy(bf16[2048,1024]{1,0:T(8,128)(2,1)} %get-tuple-element.7) | data formatting | bytes 8388608 | tf_op jit(solution)/shard_map/slice | solution.py:60
  113.2 6.5 %copy.45 = bf16[2048,1024]{0,1:T(8,128)(2,1)} copy(bf16[2048,1024]{1,0:T(8,128)(2,1)} %get-tuple-element.8) | data formatting | bytes 8388608 | tf_op jit(solution)/shard_map/slice | solution.py:61
  119.7 6.8 %fusion.6 = (f32[16,64]{1,0:T(8,128)S(1)}, f32[16,64,2048]{2,1,0:T(8,128)}) fusion(pred[2048]{0:T(1024)(128)(4,1)S(1)} %lt.46, bf16[64,16,64]{0,2,1:T(8,128)(2,1)S(1)} %bitcast.84, bf16[2048,16,64]{0,2,1:T(8,128)(2,1)} %bitcast.75), kind=kOutput, calls=%fused_computation.11 | convolution fusion | flops 274725888 | bytes 12720128 | tf_op jit(solution)/shard_map/lhd,thd->hlt/dot_general | solution.py:70
  126.6 35.4 %pmax.7 = f32[16,64]{1,0:T(8,128)S(1)} all-reduce(f32[16,64]{1,0:T(8,128)S(1)} %get-tuple-element.9), channel_id=1, replica_groups=mesh['batch'=8,'seq'=16] {'seq'}, use_global_device_ids=true, to_apply=%region_5.6 | all-reduce | flops 1024 | bytes 8192 | tf_op jit(solution)/shard_map/pmax | solution.py:74
  162.0 4.5 fusion.8
  166.5 29.0 %psum.35 = f32[16,64]{1,0:T(8,128)S(1)} all-reduce(f32[16,64]{1,0:T(8,128)S(1)} %fusion.8), channel_id=1, replica_groups=mesh['batch'=8,'seq'=16] {'seq'}, use_global_device_ids=true, to_apply=%region_7.8 | all-reduce | flops 1024 | bytes 8192 | tf_op jit(solution)/shard_map/psum | solution.py:76
  195.5 8.3 %fusion.11 = f32[16,64,64]{2,1,0:T(8,128)} fusion(bf16[2048,16,64]{0,2,1:T(8,128)(2,1)} %bitcast.81, f32[16,64,2048]{2,1,0:T(8,128)} %get-tuple-element.10, f32[16,64]{1,0:T(8,128)S(1)} %psum.35, f32[16,64]{1,0:T(8,128)S(1)} %pmax.7, pred[2048]{0:T(1024)(128)(4,1)S(1)} %lt.46), kind=kOutput, calls=%fused_computation.20 | convolution fusion | flops 281018368 | bytes 12855296 | tf_op jit(solution)/shard_map/hlt,thd->lhd/dot_general | solution.py:79
  203.9 8.8 %convolution_convert_fusion.2 = bf16[16,64,2048]{2,1,0:T(8,128)(2,1)} fusion(bf16[64,16,64]{0,2,1:T(8,128)(2,1)} %copy.53, f32[16,64,2048]{2,1,0:T(8,128)} %get-tuple-element.10, f32[16,64]{1,0:T(8,128)} %copy-done.8, f32[16,64]{1,0:T(8,128)S(1)} %pmax.7, pred[2048]{0:T(1024)(128)(4,1)S(1)} %lt.46), kind=kOutput, calls=%fused_computation.17 | convolution fusion | flops 283115520 | bytes 12724224 | tf_op jit(solution)/shard_map/hlt,lhd->thd/dot_general | solution.py:102
  212.7 85.7 %all-reduce.7.cloned.1.call-done = f32[64,1024]{0,1:T(8,128)} async-done(((f32[64,1024]{0,1:T(8,128)}), f32[64,1024]{0,1:T(8,128)}) %all-reduce.7.cloned.1.call-update) | async-done | bytes 262160 | tf_op jit(solution)/shard_map/psum | solution.py:82
  299.4 8.8 %multiply_convert_fusion = bf16[16,64,2048]{2,1,0:T(8,128)(2,1)S(1)} fusion(bf16[64,16,64]{0,2,1:T(8,128)(2,1)} %copy.53, bf16[2048,16,64]{0,2,1:T(8,128)(2,1)} %bitcast.82, f32[16,64]{1,0:T(8,128)S(1)} %multiply_reduce_fusion, f32[16,64]{1,0:T(8,128)} %copy-done.8, f32[16,64]{1,0:T(8,128)S(1)} %pmax.7, f32[16,64,2048]{2,1,0:T(8,128)} %get-tuple-element.10, ...), kind=kOutput, calls=%fused_computation.8 | convolution fusion | flops 287309824 | bytes 16922624 | tf_op jit(solution)/shard_map/lhd,thd->hlt/dot_general | solution.py:90
  312.5 13.8 %fusion.2 = f32[1152,2048]{1,0:T(8,128)} fusion(bf16[2048,1152]{1,0:T(8,128)(2,1)S(1)} %bitcast.80, bf16[2048,1024]{0,1:T(8,128)(2,1)S(1)} %bitcast.90, bf16[2048,1024]{0,1:T(8,128)(2,1)S(1)} %bitcast.83), kind=kOutput, calls=%fused_computation.4 | convolution fusion | flops 9680453632 | bytes 22544384 | tf_op jit(solution)/shard_map/dot_general | solution.py:117
  326.4 4.7 fusion.46
  331.9 66.2 %all-reduce.12 = bf16[64,1024]{0,1:T(8,128)(2,1)S(1)} all-reduce(f32[64,1024]{0,1:T(8,128)S(1)} %bitcast.86), channel_id=1, replica_groups=mesh['batch'=8,'seq'=16] {'seq'}, use_global_device_ids=true, to_apply=%region_9.10 | all-reduce | flops 65536 | bytes 393216 | tf_op jit(solution)/shard_map/psum | solution.py:98
  406.0 87.2 %all-reduce.9.cloned.1.call-done = f32[1152,2048]{1,0:T(8,128)} async-done(((f32[1152,2048]{1,0:T(8,128)}), f32[1152,2048]{1,0:T(8,128)}) %all-reduce.9.cloned.1.call-update) | async-done | bytes 9437200
  494.8 58.7 %all-reduce.11.cloned.1.call-done = (f32[64,1024]{1,0:T(8,128)}, f32[64,1024]{1,0:T(8,128)}) async-done(((f32[64,1024]{1,0:T(8,128)}, f32[64,1024]{1,0:T(8,128)}), (f32[64,1024]{1,0:T(8,128)}, f32[64,1024]{1,0:T(8,128)})) %all-reduce.11.cloned.1.call-update) | async-done | bytes 524304 | tf_op jit(solution)/shard_map/psum | solution.py:112
  (62 shorter events, 28.8 us)
Async XLA Ops:
  7.2 20.2 %copy-start = (bf16[1024,1024]{1,0:T(8,128)(2,1)S(1)}, bf16[1024,1024]{1,0:T(8,128)(2,1)}, u32[]{:S(2)}) copy-start(bf16[1024,1024]{1,0:T(8,128)(2,1)} %param.12) | copy-start | bytes 6291460
  10.4 11.7 %all-to-all-start.1 = ((s32[8,1,2]{2,1,0:T(1,128)}), s32[8,1,2]{2,1,0:T(1,128)S(1)}, u32[]{:S(2)}, u32[]{:S(2)}) async-start(s32[8,1,2]{2,1,0:T(1,128)} %copy.46), calls=%async_computation.1 | async-start | bytes 8192 | tf_op jit(solution)/shard_map/all_to_all | solution.py:50
  19.2 7.9 %copy-start.3 = (bf16[1,64,1024]{2,1,0:T(8,128)(2,1)S(1)}, bf16[1,64,1024]{2,1,0:T(8,128)(2,1)}, u32[]{:S(2)}) copy-start(bf16[1,64,1024]{2,1,0:T(8,128)(2,1)} %param.8) | copy-start | bytes 393220
  22.1 5.9 %copy-start.5 = (bf16[1,64,1024]{2,1,0:T(8,128)(2,1)S(1)}, bf16[1,64,1024]{2,1,0:T(8,128)(2,1)}, u32[]{:S(2)}) copy-start(bf16[1,64,1024]{2,1,0:T(8,128)(2,1)} %param.15) | copy-start | bytes 393220
  22.1 59.5 %all-to-all-start = ((bf16[8,2,128,1152]{3,2,1,0:T(8,128)(2,1)}), bf16[8,2,128,1152]{3,2,1,0:T(8,128)(2,1)}, u32[]{:S(2)}, u32[]{:S(2)}) async-start(bf16[8,2,128,1152]{3,2,1,0:T(8,128)(2,1)} %copy.44), calls=%async_computation | async-start | bytes 9437184 | tf_op jit(solution)/shard_map/all_to_all | solution.py:49
  27.1 271.2 %all-reduce.7.cloned.1.call-start = ((), (), s32[]{:S(2)}) async-start(), calls=%async_computation.2 | async-start | bytes 1048576 | tf_op jit(solution)/shard_map/psum | solution.py:82
  27.3 0.7 copy-start.7
  88.2 14.9 %copy-start.2 = (bf16[8,2,128,1152]{3,2,1,0:T(8,128)(2,1)}, bf16[8,2,128,1152]{3,2,1,0:T(8,128)(2,1)S(1)}, u32[]{:S(2)}) copy-start(bf16[8,2,128,1152]{3,2,1,0:T(8,128)(2,1)S(1)} %fusion.1) | copy-start | bytes 14155780
  195.5 8.3 %copy-start.8 = (f32[16,64]{1,0:T(8,128)}, f32[16,64]{1,0:T(8,128)S(1)}, u32[]{:S(2)}) copy-start(f32[16,64]{1,0:T(8,128)S(1)} %psum.35) | copy-start | bytes 12292
  203.8 289.4 %all-reduce.9.cloned.1.call-start = ((), (), s32[]{:S(2)}) async-start(), calls=%async_computation.3 | async-start | bytes 18874368
  203.9 107.7 %slice-start = ((s8[4718592]{0:T(1024)(128)(4,1)}), s8[524288]{0:T(1024)(128)(4,1)S(1)}, s32[]{:S(2)}) async-start(s8[4718592]{0:T(1024)(128)(4,1)} %bitcast.78), calls=%async_computation.5 | async-start | bytes 1048576
  299.4 12.1 %slice-start.1 = ((s8[4718592]{0:T(1024)(128)(4,1)}), s8[4194304]{0:T(1024)(128)(4,1)S(1)}, s32[]{:S(2)}) async-start(s8[4718592]{0:T(1024)(128)(4,1)} %bitcast.78), calls=%async_computation.6 | async-start | bytes 8388608
  308.3 2.0 copy-start.1
  310.3 2.2 copy-start.9
  326.3 4.8 copy-start.4
  326.3 72.7 %copy-start.6 = (bf16[1,64,1024]{2,1,0:T(8,128)(2,1)S(1)}, bf16[1,64,1024]{2,1,0:T(8,128)(2,1)}, u32[]{:S(2)}) copy-start(bf16[1,64,1024]{2,1,0:T(8,128)(2,1)} %param.15) | copy-start | bytes 393220
  326.3 227.2 %all-reduce.11.cloned.1.call-start = ((), (), s32[]{:S(2)}) async-start(), calls=%async_computation.4 | async-start | bytes 1048576 | tf_op jit(solution)/shard_map/psum | solution.py:112
Sparse Core Ops, SparseCore 0:
  204.0 94.3 all-reduce.6
  326.4 166.7 all-reduce.8
  496.3 57.1 all-reduce.10
where the time goes:
time: 566 us; the launch traced here: 563 us
  waiting for transfers between devices  279 us (49%)
  blocking collectives  131 us (23%)
  matrix products  80.1 us (14%)
  local copies, waits for them, and re-layouts  30.9 us (5%)
  other arithmetic  17.4 us (3%)
  between operations  14 us (2%)
  starting transfers between devices  10.8 us (2%)
    unnamed x4, waiting for transfers between devices  87.3 us
    psum x1, waiting for transfers between devices, local(): attended = lax.psum(partial_value, 'seq')  85.7 us
    psum x1, blocking collectives, local(): d_query = lax.psum(query_term, 'seq').astype(jnp.bfloat16)  66.2 us
    psum x1, waiting for transfers between devices, local(): grad_query, grad_outproj = lax.psum((query_part, outproj_part), 'batch')  58.7 us
    all_to_all x1, waiting for transfers between devices, local(): lax.all_to_all(outgoing, 'batch', split_axis=0, concat_axis=0, tiled=True)  47.9 us
    pmax x1, blocking collectives, local(): row_top = lax.pmax(jnp.max(masked, axis=2), 'seq')  35.4 us
    psum x1, blocking collectives, local(): totals = lax.psum(jnp.sum(raw_weights, axis=2), 'seq')  29 us
    dot_general x1, matrix products, local(): jnp.einsum('gcrf,fe->gcre', normed_here, w_kv, preferred_element_type=jnp...  14.8 us
  transfers between devices with their start and end apart: 5, of which 4 were waited for; matrix products, arithmetic and copies ran while one was open for 6% of the time, Pallas kernels for 0%

commit v1 on v0

v1 whole, which is shorter than its diff:
```python
import jax
import jax.numpy as jnp
from jax import lax
from jax.sharding import Mesh, PartitionSpec as P

H = 16
BATCH = ("x", "core")
SEQ = ("z", "y")
CHIPS = ("x", "z", "y")
ALL = BATCH + SEQ
SLOTS = 3

epsilon = 1e-06
f32 = jnp.float32
bf16 = jnp.bfloat16


def rms_rows(values):
    return values * lax.rsqrt(jnp.mean(values * values, axis=-1, keepdims=True) + epsilon)


def rms_back(values, grads):
    factor = lax.rsqrt(jnp.mean(values * values, axis=-1, keepdims=True) + epsilon)
    normed = values * factor
    return factor * (grads - normed * jnp.mean(grads * normed, axis=-1, keepdims=True))


def normalize(values):
    return rms_rows(values.astype(f32)).astype(bf16)


def exchange(values, axes):
    return lax.all_to_all(values, axes, 0, 0, tiled=True)


def share(values, axes, count):
    return exchange(jnp.broadcast_to(values[None], (count,) + values.shape), axes)


def other_core(values):
    return lax.ppermute(values, "core", [(0, 1), (1, 0)])


def chip_step(values, step):
    return lax.ppermute(values, "x", [(i, (i + step) % 4) for i in range(4)])


def gather_batch(values):
    near = jnp.stack([values, chip_step(values, 1), chip_step(values, 2), chip_step(values, 3)])
    return jnp.concatenate([near, other_core(near)], axis=0)


def place_of(group):
    chip = lax.rem(lax.axis_index("x") - group // 2 + 4, 4)
    return jnp.where(group % 2 == lax.axis_index("core"), 0, 4) + chip


def pick(values, places):
    return jnp.stack([lax.dynamic_index_in_dim(values, place, 0, False) for place in places])


def local(latents, frames, counts, groups, w_query, w_kv, w_out, d_out):
    blocks, block_rows, feature = frames.shape
    latent_count, model_width = latents.shape[1:]
    head_dim = model_width // H
    scale = head_dim ** (-0.5)
    group_count, seq_count = 8, 16
    rows = blocks * block_rows
    core = lax.axis_index("core")
    batch_at = lax.axis_index(BATCH)
    seq_at = lax.axis_index(SEQ)

    latents_all = gather_batch(latents[0])
    d_out_all = gather_batch(d_out[0])

    normed = normalize(frames).reshape(rows, feature)
    normed_both = jnp.concatenate([normed, other_core(normed)], axis=0)
    pairs = jnp.dot(normed, w_kv, preferred_element_type=f32).astype(bf16)
    keys = pairs[:, :model_width].reshape(blocks, block_rows, H, head_dim)
    values = pairs[:, model_width:].reshape(blocks, block_rows, H, head_dim)

    places = [place_of(groups[i]) for i in range(blocks)]
    picked = normalize(pick(latents_all, places))
    queries = jnp.dot(
        picked.reshape(-1, model_width), w_query, preferred_element_type=f32
    ).astype(bf16).reshape(blocks, latent_count, H, head_dim)
    d_mixed = lax.dot_general(
        pick(d_out_all, places).reshape(-1, model_width),
        w_out,
        (((1,), (1,)), ((), ())),
        preferred_element_type=f32,
    ).astype(bf16).reshape(blocks, latent_count, H, head_dim)

    order = jnp.arange(blocks)
    same = groups[:, None] == groups[None, :]
    first = jnp.min(jnp.where(same, order[None, :], blocks), axis=1)
    leads = first == order
    slot = jnp.sum(leads[None, :] & (order[None, :] < first[:, None]), axis=1)
    slot_groups = jnp.max(
        jnp.where(slot[None, :] == jnp.arange(SLOTS)[:, None], groups[None, :], -1), axis=1
    )

    usable = (jnp.arange(block_rows)[None, :] < counts[:, None])[:, None, None, :]
    scores = jnp.einsum("blhd,bthd->bhlt", queries, keys, preferred_element_type=f32) * scale
    masked = jnp.where(usable, scores, -1e30)
    top = jnp.max(masked, axis=3)
    raw = jnp.where(usable, jnp.exp(masked - top[..., None]), 0.0)
    total = jnp.sum(raw, axis=3)
    d_weights = jnp.einsum("blhd,bthd->bhlt", d_mixed, values, preferred_element_type=f32)
    moment = jnp.sum(raw * d_weights, axis=3)

    mine = (jnp.arange(group_count)[:, None] == groups[None, :])[:, :, None, None]
    tops = jnp.where(mine, top[None], -1e30)
    group_top = jnp.max(tops, axis=1)
    factor = jnp.where(mine, jnp.exp(tops - group_top[:, None]), 0.0)
    note = jnp.zeros((1, 1, latent_count), f32).at[0, 0, :SLOTS].set(slot_groups.astype(f32))
    stats = jnp.stack(
        [
            group_top,
            jnp.sum(factor * total[None], axis=1),
            jnp.sum(factor * moment[None], axis=1),
            jnp.broadcast_to(note, group_top.shape),
        ],
        axis=2,
    )
    stats = exchange(stats.reshape(128, 2, 128), ALL).reshape(128, 4, latent_count)
    far_top = jnp.max(stats[:, 0], axis=0)
    far_factor = jnp.exp(stats[:, 0] - far_top)
    far_total = jnp.sum(far_factor * stats[:, 1], axis=0)
    far_moment = jnp.sum(far_factor * stats[:, 2], axis=0)
    source_groups = lax.dynamic_index_in_dim(
        stats[:, 3, :SLOTS].reshape(group_count, seq_count, SLOTS), batch_at, 0, False
    )
    reply = jnp.stack([far_top, 1.0 / far_total, far_moment / far_total, far_total])
    reply = share(reply.reshape(2, 128), ALL, 128).reshape(group_count, H, 4, latent_count)
    reply = pick(reply, [groups[i] for i in range(blocks)])

    weights = jnp.where(
        usable, jnp.exp(masked - reply[:, :, 0, :, None]) * reply[:, :, 1, :, None], 0.0
    )
    weights_b = weights.astype(bf16)
    d_scores = (weights * (d_weights - reply[:, :, 2, :, None]) * scale).astype(bf16)
    mixed = jnp.einsum("bhlt,bthd->bhld", weights_b, values, preferred_element_type=f32)
    query_term = jnp.einsum("bhlt,bthd->bhld", d_scores, keys, preferred_element_type=f32)
    d_keys = jnp.einsum("bhlt,blhd->bthd", d_scores, queries, preferred_element_type=f32)
    d_values = jnp.einsum("bhlt,blhd->bthd", weights_b, d_mixed, preferred_element_type=f32)
    d_keys = d_keys.astype(bf16).reshape(rows, model_width)
    d_values = d_values.astype(bf16).reshape(rows, model_width)

    kept = jnp.where(core == 0, d_keys, d_values)
    sent = jnp.where(core == 0, d_values, d_keys)
    d_half = jnp.concatenate([kept, other_core(sent)], axis=0)
    term = lax.dot_general(
        normed_both, d_half, (((0,), (0,)), ((), ())), preferred_element_type=f32
    ).astype(bf16)
    share_rows = feature // 128
    term = term.reshape(4, 2, seq_count, share_rows, 8, 128).transpose(0, 2, 1, 3, 4, 5)
    term = exchange(term.reshape(64, 2 * share_rows, 8, 128), CHIPS)
    chip_sum = jnp.sum(term.astype(f32), axis=0).reshape(2, share_rows, model_width)
    kept_sum = lax.dynamic_index_in_dim(chip_sum, core, 0, False)
    got_sum = other_core(lax.dynamic_index_in_dim(chip_sum, 1 - core, 0, False))
    grad_kv = jnp.where(
        core == 0,
        jnp.concatenate([kept_sum, got_sum], axis=1),
        jnp.concatenate([got_sum, kept_sum], axis=1),
    )

    both = jnp.concatenate([mixed, query_term], axis=3)
    slotted = jnp.stack(
        [
            jnp.sum(jnp.where((slot == k)[:, None, None, None], both, 0.0), axis=0)
            for k in range(SLOTS)
        ],
        axis=1,
    ).astype(bf16)
    slotted = exchange(slotted, SEQ)
    chosen = (
        jnp.arange(group_count, dtype=f32)[:, None, None] == source_groups[None]
    ).astype(bf16)
    by_group = jnp.einsum("gsk,sklc->glc", chosen, slotted, preferred_element_type=f32)
    owned = jnp.sum(exchange(by_group, BATCH), axis=0).astype(bf16)
    over_seq = share(owned, SEQ, seq_count)
    mixed_b = over_seq[:, :, :head_dim].transpose(1, 0, 2).reshape(latent_count, model_width)
    d_query = over_seq[:, :, head_dim:].transpose(1, 0, 2).reshape(latent_count, model_width)
    latent = latents[0].astype(f32)
    cotangent = d_out[0]
    out = (latent + jnp.dot(mixed_b, w_out, preferred_element_type=f32)).astype(bf16)
    d_normed = lax.dot_general(
        d_query, w_query, (((1,), (1,)), ((), ())), preferred_element_type=f32
    )
    d_latents = (cotangent.astype(f32) + rms_back(latent, d_normed)).astype(bf16)

    group_places = [place_of(jnp.int32(g)) for g in range(group_count)]
    mixed_heads = share(owned[:, :head_dim], BATCH, group_count)
    grad_outproj = jnp.einsum(
        "glr,glc->rc", mixed_heads, pick(d_out_all, group_places), preferred_element_type=f32
    )
    latent_cols = lax.dynamic_slice_in_dim(
        normalize(latents_all), seq_at * head_dim, head_dim, 2
    )
    d_query_all = share(d_query, BATCH, group_count)
    grad_query = jnp.einsum(
        "glr,glc->rc", pick(latent_cols, group_places), d_query_all, preferred_element_type=f32
    )
    return (out[None], d_latents[None], grad_query, grad_outproj, grad_kv)


def solution(mesh):
    chips = Mesh(mesh.devices.reshape(4, 2, 4, 4), ("x", "core", "z", "y"))
    in_specs = (
        P(BATCH, None, None),
        P(ALL, None, None),
        P(ALL),
        P(ALL),
        P(),
        P(),
        P(),
        P(BATCH, None, None),
    )
    out_specs = (
        P(BATCH, None, None),
        P(BATCH, None, None),
        P(SEQ, None),
        P(SEQ, None),
        P(ALL, None),
    )
    return jax.shard_map(local, mesh=chips, in_specs=in_specs, out_specs=out_specs, check_vma=False)
```

time: 566 us -> 248 us (0.44)
  waiting for transfers between devices: 279 us -> 48 us
  blocking collectives: 131 us -> 10.6 us
  starting transfers between devices: 10.8 us -> 56 us
  matrix products: 80.1 us -> 37.3 us
  local copies, waits for them, and re-layouts: 30.9 us -> 58 us
    psum x2 -> x0, waiting for transfers between devices: 144 us -> none  [the longest x1 85.7 us: local(): attended = lax.psum(partial_value, 'seq')]
    psum x2 -> x0, blocking collectives: 95.2 us -> none  [the longest x1 66.2 us: local(): d_query = lax.psum(query_term, 'seq').astype(jnp.bfloat16)]
    unnamed x4 -> x0, waiting for transfers between devices: 87.3 us -> none
    dot_general x15, matrix products: 80.1 us -> 37.3 us  [the longest x1 5.97 us: local(): pairs = jnp.dot(normed, w_kv, preferred_element_type=f32).astype(bf16)]
    pmax x1 -> x0, blocking collectives: 35.4 us -> none  [local(): row_top = lax.pmax(jnp.max(masked, axis=2), 'seq')]
    all_to_all x2 -> x7, starting transfers between devices: 10.7 us -> 43.8 us  [exchange(): return lax.all_to_all(values, axes, 0, 0, tiled=True)]
    reshape x3 -> x14, local copies, waits for them, and re-layouts: 1.33 us -> 27.3 us  [the longest x2 7.61 us: local(): keys = pairs[:, :model_width].reshape(blocks, block_rows, H, head_dim)]
    slice x3 -> x4, local copies, waits for them, and re-layouts: 16.7 us -> 3.76 us  [the longest x1 1.53 us: local(): keys = pairs[:, :model_width].reshape(blocks, block_rows, H, head_dim)]
  transfers between devices with their start and end apart: 5 -> 18, of which waited for: 4 -> 7; matrix products, arithmetic and copies ran while one was open for 6% -> 36% of each run, Pallas kernels for 0% -> 0%
where the time goes in v1:
time: 248 us; the launch traced here: 246 us
  local copies, waits for them, and re-layouts  58 us (23%)
  starting transfers between devices  56 us (23%)
  waiting for transfers between devices  48 us (19%)
  matrix products  37.3 us (15%)
  other arithmetic  19.2 us (8%)
  between operations  16.9 us (7%)
  blocking collectives  10.6 us (4%)
    all_to_all x7, waiting for transfers between devices, exchange(): return lax.all_to_all(values, axes, 0, 0, tiled=True)  48 us
    all_to_all x7, starting transfers between devices, exchange(): return lax.all_to_all(values, axes, 0, 0, tiled=True)  43.8 us
    unnamed x77, local copies, waits for them, and re-layouts  16.4 us
    all_to_all x1, blocking collectives, exchange(): return lax.all_to_all(values, axes, 0, 0, tiled=True)  10.6 us
    ppermute x6, starting transfers between devices, chip_step(): return lax.ppermute(values, 'x', [(i, (i + step) % 4) for i in range(4)])  7.86 us
    reshape x2, local copies, waits for them, and re-layouts, local(): keys = pairs[:, :model_width].reshape(blocks, block_rows, H, head_dim)  7.61 us
    reshape x2, local copies, waits for them, and re-layouts, local(): values = pairs[:, model_width:].reshape(blocks, block_rows, H, head_dim)  7.59 us
    dot_general x1, matrix products, local(): pairs = jnp.dot(normed, w_kv, preferred_element_type=f32).astype(bf16)  5.97 us
  transfers between devices with their start and end apart: 18, of which 7 were waited for; matrix products, arithmetic and copies ran while one was open for 36% of the time, Pallas kernels for 0%

profile of v1, /device:TPU:1, one launch (start us, length us, event | category | flops | bytes accessed | tf_op | source)
XLA Modules:
  0.0 246.0 jit_solution(5674759106520317927)
XLA Ops:
  0.7 3.7 %collective-permute-start.1 = (bf16[64,1024]{1,0:T(8,128)(2,1)}, bf16[64,1024]{1,0:T(8,128)(2,1)S(1)}, u32[]{:S(2)}, u32[]{:S(2)}) collective-permute-start(bf16[64,1024]{1,0:T(8,128)(2,1)} %bitcast.154), channel_id=1, source_target_pairs={{0,64},{32,96},{64,0},{96,32},{1,65},{33,97},{65,1},{97,33},{2,66}... | collective-permute-start | bytes 393224 | tf_op jit(solution)/shard_map/ppermute | solution.py:45
  15.3 6.0 %convolution_convert_fusion.1 = bf16[512,2048]{1,0:T(8,128)(2,1)S(1)} fusion(bf16[512,1152]{1,0:T(8,128)(2,1)S(1)} %bitcast.159, bf16[1152,2048]{1,0:T(8,128)(2,1)} %param.15), kind=kOutput, calls=%fused_computation.2 | convolution fusion | flops 2416967680 | bytes 7995392 | tf_op jit(solution)/shard_map/dot_general | solution.py:78
  34.0 4.1 %reshape.252 = bf16[4,128,16,64]{3,2,1,0:T(8,128)(2,1)} reshape(bf16[512,1024]{1,0:T(8,128)(2,1)} %get-tuple-element.28) | data formatting | bytes 2097152 | tf_op jit(solution)/shard_map/reshape | solution.py:79
  38.1 3.5 %copy.107 = bf16[4,128,16,64]{1,3,2,0:T(8,128)(2,1)} copy(bf16[4,128,16,64]{3,2,1,0:T(8,128)(2,1)} %reshape.252) | data formatting | bytes 2097152 | tf_op jit(solution)/shard_map/reshape | solution.py:79
  41.6 4.1 %reshape.253 = bf16[4,128,16,64]{3,2,1,0:T(8,128)(2,1)} reshape(bf16[512,1024]{1,0:T(8,128)(2,1)} %get-tuple-element.29) | data formatting | bytes 2097152 | tf_op jit(solution)/shard_map/reshape | solution.py:80
  45.7 3.5 %copy.110 = bf16[4,128,16,64]{1,3,2,0:T(8,128)(2,1)} copy(bf16[4,128,16,64]{3,2,1,0:T(8,128)(2,1)} %reshape.253) | data formatting | bytes 2097152 | tf_op jit(solution)/shard_map/reshape | solution.py:80
  78.4 2.8 %fusion.10 = (f32[4,16,64]{2,1,0:T(8,128)S(1)}, f32[4,16,64]{2,1,0:T(8,128)S(1)}, f32[4,16,64,128]{3,2,1,0:T(8,128)}) fusion(f32[4,16,64,128]{3,2,1,0:T(8,128)S(1)} %get-tuple-element.60, f32[4,16,64]{2,1,0:T(8,128)S(1)} %get-tuple-element.59, pred[4,128]{1,0:T(4,128)(4,1)S(1)} %iota_compare_fusion.4, bf16[4,64,16,64]{1,3,2,0:T(8,128)(2,1)S(1)} %copy.124, ...), kind=kOutput, calls=%fused_computation.26 | convolution fusion | flops 69722112 | bytes 5816832 | tf_op jit(solution)/shard_map/blhd,bthd->bhlt/dot_general | solution.py:109
  82.5 11.6 %all-to-all-start = ((f32[128,2,128]{2,1,0:T(2,128)}), f32[128,2,128]{2,1,0:T(2,128)S(1)}, u32[]{:S(2)}, u32[]{:S(2)}) async-start(f32[128,2,128]{2,1,0:T(2,128)} %reshape.239), calls=%async_computation | async-start | bytes 262144 | tf_op jit(solution)/shard_map/all_to_all | solution.py:33
  100.4 4.0 %all-to-all-done = f32[128,2,128]{2,1,0:T(2,128)S(1)} async-done(((f32[128,2,128]{2,1,0:T(2,128)}), f32[128,2,128]{2,1,0:T(2,128)S(1)}, u32[]{:S(2)}, u32[]{:S(2)}) %all-to-all-start) | async-done | bytes 131104 | tf_op jit(solution)/shard_map/all_to_all | solution.py:33
  105.5 5.4 %all-to-all-start.1 = ((f32[128,2,128]{2,1,0:T(2,128)}), f32[128,2,128]{2,1,0:T(2,128)}, u32[]{:S(2)}, u32[]{:S(2)}) async-start(f32[128,2,128]{2,1,0:T(2,128)} %broadcast_in_dim.176), calls=%async_computation.1 | async-start | bytes 262144 | tf_op jit(solution)/shard_map/all_to_all | solution.py:33
  111.6 9.5 %all-to-all-done.1 = f32[128,2,128]{2,1,0:T(2,128)} async-done(((f32[128,2,128]{2,1,0:T(2,128)}), f32[128,2,128]{2,1,0:T(2,128)}, u32[]{:S(2)}, u32[]{:S(2)}) %all-to-all-start.1) | async-done | bytes 131104 | tf_op jit(solution)/shard_map/all_to_all | solution.py:33
  122.3 3.2 %fusion.47 = f32[4,16,64,64]{3,2,1,0:T(8,128)S(1)} fusion(bf16[4,128,16,64]{1,3,2,0:T(8,128)(2,1)} %copy.110, f32[4,16,64,128]{3,2,1,0:T(8,128)} %copy-done.1, f32[4,16,64]{2,1,0:T(8,128)S(1)} %bitcast.176, f32[4,16,64]{2,1,0:T(8,128)S(1)} %bitcast.173, pred[4,128]{1,0:T(4,128)(4,1)S(1)} %iota_compare_fusion.4), kind=kOutput, calls=%fused_computation.158 | convolution fusion | flops 69206016 | bytes 4227584 | tf_op jit(solution)/shard_map/bhlt,bthd->bhld/dot_general | solution.py:143
  130.4 4.5 %all-to-all-start.2 = ((bf16[16,3,64,128]{3,2,1,0:T(8,128)(2,1)}), bf16[16,3,64,128]{3,2,1,0:T(8,128)(2,1)}, u32[]{:S(2)}, u32[]{:S(2)}) async-start(bf16[16,3,64,128]{3,2,1,0:T(8,128)(2,1)} %copy.115), calls=%async_computation.2 | async-start | bytes 1572864 | tf_op jit(solution)/shard_map/all_to_all | solution.py:33
  134.9 3.0 %convolution_convert_fusion.2 = bf16[4,16,64,128]{3,2,1,0:T(8,128)(2,1)S(1)} fusion(bf16[4,64,16,64]{1,3,2,0:T(8,128)(2,1)S(1)} %copy.124, f32[4,16,64,128]{3,2,1,0:T(8,128)} %copy-done.1, f32[4,16,64]{2,1,0:T(8,128)S(1)} %bitcast.178, f32[4,16,64]{2,1,0:T(8,128)S(1)} %bitcast.175, pred[4,128]{1,0:T(4,128)(4,1)S(1)} %iota_compare_fusion.4), kind=kOutput, calls=%fused_computation.29 | convolution fusion | flops 69730304 | bytes 3703296 | tf_op jit(solution)/shard_map/bhlt,blhd->bthd/dot_general | solution.py:146
  141.7 6.8 %all-to-all-done.2 = bf16[16,3,64,128]{3,2,1,0:T(8,128)(2,1)} async-done(((bf16[16,3,64,128]{3,2,1,0:T(8,128)(2,1)}), bf16[16,3,64,128]{3,2,1,0:T(8,128)(2,1)}, u32[]{:S(2)}, u32[]{:S(2)}) %all-to-all-start.2) | async-done | bytes 786464 | tf_op jit(solution)/shard_map/all_to_all | solution.py:33
  150.3 10.6 %all_to_all.40 = f32[8,64,128]{2,1,0:T(8,128)S(1)} all-to-all(f32[8,64,128]{2,1,0:T(8,128)S(1)} %copy.117), channel_id=1, replica_groups=mesh['x'=4,'core'=2,'z'=4,'y'=4] {'x','core'}, dimensions={0} | all-to-all | bytes 524288 | tf_op jit(solution)/shard_map/all_to_all | solution.py:33
  161.8 4.3 %all-to-all-start.6 = ((bf16[8,2,2048]{2,1,0:T(2,128)(2,1)}), bf16[8,2,2048]{2,1,0:T(2,128)(2,1)S(1)}, u32[]{:S(2)}, u32[]{:S(2)}) async-start(bf16[8,2,2048]{2,1,0:T(2,128)(2,1)} %reshape.254), calls=%async_computation.6 | async-start | bytes 131072 | tf_op jit(solution)/shard_map/all_to_all | solution.py:33
  167.8 3.2 %all-to-all-done.6 = bf16[8,2,2048]{2,1,0:T(2,128)(2,1)S(1)} async-done(((bf16[8,2,2048]{2,1,0:T(2,128)(2,1)}), bf16[8,2,2048]{2,1,0:T(2,128)(2,1)S(1)}, u32[]{:S(2)}, u32[]{:S(2)}) %all-to-all-start.6) | async-done | bytes 65568 | tf_op jit(solution)/shard_map/all_to_all | solution.py:33
  171.7 3.5 %all-to-all-start.4 = ((bf16[16,64,128]{2,1,0:T(8,128)(2,1)}), bf16[16,64,128]{2,1,0:T(8,128)(2,1)S(1)}, u32[]{:S(2)}, u32[]{:S(2)}) async-start(bf16[16,64,128]{2,1,0:T(8,128)(2,1)} %broadcast_in_dim.179), calls=%async_computation.4 | async-start | bytes 524288 | tf_op jit(solution)/shard_map/all_to_all | solution.py:33
  175.2 4.6 %fusion.11 = bf16[144,8,8,128]{3,1,2,0:T(8,128)(2,1)S(1)} fusion(bf16[512,1024]{0,1:T(8,128)(2,1)} %collective-permute-done.9, bf16[512,1024]{0,1:T(8,128)(2,1)S(1)} %bitcast.165, bf16[512,1152]{1,0:T(8,128)(2,1)} %collective-permute-done.8, bf16[512,1152]{1,0:T(8,128)(2,1)} %bitcast.161), kind=kOutput, calls=%fused_computation.27 | convolution fusion | flops 2426011648 | bytes 6815744 | tf_op jit(solution)/shard_map/dot_general | solution.py:153
  183.2 7.4 %all-to-all-start.7 = ((bf16[64,18,8,128]{3,2,1,0:T(8,128)(2,1)}), bf16[64,18,8,128]{3,2,1,0:T(8,128)(2,1)}, u32[]{:S(2)}, u32[]{:S(2)}) async-start(bf16[64,18,8,128]{3,2,1,0:T(8,128)(2,1)} %bitcast.152), calls=%async_computation.7 | async-start | bytes 4718592 | tf_op jit(solution)/shard_map/all_to_all | solution.py:33
  202.7 17.3 %all-to-all-done.7 = bf16[64,18,8,128]{3,2,1,0:T(8,128)(2,1)} async-done(((bf16[64,18,8,128]{3,2,1,0:T(8,128)(2,1)}), bf16[64,18,8,128]{3,2,1,0:T(8,128)(2,1)}, u32[]{:S(2)}, u32[]{:S(2)}) %all-to-all-start.7) | async-done | bytes 2359328 | tf_op jit(solution)/shard_map/all_to_all | solution.py:33
  221.1 7.2 %all-to-all-start.5 = ((bf16[8,64,1024]{2,1,0:T(8,128)(2,1)}), bf16[8,64,1024]{2,1,0:T(8,128)(2,1)S(1)}, u32[]{:S(2)}, u32[]{:S(2)}) async-start(bf16[8,64,1024]{2,1,0:T(8,128)(2,1)} %broadcast_in_dim.182), calls=%async_computation.5 | async-start | bytes 2097152 | tf_op jit(solution)/shard_map/all_to_all | solution.py:33
  237.1 6.2 %all-to-all-done.5 = bf16[8,64,1024]{2,1,0:T(8,128)(2,1)S(1)} async-done(((bf16[8,64,1024]{2,1,0:T(8,128)(2,1)}), bf16[8,64,1024]{2,1,0:T(8,128)(2,1)S(1)}, u32[]{:S(2)}, u32[]{:S(2)}) %all-to-all-start.5) | async-done | bytes 1048608 | tf_op jit(solution)/shard_map/all_to_all | solution.py:33
  (186 shorter events, 89.3 us)
Async XLA Ops:
  0.6 63.0 %copy-start = (bf16[1024,1024]{1,0:T(8,128)(2,1)S(1)}, bf16[1024,1024]{1,0:T(8,128)(2,1)}, u32[]{:S(2)}) copy-start(bf16[1024,1024]{1,0:T(8,128)(2,1)} %param.14) | copy-start | bytes 6291460
  0.6 14.3 %copy-start.11 = (bf16[4,128,1152]{2,1,0:T(8,128)(2,1)S(1)}, bf16[4,128,1152]{2,1,0:T(8,128)(2,1)}, u32[]{:S(2)}) copy-start(bf16[4,128,1152]{2,1,0:T(8,128)(2,1)} %param.11) | copy-start | bytes 3538948
  0.7 27.4 %collective-permute-start.1 = (bf16[64,1024]{1,0:T(8,128)(2,1)}, bf16[64,1024]{1,0:T(8,128)(2,1)S(1)}, u32[]{:S(2)}, u32[]{:S(2)}) collective-permute-start(bf16[64,1024]{1,0:T(8,128)(2,1)} %bitcast.154), channel_id=1, source_target_pairs={{0,64},{32,96},{64,0},{96,32},{1,65},{33,97},{65,1},{97,33},{2,66}... | collective-permute-start | bytes 393224 | tf_op jit(solution)/shard_map/ppermute | solution.py:45
  4.3 44.9 %collective-permute-start = (bf16[64,1024]{1,0:T(8,128)(2,1)}, bf16[64,1024]{1,0:T(8,128)(2,1)}, u32[]{:S(2)}, u32[]{:S(2)}) collective-permute-start(bf16[64,1024]{1,0:T(8,128)(2,1)} %bitcast.155), channel_id=1, source_target_pairs={{0,32},{32,64},{64,96},{96,0},{1,33},{33,65},{65,97},{97,1},{2,34}... | collective-permute-start | bytes 393224 | tf_op jit(solution)/shard_map/ppermute | solution.py:45
  4.6 44.6 %collective-permute-start.2 = (bf16[64,1024]{1,0:T(8,128)(2,1)}, bf16[64,1024]{1,0:T(8,128)(2,1)}, u32[]{:S(2)}, u32[]{:S(2)}) collective-permute-start(bf16[64,1024]{1,0:T(8,128)(2,1)} %bitcast.156), channel_id=1, source_target_pairs={{0,96},{32,0},{64,32},{96,64},{1,97},{33,1},{65,33},{97,65},{2,98}... | collective-permute-start | bytes 393224 | tf_op jit(solution)/shard_map/ppermute | solution.py:45
  7.0 45.5 %collective-permute-start.6 = (bf16[64,1024]{1,0:T(8,128)(2,1)}, bf16[64,1024]{1,0:T(8,128)(2,1)}, u32[]{:S(2)}, u32[]{:S(2)}) collective-permute-start(bf16[64,1024]{1,0:T(8,128)(2,1)} %bitcast.162), channel_id=1, source_target_pairs={{0,96},{32,0},{64,32},{96,64},{1,97},{33,1},{65,33},{97,65},{2,98}... | collective-permute-start | bytes 393224 | tf_op jit(solution)/shard_map/ppermute | solution.py:45
  7.0 45.5 %collective-permute-start.5 = (bf16[64,1024]{1,0:T(8,128)(2,1)}, bf16[64,1024]{1,0:T(8,128)(2,1)}, u32[]{:S(2)}, u32[]{:S(2)}) collective-permute-start(bf16[64,1024]{1,0:T(8,128)(2,1)} %bitcast.163), channel_id=1, source_target_pairs={{0,64},{32,96},{64,0},{96,32},{1,65},{33,97},{65,1},{97,33},{2,66}... | collective-permute-start | bytes 393224 | tf_op jit(solution)/shard_map/ppermute | solution.py:45
  13.4 9.4 %copy-start.23 = (s32[4]{0:T(128)}, s32[4]{0:T(128)S(1)}, u32[]{:S(2)}) copy-start(s32[4]{0:T(128)S(1)} %convert_reduce_fusion.1) | copy-start | bytes 52
  28.1 24.4 %collective-permute-start.4 = (bf16[64,1024]{1,0:T(8,128)(2,1)S(1)}, bf16[64,1024]{1,0:T(8,128)(2,1)}, u32[]{:S(2)}, u32[]{:S(2)}) collective-permute-start(bf16[64,1024]{1,0:T(8,128)(2,1)S(1)} %bitcast.164), channel_id=1, source_target_pairs={{0,32},{32,64},{64,96},{96,0},{1,33},{33,65},{65,97},{97,1},{2,34}... | collective-permute-start | bytes 393224 | tf_op jit(solution)/shard_map/ppermute | solution.py:45
  50.4 8.4 %collective-permute-start.3 = (bf16[4,64,1024]{2,1,0:T(8,128)(2,1)S(1)}, bf16[4,64,1024]{2,1,0:T(8,128)(2,1)S(1)}, u32[]{:S(2)}, u32[]{:S(2)}) collective-permute-start(bf16[4,64,1024]{2,1,0:T(8,128)(2,1)S(1)} %pad_maximum_fusion.2), channel_id=1, source_target_pairs={{0,16},{16,0},{1,17},{17,1},{2,18},{18,2},{3,19},{19,3},{4,20},{20... | collective-permute-start | bytes 1572872 | tf_op jit(solution)/shard_map/ppermute | solution.py:41
  53.6 4.9 %collective-permute-start.7 = (bf16[4,64,1024]{2,1,0:T(8,128)(2,1)S(1)}, bf16[4,64,1024]{2,1,0:T(8,128)(2,1)S(1)}, u32[]{:S(2)}, u32[]{:S(2)}) collective-permute-start(bf16[4,64,1024]{2,1,0:T(8,128)(2,1)S(1)} %pad_maximum_fusion.3), channel_id=1, source_target_pairs={{0,16},{16,0},{1,17},{17,1},{2,18},{18,2},{3,19},{19,3},{4,20},{20... | collective-permute-start | bytes 1572872 | tf_op jit(solution)/shard_map/ppermute | solution.py:41
  82.5 21.8 %all-to-all-start = ((f32[128,2,128]{2,1,0:T(2,128)}), f32[128,2,128]{2,1,0:T(2,128)S(1)}, u32[]{:S(2)}, u32[]{:S(2)}) async-start(f32[128,2,128]{2,1,0:T(2,128)} %reshape.239), calls=%async_computation | async-start | bytes 262144 | tf_op jit(solution)/shard_map/all_to_all | solution.py:33
  94.1 81.1 %collective-permute-start.8 = (bf16[512,1152]{1,0:T(8,128)(2,1)}, bf16[512,1152]{1,0:T(8,128)(2,1)}, u32[]{:S(2)}, u32[]{:S(2)}) collective-permute-start(bf16[512,1152]{1,0:T(8,128)(2,1)} %bitcast.160), channel_id=1, source_target_pairs={{0,16},{16,0},{1,17},{17,1},{2,18},{18,2},{3,19},{19,3},{4,20},{20... | collective-permute-start | bytes 3538952 | tf_op jit(solution)/shard_map/ppermute | solution.py:41
  104.4 7.2 %copy-start.19 = (f32[128,2,128]{0,2,1:T(8,128)}, f32[128,2,128]{0,2,1:T(8,128)S(1)}, u32[]{:S(2)}) copy-start(f32[128,2,128]{0,2,1:T(8,128)S(1)} %copy.112) | copy-start | bytes 393220
  105.5 15.5 %all-to-all-start.1 = ((f32[128,2,128]{2,1,0:T(2,128)}), f32[128,2,128]{2,1,0:T(2,128)}, u32[]{:S(2)}, u32[]{:S(2)}) async-start(f32[128,2,128]{2,1,0:T(2,128)} %broadcast_in_dim.176), calls=%async_computation.1 | async-start | bytes 262144 | tf_op jit(solution)/shard_map/all_to_all | solution.py:33
  130.4 18.2 %all-to-all-start.2 = ((bf16[16,3,64,128]{3,2,1,0:T(8,128)(2,1)}), bf16[16,3,64,128]{3,2,1,0:T(8,128)(2,1)}, u32[]{:S(2)}, u32[]{:S(2)}) async-start(bf16[16,3,64,128]{3,2,1,0:T(8,128)(2,1)} %copy.115), calls=%async_computation.2 | async-start | bytes 1572864 | tf_op jit(solution)/shard_map/all_to_all | solution.py:33
  140.5 34.8 %collective-permute-start.9 = (bf16[512,1024]{0,1:T(8,128)(2,1)}, bf16[512,1024]{0,1:T(8,128)(2,1)}, u32[]{:S(2)}, u32[]{:S(2)}) collective-permute-start(bf16[512,1024]{0,1:T(8,128)(2,1)} %bitcast.148), channel_id=1, source_target_pairs={{0,16},{16,0},{1,17},{17,1},{2,18},{18,2},{3,19},{19,3},{4,20},{20... | collective-permute-start | bytes 3145736 | tf_op jit(solution)/shard_map/ppermute | solution.py:41
  161.8 9.2 %all-to-all-start.6 = ((bf16[8,2,2048]{2,1,0:T(2,128)(2,1)}), bf16[8,2,2048]{2,1,0:T(2,128)(2,1)S(1)}, u32[]{:S(2)}, u32[]{:S(2)}) async-start(bf16[8,2,2048]{2,1,0:T(2,128)(2,1)} %reshape.254), calls=%async_computation.6 | async-start | bytes 131072 | tf_op jit(solution)/shard_map/all_to_all | solution.py:33
  171.7 11.5 %all-to-all-start.4 = ((bf16[16,64,128]{2,1,0:T(8,128)(2,1)}), bf16[16,64,128]{2,1,0:T(8,128)(2,1)S(1)}, u32[]{:S(2)}, u32[]{:S(2)}) async-start(bf16[16,64,128]{2,1,0:T(8,128)(2,1)} %broadcast_in_dim.179), calls=%async_computation.4 | async-start | bytes 524288 | tf_op jit(solution)/shard_map/all_to_all | solution.py:33
  183.2 7.4 %copy-start.22 = (f32[64]{0:T(128)S(1)}, f32[64]{0:T(128)}, u32[]{:S(2)}) copy-start(f32[64]{0:T(128)} %fusion.34) | copy-start | bytes 772
  183.2 7.5 %copy-start.10 = (bf16[8,64,1024]{2,1,0:T(8,128)(2,1)S(1)}, bf16[8,64,1024]{2,1,0:T(8,128)(2,1)}, u32[]{:S(2)}) copy-start(bf16[8,64,1024]{2,1,0:T(8,128)(2,1)} %copy-done.9) | copy-start | bytes 3145732
  183.2 36.8 %all-to-all-start.7 = ((bf16[64,18,8,128]{3,2,1,0:T(8,128)(2,1)}), bf16[64,18,8,128]{3,2,1,0:T(8,128)(2,1)}, u32[]{:S(2)}, u32[]{:S(2)}) async-start(bf16[64,18,8,128]{3,2,1,0:T(8,128)(2,1)} %bitcast.152), calls=%async_computation.7 | async-start | bytes 4718592 | tf_op jit(solution)/shard_map/all_to_all | solution.py:33
  221.1 22.3 %all-to-all-start.5 = ((bf16[8,64,1024]{2,1,0:T(8,128)(2,1)}), bf16[8,64,1024]{2,1,0:T(8,128)(2,1)S(1)}, u32[]{:S(2)}, u32[]{:S(2)}) async-start(bf16[8,64,1024]{2,1,0:T(8,128)(2,1)} %broadcast_in_dim.182), calls=%async_computation.5 | async-start | bytes 2097152 | tf_op jit(solution)/shard_map/all_to_all | solution.py:33
  236.9 8.4 %collective-permute-start.10 = (f32[9,1024]{1,0:T(8,128)S(1)}, f32[9,1024]{1,0:T(8,128)S(1)}, u32[]{:S(2)}, u32[]{:S(2)}) collective-permute-start(f32[9,1024]{1,0:T(8,128)S(1)} %get-tuple-element.46), channel_id=1, source_target_pairs={{0,16},{16,0},{1,17},{17,1},{2,18},{18,2},{3,19},{19,3},{4,20},{20... | collective-permute-start | bytes 110600 | tf_op jit(solution)/shard_map/ppermute | solution.py:41
  (18 other events, 60.7 us)

commit v2 on v1

v2 whole, which is shorter than its diff:
```python
import functools

import jax
import jax.numpy as jnp
from jax import lax
from jax.experimental import pallas as pl
from jax.experimental.pallas import tpu as pltpu
from jax.sharding import Mesh, PartitionSpec as P

H = 16
BATCH = ("x", "core")
SEQ = ("z", "y")
CHIPS = ("x", "z", "y")
ALL = BATCH + SEQ
SLOTS = 3

epsilon = 1e-06
f32 = jnp.float32
bf16 = jnp.bfloat16


def rms_rows(values):
    return values * lax.rsqrt(jnp.mean(values * values, axis=-1, keepdims=True) + epsilon)


def rms_back(values, grads):
    factor = lax.rsqrt(jnp.mean(values * values, axis=-1, keepdims=True) + epsilon)
    normed = values * factor
    return factor * (grads - normed * jnp.mean(grads * normed, axis=-1, keepdims=True))


def normalize(values):
    return rms_rows(values.astype(f32)).astype(bf16)


def exchange(values, axes):
    return lax.all_to_all(values, axes, 0, 0, tiled=True)


def share(values, axes, count):
    return exchange(jnp.broadcast_to(values[None], (count,) + values.shape), axes)


def other_core(values):
    return lax.ppermute(values, "core", [(0, 1), (1, 0)])


def chip_step(values, step):
    return lax.ppermute(values, "x", [(i, (i + step) % 4) for i in range(4)])


def gather_batch(values):
    near = [values, chip_step(values, 1), chip_step(values, 2), chip_step(values, 3)]
    return near + [other_core(piece) for piece in near]


def place_of(group):
    chip = lax.rem(lax.axis_index("x") - group // 2 + 4, 4)
    return jnp.where(group % 2 == lax.axis_index("core"), 0, 4) + chip


def group_at(place):
    chip = lax.rem(lax.axis_index("x") - place % 4 + 4, 4)
    core = lax.axis_index("core")
    return 2 * chip + (core if place < 4 else 1 - core)


SMEM = pl.BlockSpec(memory_space=pltpu.SMEM)
VMEM = pl.BlockSpec(memory_space=pltpu.VMEM)
LAST = (((1,), (1,)), ((), ()))
FIRST = (((0,), (0,)), ((), ()))


def project_kernel(norm, transposed, places, *refs):
    pieces, (w_ref, out_ref, picked) = refs[:8], refs[8:]
    rows = pieces[0].shape[0]
    for i in range(out_ref.shape[0] // rows):
        for j in range(8):

            @pl.when(places[i] == j)
            def _():
                picked[i * rows : (i + 1) * rows, :] = pieces[j][...]

    x = picked[...]
    if norm:
        x = normalize(x)
    numbers = LAST if transposed else (((1,), (0,)), ((), ()))
    out_ref[...] = lax.dot_general(x, w_ref[...], numbers, preferred_element_type=f32).astype(bf16)


def project(places, pieces, weight, norm, transposed):
    rows, width = pieces[0].shape
    out = jax.ShapeDtypeStruct((places.shape[0] * rows, weight.shape[0]), bf16)
    return pl.pallas_call(
        functools.partial(project_kernel, norm, transposed),
        out_shape=out,
        in_specs=[SMEM] + [VMEM] * 9,
        out_specs=VMEM,
        scratch_shapes=[pltpu.VMEM((out.shape[0], width), bf16)],
        cost_estimate=pl.CostEstimate(
            flops=2 * out.shape[0] * width * weight.shape[0],
            bytes_accessed=4 * 1024 * 1024,
            transcendentals=0,
        ),
    )(places, *pieces, weight)


def low_lanes(shape):
    return lax.broadcasted_iota(jnp.int32, shape, len(shape) - 1) < 64


def spread(pair, low, high):
    return jnp.concatenate([pair * low, pair * high], axis=0)


def half_masks():
    lane = low_lanes((1, 128))
    return jnp.where(lane, 1.0, 0.0).astype(bf16), jnp.where(lane, 0.0, 1.0).astype(bf16)


def slots_of(groups):
    slots, used = [0], 1
    for i in range(1, 4):
        slot = used
        fresh = True
        for j in reversed(range(i)):
            slot = jnp.where(groups[i] == groups[j], slots[j], slot)
            fresh = fresh & (groups[i] != groups[j])
        slots.append(slot)
        used = used + jnp.where(fresh, 1, 0)
    return slots


def stats_kernel(counts, groups, q_ref, d_ref, pairs_ref, out_ref, top_ref, total_ref, moment_ref):
    block = pl.program_id(0)
    low, high = half_masks()
    width = q_ref.shape[1]
    scale = (width // H) ** (-0.5)
    usable = lax.broadcasted_iota(jnp.int32, (128, 128), 0) < counts[block]
    for p in range(width // 128):
        cols = slice(128 * p, 128 * p + 128)
        value_cols = slice(width + 128 * p, width + 128 * p + 128)
        s = lax.dot_general(
            pairs_ref[:, cols], spread(q_ref[:, cols], low, high), LAST, preferred_element_type=f32
        )
        s = jnp.where(usable, s * scale, -1e30)
        top = jnp.max(s, axis=0, keepdims=True)
        raw = jnp.where(usable, jnp.exp(s - top), 0.0)
        dw = lax.dot_general(
            pairs_ref[:, value_cols],
            spread(d_ref[:, cols], low, high),
            LAST,
            preferred_element_type=f32,
        )
        top_ref[block, p : p + 1, :] = top
        total_ref[block, p : p + 1, :] = jnp.sum(raw, axis=0, keepdims=True)
        moment_ref[block, p : p + 1, :] = jnp.sum(raw * dw, axis=0, keepdims=True)

    @pl.when(block == 3)
    def _():
        own = [groups[i] for i in range(4)]
        slots = slots_of(own)
        left = low_lanes((8, 128))
        lane = lax.broadcasted_iota(jnp.int32, (8, 128), 1)
        note = jnp.full((8, 128), -1.0, f32)
        for i in range(4):
            note = jnp.where(lane == 64 + slots[i], own[i].astype(f32), note)
        for g in range(8):
            tops = [jnp.where(own[i] == g, top_ref[i], -1e30) for i in range(4)]
            top = functools.reduce(jnp.maximum, tops)
            total = jnp.zeros((8, 128), f32)
            moment = jnp.zeros((8, 128), f32)
            for i in range(4):
                factor = jnp.where(own[i] == g, jnp.exp(tops[i] - top), 0.0)
                total = total + factor * total_ref[i]
                moment = moment + factor * moment_ref[i]
            out_ref[g, 0:8, 0:128] = jnp.where(left, top, pltpu.roll(total, 64, 1))
            out_ref[g, 8:16, 0:128] = jnp.where(left, pltpu.roll(top, 64, 1), total)
            out_ref[g, 0:8, 128:256] = jnp.where(left, moment, note)
            out_ref[g, 8:16, 128:256] = jnp.where(left, pltpu.roll(moment, 64, 1), note)


def block_specs(latent_count, width):
    return [
        pl.BlockSpec((latent_count, width), lambda i: (i, 0)),
        pl.BlockSpec((latent_count, width), lambda i: (i, 0)),
        pl.BlockSpec((128, 2 * width), lambda i: (i, 0)),
    ]


def statistics(counts, groups, queries, d_mixed, pairs):
    width = queries.shape[1]
    return pl.pallas_call(
        stats_kernel,
        grid=(4,),
        out_shape=jax.ShapeDtypeStruct((8, 16, 256), f32),
        in_specs=[SMEM, SMEM] + block_specs(queries.shape[0] // 4, width),
        out_specs=pl.BlockSpec((8, 16, 256), lambda i: (0, 0, 0)),
        scratch_shapes=[pltpu.VMEM((4, 8, 128), f32)] * 3,
        cost_estimate=pl.CostEstimate(
            flops=4 * 1024 * 1024 * 1024, bytes_accessed=4 * 1024 * 1024, transcendentals=512 * 1024
        ),
    )(counts, groups, queries, d_mixed, pairs)


def totals_kernel(in_ref, out_ref):
    left = low_lanes((1, 128))
    first = in_ref[:, 0:128]
    top = jnp.max(first, axis=0, keepdims=True)
    top = jnp.where(left, top, pltpu.roll(top, 64, 1))
    factor = jnp.exp(jnp.where(left, first, pltpu.roll(first, 64, 1)) - top)
    total = jnp.sum(factor * first, axis=0, keepdims=True)
    inverse = 1.0 / jnp.where(left, pltpu.roll(total, 64, 1), total)
    delta = jnp.sum(factor * in_ref[:, 128:256], axis=0, keepdims=True) * inverse
    out_ref[:, 0:128] = jnp.broadcast_to(jnp.where(left, top, inverse), first.shape)
    out_ref[:, 128:256] = jnp.broadcast_to(jnp.where(left, delta, 0.0), first.shape)


def totals(stats):
    return pl.pallas_call(
        totals_kernel,
        out_shape=jax.ShapeDtypeStruct(stats.shape, f32),
        in_specs=[VMEM],
        out_specs=VMEM,
    )(stats)


def grads_kernel(
    counts, groups, core, q_ref, d_ref, pairs_ref, reply_ref, d_pairs_ref, slotted_ref, mixed_acc, query_acc
):
    block = pl.program_id(0)
    low, high = half_masks()
    rows, width = q_ref.shape
    scale = (width // H) ** (-0.5)
    usable = lax.broadcasted_iota(jnp.int32, (128, 128), 0) < counts[block]
    left = low_lanes((8, 128))
    wide = low_lanes((rows, 128))

    @pl.when(block == 0)
    def _():
        mixed_acc[...] = jnp.zeros_like(mixed_acc)
        query_acc[...] = jnp.zeros_like(query_acc)

    slots = slots_of([groups[i] for i in range(4)])
    slot = slots[0]
    for i in range(1, 4):
        slot = jnp.where(block == i, slots[i], slot)
    group = groups[block]
    even = reply_ref[group, 0:8, 0:128]
    odd = reply_ref[group, 8:16, 0:128]
    top = jnp.where(left, even, pltpu.roll(odd, 64, 1))
    inverse = jnp.where(left, pltpu.roll(even, 64, 1), odd)
    delta = jnp.where(
        left, reply_ref[group, 0:8, 128:256], pltpu.roll(reply_ref[group, 8:16, 128:256], 64, 1)
    )
    for p in range(width // 128):
        cols = slice(128 * p, 128 * p + 128)
        value_cols = slice(width + 128 * p, width + 128 * p + 128)
        q = spread(q_ref[:, cols], low, high)
        d = spread(d_ref[:, cols], low, high)
        k = pairs_ref[:, cols]
        v = pairs_ref[:, value_cols]
        s = lax.dot_general(k, q, LAST, preferred_element_type=f32) * scale
        dw = lax.dot_general(v, d, LAST, preferred_element_type=f32)
        weights = jnp.where(usable, jnp.exp(s - top[p : p + 1]) * inverse[p : p + 1], 0.0)
        weights_b = weights.astype(bf16)
        d_scores = (weights * (dw - delta[p : p + 1]) * scale).astype(bf16)
        d_pairs_ref[1 - core[0], :, cols] = jnp.dot(
            weights_b, d, preferred_element_type=f32
        ).astype(bf16)
        d_pairs_ref[core[0], :, cols] = jnp.dot(d_scores, q, preferred_element_type=f32).astype(bf16)
        mixed = lax.dot_general(weights_b, v, FIRST, preferred_element_type=f32)
        mixed_acc[slot, :, cols] += jnp.where(wide, mixed[:rows], mixed[rows:])
        query = lax.dot_general(d_scores, k, FIRST, preferred_element_type=f32)
        query_acc[slot, :, cols] += jnp.where(wide, query[:rows], query[rows:])

    @pl.when(block == 3)
    def _():
        for at in range(SLOTS):
            for p in range(width // 128):
                cols = slice(128 * p, 128 * p + 128)
                mixed = mixed_acc[at, :, cols]
                query = query_acc[at, :, cols]
                slotted_ref[2 * p, at] = jnp.where(
                    wide, mixed, pltpu.roll(query, 64, 1)
                ).astype(bf16)
                slotted_ref[2 * p + 1, at] = jnp.where(
                    wide, pltpu.roll(mixed, 64, 1), query
                ).astype(bf16)


def gradients(counts, groups, core, queries, d_mixed, pairs, reply):
    width = queries.shape[1]
    rows = queries.shape[0] // 4
    return pl.pallas_call(
        grads_kernel,
        grid=(4,),
        out_shape=(
            jax.ShapeDtypeStruct((2, pairs.shape[0], width), bf16),
            jax.ShapeDtypeStruct((H, SLOTS, rows, 128), bf16),
        ),
        in_specs=[SMEM, SMEM, SMEM]
        + block_specs(rows, width)
        + [pl.BlockSpec((8, 16, 256), lambda i: (0, 0, 0))],
        out_specs=(
            pl.BlockSpec((2, 128, width), lambda i: (0, i, 0)),
            pl.BlockSpec((H, SLOTS, rows, 128), lambda i: (0, 0, 0, 0)),
        ),
        scratch_shapes=[pltpu.VMEM((SLOTS, rows, width), f32)] * 2,
        cost_estimate=pl.CostEstimate(
            flops=8 * 1024 * 1024 * 1024, bytes_accessed=8 * 1024 * 1024, transcendentals=512 * 1024
        ),
    )(counts, groups, core, queries, d_mixed, pairs, reply)


def local(latents, frames, counts, groups, w_query, w_kv, w_out, d_out):
    blocks, block_rows, feature = frames.shape
    latent_count, model_width = latents.shape[1:]
    head_dim = model_width // H
    group_count, seq_count = 8, 16
    rows = blocks * block_rows
    core = lax.axis_index("core")
    batch_at = lax.axis_index(BATCH)

    latents_all = gather_batch(latents[0])
    d_out_all = gather_batch(d_out[0])
    normed = normalize(frames).reshape(rows, feature)
    pairs = jnp.dot(normed, w_kv, preferred_element_type=f32).astype(bf16)
    places = place_of(groups)
    queries = project(places, latents_all, w_query, True, False)
    d_mixed = project(places, d_out_all, w_out, False, True)
    stats = statistics(counts, groups, queries, d_mixed, pairs)
    normed, stats = lax.optimization_barrier((normed, stats))
    normed_both = jnp.concatenate([normed, other_core(normed)], axis=0)
    stats = exchange(stats.reshape(128, 256), ALL)
    source_groups = lax.dynamic_slice(
        stats, (batch_at * seq_count, 192), (seq_count, SLOTS)
    )
    reply = exchange(totals(stats), ALL).reshape(group_count, seq_count, 256)
    d_pairs, slotted = gradients(
        counts, groups, core.reshape(1), queries, d_mixed, pairs, reply
    )

    d_half = jnp.concatenate([d_pairs[0], other_core(d_pairs[1])], axis=0)
    term = lax.dot_general(normed_both, d_half, FIRST, preferred_element_type=f32).astype(bf16)
    share_rows = feature // 128
    term = term.reshape(4, 2, seq_count, share_rows, 8, 128).transpose(0, 2, 1, 3, 4, 5)
    term = exchange(term.reshape(64, 2 * share_rows, 8, 128), CHIPS)
    chip_sum = jnp.sum(term.astype(f32), axis=0).reshape(2, share_rows, model_width)
    kept_sum = lax.dynamic_index_in_dim(chip_sum, core, 0, False)
    got_sum = other_core(lax.dynamic_index_in_dim(chip_sum, 1 - core, 0, False))
    grad_kv = jnp.where(
        core == 0,
        jnp.concatenate([kept_sum, got_sum], axis=1),
        jnp.concatenate([got_sum, kept_sum], axis=1),
    )

    slotted = exchange(slotted, SEQ)
    chosen = (
        jnp.arange(group_count, dtype=f32)[:, None, None] == source_groups[None]
    ).astype(bf16)
    by_group = jnp.einsum("gsk,sklc->glc", chosen, slotted, preferred_element_type=f32)
    owned = jnp.sum(exchange(by_group, BATCH), axis=0).astype(bf16)
    over_batch = share(owned, BATCH, group_count)
    over_batch = jnp.concatenate(
        [lax.dynamic_index_in_dim(over_batch, group_at(j), 0, False) for j in range(8)], axis=0
    )
    normed_latents = normalize(jnp.concatenate(latents_all, axis=0))
    query_cols = lax.dot_general(
        normed_latents, over_batch[:, head_dim:], FIRST, preferred_element_type=f32
    )
    query_high = query_cols.astype(bf16)
    query_low = (query_cols - query_high.astype(f32)).astype(bf16)
    query_cols = jnp.concatenate([query_high, query_low], axis=1)
    grad_outproj = lax.dot_general(
        over_batch[:, :head_dim],
        jnp.concatenate(d_out_all, axis=0),
        FIRST,
        preferred_element_type=f32,
    )
    over_seq = exchange(
        jnp.stack(
            [
                jnp.broadcast_to(owned[None], (seq_count,) + owned.shape),
                query_cols.reshape(seq_count, head_dim, 128),
            ],
            axis=1,
        ),
        SEQ,
    )

    def joined(part):
        return part.transpose(1, 0, 2).reshape(part.shape[1], model_width)

    mixed_b = joined(over_seq[:, 0, :, :head_dim])
    d_query = joined(over_seq[:, 0, :, head_dim:])
    grad_query = joined(
        over_seq[:, 1, :, :head_dim].astype(f32) + over_seq[:, 1, :, head_dim:].astype(f32)
    )
    latent = latents[0].astype(f32)
    cotangent = d_out[0]
    out = (latent + jnp.dot(mixed_b, w_out, preferred_element_type=f32)).astype(bf16)
    d_normed = lax.dot_general(d_query, w_query, LAST, preferred_element_type=f32)
    d_latents = (cotangent.astype(f32) + rms_back(latent, d_normed)).astype(bf16)
    return (out[None], d_latents[None], grad_query, grad_outproj, grad_kv)


def solution(mesh):
    chips = Mesh(mesh.devices.reshape(4, 2, 4, 4), ("x", "core", "z", "y"))
    in_specs = (
        P(BATCH, None, None),
        P(ALL, None, None),
        P(ALL),
        P(ALL),
        P(),
        P(),
        P(),
        P(BATCH, None, None),
    )
    out_specs = (
        P(BATCH, None, None),
        P(BATCH, None, None),
        P(SEQ, None),
        P(SEQ, None),
        P(ALL, None),
    )
    return jax.shard_map(local, mesh=chips, in_specs=in_specs, out_specs=out_specs, check_vma=False)
```

time: 248 us -> 193 us (0.78)
  local copies, waits for them, and re-layouts: 58 us -> 32.1 us
  Pallas kernels: 0 us -> 25.7 us
  matrix products: 37.3 us -> 20.8 us
  between operations: 16.9 us -> 1.12 us
  other arithmetic: 19.2 us -> 7.36 us
  blocking collectives: 10.6 us -> 0 us
  waiting for transfers between devices: 48 us -> 52.4 us
  starting transfers between devices: 56 us -> 52.7 us
    pallas_call x0 -> x5, Pallas kernels: none -> 25.7 us  [the longest x1 11.3 us: gradients(): pl.pallas_call(grads_kernel, grid=(4,), out_shape=(jax.ShapeDtypeStruct((...]
    reshape x12 -> x3, local copies, waits for them, and re-layouts: 25.7 us -> 1.94 us  [joined(): return part.transpose(1, 0, 2).reshape(part.shape[1], model_width)]
    dot_general x12 -> x4, matrix products: 26.9 us -> 11.1 us  [the longest x1 4.54 us: local(): lax.dot_general(normed_both, d_half, FIRST, preferred_element_type=f32)]
    all_to_all x1 -> x0, blocking collectives: 10.6 us -> none  [exchange(): return lax.all_to_all(values, axes, 0, 0, tiled=True)]
    all_to_all x7, starting transfers between devices: 43.8 us -> 35.7 us  [exchange(): return lax.all_to_all(values, axes, 0, 0, tiled=True)]
    all_to_all x7, waiting for transfers between devices: 48 us -> 52.4 us  [exchange(): return lax.all_to_all(values, axes, 0, 0, tiled=True)]
    ppermute x5 -> x11, starting transfers between devices: 4.3 us -> 8.44 us  [other_core(): return lax.ppermute(values, 'core', [(0, 1), (1, 0)])]
    slice x4 -> x0, local copies, waits for them, and re-layouts: 3.76 us -> none  [the longest x1 1.53 us: local(): keys = pairs[:, :model_width].reshape(blocks, block_rows, H, head_dim)]
  transfers between devices with their start and end apart: 18 -> 24, of which waited for: 7 -> 7; matrix products, arithmetic and copies ran while one was open for 36% -> 27% of each run, Pallas kernels for 0% -> 2%
where the time goes in v2:
time: 193 us; the launch traced here: 192 us
  starting transfers between devices  52.7 us (27%)
  waiting for transfers between devices  52.4 us (27%)
  local copies, waits for them, and re-layouts  32.1 us (17%)
  Pallas kernels  25.7 us (13%)
  matrix products  20.8 us (11%)
  other arithmetic  7.36 us (4%)
    all_to_all x7, waiting for transfers between devices, exchange(): return lax.all_to_all(values, axes, 0, 0, tiled=True)  52.4 us
    all_to_all x7, starting transfers between devices, exchange(): return lax.all_to_all(values, axes, 0, 0, tiled=True)  35.7 us
    unnamed x90, local copies, waits for them, and re-layouts  16.1 us
    pallas_call x1, Pallas kernels, gradients(): pl.pallas_call(grads_kernel, grid=(4,), out_shape=(jax.ShapeDtypeStruct((...  11.3 us
    ppermute x6, starting transfers between devices, chip_step(): return lax.ppermute(values, 'x', [(i, (i + step) % 4) for i in range(4)])  8.57 us
    ppermute x11, starting transfers between devices, other_core(): return lax.ppermute(values, 'core', [(0, 1), (1, 0)])  8.44 us
    pallas_call x2, Pallas kernels, project(): pl.pallas_call(functools.partial(project_kernel, norm, transposed), out_s...  7.82 us
    dot_general x1, matrix products, local(): pairs = jnp.dot(normed, w_kv, preferred_element_type=f32).astype(bf16)  6.51 us
  transfers between devices with their start and end apart: 24, of which 7 were waited for; matrix products, arithmetic and copies ran while one was open for 27% of the time, Pallas kernels for 2%

profile of v2, /device:TPU:1, one launch (start us, length us, event | category | flops | bytes accessed | tf_op | source)
XLA Modules:
  0.0 192.1 jit_solution(10822094829864450389)
XLA Ops:
  2.8 2.5 %collective-permute-start.1 = (bf16[64,1024]{1,0:T(8,128)(2,1)}, bf16[64,1024]{1,0:T(8,128)(2,1)S(1)}, u32[]{:S(2)}, u32[]{:S(2)}) collective-permute-start(bf16[64,1024]{1,0:T(8,128)(2,1)} %bitcast.81), channel_id=1, source_target_pairs={{0,64},{32,96},{64,0},{96,32},{1,65},{33,97},{65,1},{97,33},{2,66}... | collective-permute-start | bytes 393224 | tf_op jit(solution)/shard_map/ppermute | solution.py:49
  14.6 6.5 %convolution_convert_fusion.1.pairs_ref = bf16[512,2048]{1,0:T(8,128)(2,1)} fusion(bf16[512,1152]{1,0:T(8,128)(2,1)S(1)} %bitcast.90, bf16[1152,2048]{1,0:T(8,128)(2,1)} %param.13), kind=kOutput, calls=%fused_computation.2 | convolution fusion | flops 2416967680 | bytes 7995392 | tf_op jit(solution)/shard_map/dot_general | solution.py:328
  24.0 4.0 %shard_map.119.q_ref = bf16[256,1024]{1,0:T(8,128)(2,1)} custom-call(s32[4]{0:T(128)} %fusion.36.places, bf16[64,1024]{1,0:T(8,128)(2,1)} %bitcast.84, bf16[64,1024]{1,0:T(8,128)(2,1)} %copy-done.23, bf16[64,1024]{1,0:T(8,128)(2,1)} %copy-done.17, bf16[64,1024]{1,0:T(8,128)(2,1)} %copy-done.19, bf16[64,1024]{1,0:T(8,128)(2,1)} %copy-done.21, ...), custom_call_target="tpu_custom_call" | custom-call | flops 536870912 | bytes 4194304 | tf_op jit(solution)/shard_map/pallas_call | solution.py:94
  29.4 3.9 %shard_map.120.d_ref = bf16[256,1024]{1,0:T(8,128)(2,1)} custom-call(s32[4]{0:T(128)} %fusion.36.places, bf16[64,1024]{1,0:T(8,128)(2,1)} %bitcast.86, bf16[64,1024]{1,0:T(8,128)(2,1)} %copy-done.7, bf16[64,1024]{1,0:T(8,128)(2,1)} %copy-done.9, bf16[64,1024]{1,0:T(8,128)(2,1)} %copy-done.11, bf16[64,1024]{1,0:T(8,128)(2,1)} %copy-done.13, ...), custom_call_target="tpu_custom_call" | custom-call | flops 536870912 | bytes 4194304 | tf_op jit(solution)/shard_map/pallas_call | solution.py:94
  33.2 4.9 %shard_map.121 = f32[8,16,256]{2,1,0:T(8,128)} custom-call(s32[4]{0:T(128)} %counts.3, s32[4]{0:T(128)} %groups.3, bf16[256,1024]{1,0:T(8,128)(2,1)} %shard_map.119.q_ref, bf16[256,1024]{1,0:T(8,128)(2,1)} %shard_map.120.d_ref, bf16[512,2048]{1,0:T(8,128)(2,1)} %convolution_convert_fusion.1.pairs_ref), custom_call_target="tpu_custom_call" | custom-call | flops 4294967296 | bytes 4194304 | tf_op jit(solution)/shard_map/pallas_call | solution.py:193
  39.8 9.9 %all-to-all-start = ((f32[128,1,256]{2,1,0:T(1,128)}), f32[128,1,256]{2,1,0:T(1,128)S(1)}, u32[]{:S(2)}, u32[]{:S(2)}) async-start(f32[128,1,256]{2,1,0:T(1,128)} %copy.30), calls=%async_computation | async-start | bytes 262144 | tf_op jit(solution)/shard_map/all_to_all | solution.py:37
  50.5 9.5 %all-to-all-done = f32[128,1,256]{2,1,0:T(1,128)S(1)} async-done(((f32[128,1,256]{2,1,0:T(1,128)}), f32[128,1,256]{2,1,0:T(1,128)S(1)}, u32[]{:S(2)}, u32[]{:S(2)}) %all-to-all-start) | async-done | bytes 131104 | tf_op jit(solution)/shard_map/all_to_all | solution.py:37
  64.1 4.0 %all-to-all-start.1 = ((f32[128,1,256]{2,1,0:T(1,128)}), f32[128,1,256]{2,1,0:T(1,128)S(1)}, u32[]{:S(2)}, u32[]{:S(2)}) async-start(f32[128,1,256]{2,1,0:T(1,128)} %copy.32), calls=%async_computation.1 | async-start | bytes 262144 | tf_op jit(solution)/shard_map/all_to_all | solution.py:37
  69.5 8.9 %all-to-all-done.1 = f32[128,1,256]{2,1,0:T(1,128)S(1)} async-done(((f32[128,1,256]{2,1,0:T(1,128)}), f32[128,1,256]{2,1,0:T(1,128)S(1)}, u32[]{:S(2)}, u32[]{:S(2)}) %all-to-all-start.1) | async-done | bytes 131104 | tf_op jit(solution)/shard_map/all_to_all | solution.py:37
  79.0 11.3 %shard_map.123 = (bf16[2,512,1024]{2,1,0:T(8,128)(2,1)}, bf16[16,3,64,128]{3,2,1,0:T(8,128)(2,1)}) custom-call(s32[4]{0:T(128)} %counts.3, s32[4]{0:T(128)} %groups.3, s32[1]{0:T(128)} %bitcast.6.core, bf16[256,1024]{1,0:T(8,128)(2,1)} %shard_map.119.q_ref, bf16[256,1024]{1,0:T(8,128)(2,1)} %shard_map.120.d_ref, ...), custom_call_target="tpu_custom_call" | custom-call | flops 8589934592 | bytes 8388608 | tf_op jit(solution)/shard_map/pallas_call | solution.py:295
  90.3 3.8 %all-to-all-start.2 = ((bf16[16,3,64,128]{3,2,1,0:T(8,128)(2,1)}), bf16[16,3,64,128]{3,2,1,0:T(8,128)(2,1)S(1)}, u32[]{:S(2)}, u32[]{:S(2)}) async-start(bf16[16,3,64,128]{3,2,1,0:T(8,128)(2,1)} %get-tuple-element.10), calls=%async_computation.2 | async-start | bytes 1572864 | tf_op jit(solution)/shard_map/all_to_all | solution.py:37
  98.2 9.5 %all-to-all-done.2 = bf16[16,3,64,128]{3,2,1,0:T(8,128)(2,1)S(1)} async-done(((bf16[16,3,64,128]{3,2,1,0:T(8,128)(2,1)}), bf16[16,3,64,128]{3,2,1,0:T(8,128)(2,1)S(1)}, u32[]{:S(2)}, u32[]{:S(2)}) %all-to-all-start.2) | async-done | bytes 786464 | tf_op jit(solution)/shard_map/all_to_all | solution.py:37
  109.0 4.9 %all-to-all-start.3 = ((f32[8,64,128]{2,1,0:T(8,128)}), f32[8,64,128]{2,1,0:T(8,128)S(1)}, u32[]{:S(2)}, u32[]{:S(2)}) async-start(f32[8,64,128]{2,1,0:T(8,128)} %copy.34), calls=%async_computation.3 | async-start | bytes 524288 | tf_op jit(solution)/shard_map/all_to_all | solution.py:37
  115.6 4.8 %all-to-all-done.3 = f32[8,64,128]{2,1,0:T(8,128)S(1)} async-done(((f32[8,64,128]{2,1,0:T(8,128)}), f32[8,64,128]{2,1,0:T(8,128)S(1)}, u32[]{:S(2)}, u32[]{:S(2)}) %all-to-all-start.3) | async-done | bytes 262176 | tf_op jit(solution)/shard_map/all_to_all | solution.py:37
  121.1 4.3 %all-to-all-start.4 = ((bf16[8,64,128]{2,1,0:T(8,128)(2,1)}), bf16[8,64,128]{2,1,0:T(8,128)(2,1)S(1)}, u32[]{:S(2)}, u32[]{:S(2)}) async-start(bf16[8,64,128]{2,1,0:T(8,128)(2,1)} %broadcast_in_dim.13), calls=%async_computation.4 | async-start | bytes 262144 | tf_op jit(solution)/shard_map/all_to_all | solution.py:37
  127.1 3.6 %all-to-all-done.4 = bf16[8,64,128]{2,1,0:T(8,128)(2,1)S(1)} async-done(((bf16[8,64,128]{2,1,0:T(8,128)(2,1)}), bf16[8,64,128]{2,1,0:T(8,128)(2,1)S(1)}, u32[]{:S(2)}, u32[]{:S(2)}) %all-to-all-start.4) | async-done | bytes 131104 | tf_op jit(solution)/shard_map/all_to_all | solution.py:37
  133.8 3.6 %all-to-all-start.5 = ((bf16[16,2,64,128]{3,2,1,0:T(8,128)(2,1)}), bf16[16,2,64,128]{3,2,1,0:T(8,128)(2,1)S(1)}, u32[]{:S(2)}, u32[]{:S(2)}) async-start(bf16[16,2,64,128]{3,2,1,0:T(8,128)(2,1)} %copy.36), calls=%async_computation.5 | async-start | bytes 1048576 | tf_op jit(solution)/shard_map/all_to_all | solution.py:37
  137.5 4.5 %fusion.10 = bf16[144,8,8,128]{3,1,2,0:T(8,128)(2,1)S(1)} fusion(bf16[512,1024]{1,0:T(8,128)(2,1)} %collective-permute-done.15, bf16[512,1024]{1,0:T(8,128)(2,1)} %get-tuple-element.15, bf16[512,1152]{1,0:T(8,128)(2,1)} %collective-permute-done.14, bf16[512,1152]{1,0:T(8,128)(2,1)S(1)} %bitcast.92), kind=kOutput, calls=%fused_computation.17 | convolution fusion | flops 2426011648 | bytes 6815744 | tf_op jit(solution)/shard_map/dot_general | solution.py:345
  144.3 3.5 %all-to-all-done.5 = bf16[16,2,64,128]{3,2,1,0:T(8,128)(2,1)S(1)} async-done(((bf16[16,2,64,128]{3,2,1,0:T(8,128)(2,1)}), bf16[16,2,64,128]{3,2,1,0:T(8,128)(2,1)S(1)}, u32[]{:S(2)}, u32[]{:S(2)}) %all-to-all-start.5) | async-done | bytes 524320 | tf_op jit(solution)/shard_map/all_to_all | solution.py:37
  147.8 5.2 %all-to-all-start.6 = ((bf16[64,18,8,128]{3,2,1,0:T(8,128)(2,1)}), bf16[64,18,8,128]{3,2,1,0:T(8,128)(2,1)S(1)}, u32[]{:S(2)}, u32[]{:S(2)}) async-start(bf16[64,18,8,128]{3,2,1,0:T(8,128)(2,1)} %bitcast.30), calls=%async_computation.6 | async-start | bytes 4718592 | tf_op jit(solution)/shard_map/all_to_all | solution.py:37
  166.8 2.5 %fusion.23 = (f32[64]{0:T(128)S(1)}, f32[64,1024]{1,0:T(8,128)S(1)}) fusion(f32[64]{0:T(128)S(1)} %add_rsqrt_fusion.2, bf16[1,64,1024]{2,1,0:T(8,128)(2,1)S(1)} %copy-done, bf16[64,1024]{1,0:T(8,128)(2,1)S(1)} %reshape.85, bf16[1024,1024]{1,0:T(8,128)(2,1)} %refs_8_.2), kind=kOutput, calls=%fused_computation.33 | convolution fusion | flops 134479808 | bytes 2621952 | tf_op jit(solution)/shard_map/dot_general | solution.py:403
  170.2 12.5 %all-to-all-done.6 = bf16[64,18,8,128]{3,2,1,0:T(8,128)(2,1)S(1)} async-done(((bf16[64,18,8,128]{3,2,1,0:T(8,128)(2,1)}), bf16[64,18,8,128]{3,2,1,0:T(8,128)(2,1)S(1)}, u32[]{:S(2)}, u32[]{:S(2)}) %all-to-all-start.6) | async-done | bytes 2359328 | tf_op jit(solution)/shard_map/all_to_all | solution.py:37
  183.1 4.4 %collective-permute-start.16 = (f32[9,1024]{1,0:T(8,128)S(1)}, f32[9,1024]{1,0:T(8,128)S(1)}, u32[]{:S(2)}, u32[]{:S(2)}) collective-permute-start(f32[9,1024]{1,0:T(8,128)S(1)} %get-tuple-element.20), channel_id=1, source_target_pairs={{0,16},{16,0},{1,17},{17,1},{2,18},{18,2},{3,19},{19,3},{4,20},{20... | collective-permute-start | bytes 110600 | tf_op jit(solution)/shard_map/ppermute | solution.py:45
  187.5 2.7 %fusion.16 = bf16[1,64,1024]{2,1,0:T(8,128)(2,1)} fusion(bf16[64,1024]{1,0:T(8,128)(2,1)S(1)} %copy-done.6, bf16[1024,1024]{1,0:T(8,128)(2,1)} %refs_8_.3, bf16[1,64,1024]{2,1,0:T(8,128)(2,1)S(1)} %copy-done), kind=kOutput, calls=%fused_computation.21 | convolution fusion | flops 134414336 | bytes 2490368 | tf_op jit(solution)/shard_map/dot_general | solution.py:402
  (165 shorter events, 56.0 us)
Async XLA Ops:
  0.6 10.7 %collective-permute-start = (bf16[64,1024]{1,0:T(8,128)(2,1)}, bf16[64,1024]{1,0:T(8,128)(2,1)S(1)}, u32[]{:S(2)}, u32[]{:S(2)}) collective-permute-start(bf16[64,1024]{1,0:T(8,128)(2,1)} %bitcast.80), channel_id=1, source_target_pairs={{0,32},{32,64},{64,96},{96,0},{1,33},{33,65},{65,97},{97,1},{2,34}... | collective-permute-start | bytes 393224 | tf_op jit(solution)/shard_map/ppermute | solution.py:49
  2.8 9.3 %collective-permute-start.1 = (bf16[64,1024]{1,0:T(8,128)(2,1)}, bf16[64,1024]{1,0:T(8,128)(2,1)S(1)}, u32[]{:S(2)}, u32[]{:S(2)}) collective-permute-start(bf16[64,1024]{1,0:T(8,128)(2,1)} %bitcast.81), channel_id=1, source_target_pairs={{0,64},{32,96},{64,0},{96,32},{1,65},{33,97},{65,1},{97,33},{2,66}... | collective-permute-start | bytes 393224 | tf_op jit(solution)/shard_map/ppermute | solution.py:49
  5.2 8.7 %collective-permute-start.2 = (bf16[64,1024]{1,0:T(8,128)(2,1)}, bf16[64,1024]{1,0:T(8,128)(2,1)S(1)}, u32[]{:S(2)}, u32[]{:S(2)}) collective-permute-start(bf16[64,1024]{1,0:T(8,128)(2,1)} %bitcast.82), channel_id=1, source_target_pairs={{0,96},{32,0},{64,32},{96,64},{1,97},{33,1},{65,33},{97,65},{2,98}... | collective-permute-start | bytes 393224 | tf_op jit(solution)/shard_map/ppermute | solution.py:49
  6.4 8.1 %collective-permute-start.3 = (bf16[64,1024]{1,0:T(8,128)(2,1)}, bf16[64,1024]{1,0:T(8,128)(2,1)S(1)}, u32[]{:S(2)}, u32[]{:S(2)}) collective-permute-start(bf16[64,1024]{1,0:T(8,128)(2,1)} %bitcast.83), channel_id=1, source_target_pairs={{0,16},{16,0},{1,17},{17,1},{2,18},{18,2},{3,19},{19,3},{4,20},{20... | collective-permute-start | bytes 393224 | tf_op jit(solution)/shard_map/ppermute | solution.py:45
  7.9 13.3 %collective-permute-start.7 = (bf16[64,1024]{1,0:T(8,128)(2,1)}, bf16[64,1024]{1,0:T(8,128)(2,1)S(1)}, u32[]{:S(2)}, u32[]{:S(2)}) collective-permute-start(bf16[64,1024]{1,0:T(8,128)(2,1)} %bitcast.85), channel_id=1, source_target_pairs={{0,32},{32,64},{64,96},{96,0},{1,33},{33,65},{65,97},{97,1},{2,34}... | collective-permute-start | bytes 393224 | tf_op jit(solution)/shard_map/ppermute | solution.py:49
  11.4 10.3 %collective-permute-start.8 = (bf16[64,1024]{1,0:T(8,128)(2,1)S(1)}, bf16[64,1024]{1,0:T(8,128)(2,1)S(1)}, u32[]{:S(2)}, u32[]{:S(2)}) collective-permute-start(bf16[64,1024]{1,0:T(8,128)(2,1)S(1)} %bitcast.87), channel_id=1, source_target_pairs={{0,64},{32,96},{64,0},{96,32},{1,65},{33,97},{65,1},{97,33},{2,66}... | collective-permute-start | bytes 393224 | tf_op jit(solution)/shard_map/ppermute | solution.py:49
  12.0 9.8 %collective-permute-start.9 = (bf16[64,1024]{1,0:T(8,128)(2,1)S(1)}, bf16[64,1024]{1,0:T(8,128)(2,1)S(1)}, u32[]{:S(2)}, u32[]{:S(2)}) collective-permute-start(bf16[64,1024]{1,0:T(8,128)(2,1)S(1)} %bitcast.88), channel_id=1, source_target_pairs={{0,96},{32,0},{64,32},{96,64},{1,97},{33,1},{65,33},{97,65},{2,98}... | collective-permute-start | bytes 393224 | tf_op jit(solution)/shard_map/ppermute | solution.py:49
  13.9 8.3 %collective-permute-start.4 = (bf16[64,1024]{1,0:T(8,128)(2,1)S(1)}, bf16[64,1024]{1,0:T(8,128)(2,1)S(1)}, u32[]{:S(2)}, u32[]{:S(2)}) collective-permute-start(bf16[64,1024]{1,0:T(8,128)(2,1)S(1)} %collective-permute-done.refs_1_), channel_id=1, source_target_pairs={{0,16},{16,0},{1,17},{17,1},{2,18},{18,2},{3,19},{19,3},{4,20},{20... | collective-permute-start | bytes 393224 | tf_op jit(solution)/shard_map/ppermute | solution.py:45
  14.5 7.9 %collective-permute-start.5 = (bf16[64,1024]{1,0:T(8,128)(2,1)S(1)}, bf16[64,1024]{1,0:T(8,128)(2,1)S(1)}, u32[]{:S(2)}, u32[]{:S(2)}) collective-permute-start(bf16[64,1024]{1,0:T(8,128)(2,1)S(1)} %collective-permute-done.1.refs_2_), channel_id=1, source_target_pairs={{0,16},{16,0},{1,17},{17,1},{2,18},{18,2},{3,19},{19,3},{4,20},{20... | collective-permute-start | bytes 393224 | tf_op jit(solution)/shard_map/ppermute | solution.py:45
  21.1 6.8 %collective-permute-start.10 = (bf16[64,1024]{1,0:T(8,128)(2,1)S(1)}, bf16[64,1024]{1,0:T(8,128)(2,1)S(1)}, u32[]{:S(2)}, u32[]{:S(2)}) collective-permute-start(bf16[64,1024]{1,0:T(8,128)(2,1)S(1)} %bitcast.89), channel_id=1, source_target_pairs={{0,16},{16,0},{1,17},{17,1},{2,18},{18,2},{3,19},{19,3},{4,20},{20... | collective-permute-start | bytes 393224 | tf_op jit(solution)/shard_map/ppermute | solution.py:45
  21.6 1.7 collective-permute-start.6
  21.8 6.1 %collective-permute-start.11 = (bf16[64,1024]{1,0:T(8,128)(2,1)S(1)}, bf16[64,1024]{1,0:T(8,128)(2,1)S(1)}, u32[]{:S(2)}, u32[]{:S(2)}) collective-permute-start(bf16[64,1024]{1,0:T(8,128)(2,1)S(1)} %collective-permute-done.7.refs_1_), channel_id=1, source_target_pairs={{0,16},{16,0},{1,17},{17,1},{2,18},{18,2},{3,19},{19,3},{4,20},{20... | collective-permute-start | bytes 393224 | tf_op jit(solution)/shard_map/ppermute | solution.py:45
  22.2 5.7 %collective-permute-start.12 = (bf16[64,1024]{1,0:T(8,128)(2,1)S(1)}, bf16[64,1024]{1,0:T(8,128)(2,1)S(1)}, u32[]{:S(2)}, u32[]{:S(2)}) collective-permute-start(bf16[64,1024]{1,0:T(8,128)(2,1)S(1)} %collective-permute-done.8.refs_2_), channel_id=1, source_target_pairs={{0,16},{16,0},{1,17},{17,1},{2,18},{18,2},{3,19},{19,3},{4,20},{20... | collective-permute-start | bytes 393224 | tf_op jit(solution)/shard_map/ppermute | solution.py:45
  22.4 5.6 %collective-permute-start.13 = (bf16[64,1024]{1,0:T(8,128)(2,1)S(1)}, bf16[64,1024]{1,0:T(8,128)(2,1)S(1)}, u32[]{:S(2)}, u32[]{:S(2)}) collective-permute-start(bf16[64,1024]{1,0:T(8,128)(2,1)S(1)} %collective-permute-done.9.refs_3_), channel_id=1, source_target_pairs={{0,16},{16,0},{1,17},{17,1},{2,18},{18,2},{3,19},{19,3},{4,20},{20... | collective-permute-start | bytes 393224 | tf_op jit(solution)/shard_map/ppermute | solution.py:45
  39.8 20.2 %all-to-all-start = ((f32[128,1,256]{2,1,0:T(1,128)}), f32[128,1,256]{2,1,0:T(1,128)S(1)}, u32[]{:S(2)}, u32[]{:S(2)}) async-start(f32[128,1,256]{2,1,0:T(1,128)} %copy.30), calls=%async_computation | async-start | bytes 262144 | tf_op jit(solution)/shard_map/all_to_all | solution.py:37
  64.1 14.2 %all-to-all-start.1 = ((f32[128,1,256]{2,1,0:T(1,128)}), f32[128,1,256]{2,1,0:T(1,128)S(1)}, u32[]{:S(2)}, u32[]{:S(2)}) async-start(f32[128,1,256]{2,1,0:T(1,128)} %copy.32), calls=%async_computation.1 | async-start | bytes 262144 | tf_op jit(solution)/shard_map/all_to_all | solution.py:37
  90.3 17.4 %all-to-all-start.2 = ((bf16[16,3,64,128]{3,2,1,0:T(8,128)(2,1)}), bf16[16,3,64,128]{3,2,1,0:T(8,128)(2,1)S(1)}, u32[]{:S(2)}, u32[]{:S(2)}) async-start(bf16[16,3,64,128]{3,2,1,0:T(8,128)(2,1)} %get-tuple-element.10), calls=%async_computation.2 | async-start | bytes 1572864 | tf_op jit(solution)/shard_map/all_to_all | solution.py:37
  109.0 11.4 %all-to-all-start.3 = ((f32[8,64,128]{2,1,0:T(8,128)}), f32[8,64,128]{2,1,0:T(8,128)S(1)}, u32[]{:S(2)}, u32[]{:S(2)}) async-start(f32[8,64,128]{2,1,0:T(8,128)} %copy.34), calls=%async_computation.3 | async-start | bytes 524288 | tf_op jit(solution)/shard_map/all_to_all | solution.py:37
  115.4 22.1 %collective-permute-start.14 = (bf16[512,1152]{1,0:T(8,128)(2,1)}, bf16[512,1152]{1,0:T(8,128)(2,1)}, u32[]{:S(2)}, u32[]{:S(2)}) collective-permute-start(bf16[512,1152]{1,0:T(8,128)(2,1)} %bitcast.91), channel_id=1, source_target_pairs={{0,16},{16,0},{1,17},{17,1},{2,18},{18,2},{3,19},{19,3},{4,20},{20... | collective-permute-start | bytes 3538952 | tf_op jit(solution)/shard_map/ppermute | solution.py:45
  121.1 9.6 %all-to-all-start.4 = ((bf16[8,64,128]{2,1,0:T(8,128)(2,1)}), bf16[8,64,128]{2,1,0:T(8,128)(2,1)S(1)}, u32[]{:S(2)}, u32[]{:S(2)}) async-start(bf16[8,64,128]{2,1,0:T(8,128)(2,1)} %broadcast_in_dim.13), calls=%async_computation.4 | async-start | bytes 262144 | tf_op jit(solution)/shard_map/all_to_all | solution.py:37
  127.0 10.5 %collective-permute-start.15 = (bf16[512,1024]{1,0:T(8,128)(2,1)}, bf16[512,1024]{1,0:T(8,128)(2,1)}, u32[]{:S(2)}, u32[]{:S(2)}) collective-permute-start(bf16[512,1024]{1,0:T(8,128)(2,1)} %get-tuple-element.16), channel_id=1, source_target_pairs={{0,16},{16,0},{1,17},{17,1},{2,18},{18,2},{3,19},{19,3},{4,20},{20... | collective-permute-start | bytes 3145736 | tf_op jit(solution)/shard_map/ppermute | solution.py:45
  133.8 14.0 %all-to-all-start.5 = ((bf16[16,2,64,128]{3,2,1,0:T(8,128)(2,1)}), bf16[16,2,64,128]{3,2,1,0:T(8,128)(2,1)S(1)}, u32[]{:S(2)}, u32[]{:S(2)}) async-start(bf16[16,2,64,128]{3,2,1,0:T(8,128)(2,1)} %copy.36), calls=%async_computation.5 | async-start | bytes 1048576 | tf_op jit(solution)/shard_map/all_to_all | solution.py:37
  147.8 35.0 %all-to-all-start.6 = ((bf16[64,18,8,128]{3,2,1,0:T(8,128)(2,1)}), bf16[64,18,8,128]{3,2,1,0:T(8,128)(2,1)S(1)}, u32[]{:S(2)}, u32[]{:S(2)}) async-start(bf16[64,18,8,128]{3,2,1,0:T(8,128)(2,1)} %bitcast.30), calls=%async_computation.6 | async-start | bytes 4718592 | tf_op jit(solution)/shard_map/all_to_all | solution.py:37
  183.1 8.3 %collective-permute-start.16 = (f32[9,1024]{1,0:T(8,128)S(1)}, f32[9,1024]{1,0:T(8,128)S(1)}, u32[]{:S(2)}, u32[]{:S(2)}) collective-permute-start(f32[9,1024]{1,0:T(8,128)S(1)} %get-tuple-element.20), channel_id=1, source_target_pairs={{0,16},{16,0},{1,17},{17,1},{2,18},{18,2},{3,19},{19,3},{4,20},{20... | collective-permute-start | bytes 110600 | tf_op jit(solution)/shard_map/ppermute | solution.py:45
  (33 other events, 295.0 us)

commit v3 on v2

--- a/solution.py
+++ b/solution.py
@@ -45,8 +45,12 @@
     return lax.ppermute(values, "core", [(0, 1), (1, 0)])
 
 
+def ring_step(values, axis, step):
+    return lax.ppermute(values, axis, [(i, (i + step) % 4) for i in range(4)])
+
+
 def chip_step(values, step):
-    return lax.ppermute(values, "x", [(i, (i + step) % 4) for i in range(4)])
+    return ring_step(values, "x", step)
 
 
 def gather_batch(values):
@@ -81,11 +85,15 @@
             def _():
                 picked[i * rows : (i + 1) * rows, :] = pieces[j][...]
 
-    x = picked[...]
     if norm:
-        x = normalize(x)
-    numbers = LAST if transposed else (((1,), (0,)), ((), ()))
-    out_ref[...] = lax.dot_general(x, w_ref[...], numbers, preferred_element_type=f32).astype(bf16)
+        picked[...] = normalize(picked[...])
+    for at in range(0, out_ref.shape[1], 256):
+        tile = slice(at, at + 256)
+        if transposed:
+            part = lax.dot_general(picked[...], w_ref[tile, :], LAST, preferred_element_type=f32)
+        else:
+            part = jnp.dot(picked[...], w_ref[:, tile], preferred_element_type=f32)
+        out_ref[:, tile] = part.astype(bf16)
 
 
 def project(places, pieces, weight, norm, transposed):
@@ -103,6 +111,38 @@
             transcendentals=0,
         ),
     )(places, *pieces, weight)
+
+
+def pairs_kernel(frames_ref, w_ref, normed_ref, out_ref):
+    @pl.when(pl.program_id(0) == 0)
+    def _():
+        normed_ref[...] = normalize(frames_ref[...])
+
+    out_ref[...] = jnp.dot(normed_ref[...], w_ref[...], preferred_element_type=f32).astype(bf16)
+
+
+def project_pairs(frames, w_kv):
+    rows, feature = frames.shape
+    width, tile = w_kv.shape[1], 256
+    return pl.pallas_call(
+        pairs_kernel,
+        grid=(width // tile,),
+        out_shape=(
+            jax.ShapeDtypeStruct((rows, feature), bf16),
+            jax.ShapeDtypeStruct((rows, width), bf16),
+        ),
+        in_specs=[
+            pl.BlockSpec((rows, feature), lambda i: (0, 0)),
+            pl.BlockSpec((feature, tile), lambda i: (0, i)),
+        ],
+        out_specs=(
+            pl.BlockSpec((rows, feature), lambda i: (0, 0)),
+            pl.BlockSpec((rows, tile), lambda i: (0, i)),
+        ),
+        cost_estimate=pl.CostEstimate(
+            flops=2 * rows * feature * width, bytes_accessed=9 * 1024 * 1024, transcendentals=0
+        ),
+    )(frames, w_kv)
 
 
 def low_lanes(shape):
@@ -174,10 +214,18 @@
                 factor = jnp.where(own[i] == g, jnp.exp(tops[i] - top), 0.0)
                 total = total + factor * total_ref[i]
                 moment = moment + factor * moment_ref[i]
-            out_ref[g, 0:8, 0:128] = jnp.where(left, top, pltpu.roll(total, 64, 1))
-            out_ref[g, 8:16, 0:128] = jnp.where(left, pltpu.roll(top, 64, 1), total)
-            out_ref[g, 0:8, 128:256] = jnp.where(left, moment, note)
-            out_ref[g, 8:16, 128:256] = jnp.where(left, pltpu.roll(moment, 64, 1), note)
+            parts = (
+                (jnp.where(left, top, pltpu.roll(total, 64, 1)), jnp.where(left, moment, note)),
+                (
+                    jnp.where(left, pltpu.roll(top, 64, 1), total),
+                    jnp.where(left, pltpu.roll(moment, 64, 1), note),
+                ),
+            )
+            for odd in range(2):
+                for p in range(8):
+                    at = 16 * g + 8 * odd + p
+                    out_ref[at, :, 0:128] = parts[odd][0][p : p + 1]
+                    out_ref[at, :, 128:256] = parts[odd][1][p : p + 1]
 
 
 def block_specs(latent_count, width):
@@ -193,9 +241,9 @@
     return pl.pallas_call(
         stats_kernel,
         grid=(4,),
-        out_shape=jax.ShapeDtypeStruct((8, 16, 256), f32),
+        out_shape=jax.ShapeDtypeStruct((128, 1, 256), f32),
         in_specs=[SMEM, SMEM] + block_specs(queries.shape[0] // 4, width),
-        out_specs=pl.BlockSpec((8, 16, 256), lambda i: (0, 0, 0)),
+        out_specs=pl.BlockSpec((128, 1, 256), lambda i: (0, 0, 0)),
         scratch_shapes=[pltpu.VMEM((4, 8, 128), f32)] * 3,
         cost_estimate=pl.CostEstimate(
             flops=4 * 1024 * 1024 * 1024, bytes_accessed=4 * 1024 * 1024, transcendentals=512 * 1024
@@ -205,15 +253,18 @@
 
 def totals_kernel(in_ref, out_ref):
     left = low_lanes((1, 128))
-    first = in_ref[:, 0:128]
+    first = in_ref[:, 0, 0:128]
     top = jnp.max(first, axis=0, keepdims=True)
     top = jnp.where(left, top, pltpu.roll(top, 64, 1))
     factor = jnp.exp(jnp.where(left, first, pltpu.roll(first, 64, 1)) - top)
     total = jnp.sum(factor * first, axis=0, keepdims=True)
     inverse = 1.0 / jnp.where(left, pltpu.roll(total, 64, 1), total)
-    delta = jnp.sum(factor * in_ref[:, 128:256], axis=0, keepdims=True) * inverse
-    out_ref[:, 0:128] = jnp.broadcast_to(jnp.where(left, top, inverse), first.shape)
-    out_ref[:, 128:256] = jnp.broadcast_to(jnp.where(left, delta, 0.0), first.shape)
+    delta = jnp.sum(factor * in_ref[:, 0, 128:256], axis=0, keepdims=True) * inverse
+    reply = jnp.concatenate(
+        [jnp.where(left, top, inverse), jnp.where(left, delta, 0.0)], axis=1
+    )
+    for at in range(in_ref.shape[0]):
+        out_ref[at] = reply
 
 
 def totals(stats):
@@ -226,7 +277,20 @@
 
 
 def grads_kernel(
-    counts, groups, core, q_ref, d_ref, pairs_ref, reply_ref, d_pairs_ref, slotted_ref, mixed_acc, query_acc
+    counts,
+    groups,
+    core,
+    q_ref,
+    d_ref,
+    pairs_ref,
+    reply_ref,
+    kept_ref,
+    sent_ref,
+    slotted_ref,
+    mixed_acc,
+    query_acc,
+    mixed_now,
+    query_now,
 ):
     block = pl.program_id(0)
     low, high = half_masks()
@@ -246,12 +310,16 @@
     for i in range(1, 4):
         slot = jnp.where(block == i, slots[i], slot)
     group = groups[block]
-    even = reply_ref[group, 0:8, 0:128]
-    odd = reply_ref[group, 8:16, 0:128]
+    def reply_rows(odd, cols):
+        first = 16 * group + 8 * odd
+        return jnp.concatenate([reply_ref[first + p, :, cols] for p in range(8)], axis=0)
+
+    even = reply_rows(0, slice(0, 128))
+    odd = reply_rows(1, slice(0, 128))
     top = jnp.where(left, even, pltpu.roll(odd, 64, 1))
     inverse = jnp.where(left, pltpu.roll(even, 64, 1), odd)
     delta = jnp.where(
-        left, reply_ref[group, 0:8, 128:256], pltpu.roll(reply_ref[group, 8:16, 128:256], 64, 1)
+        left, reply_rows(0, slice(128, 256)), pltpu.roll(reply_rows(1, slice(128, 256)), 64, 1)
     )
     for p in range(width // 128):
         cols = slice(128 * p, 128 * p + 128)
@@ -265,14 +333,16 @@
         weights = jnp.where(usable, jnp.exp(s - top[p : p + 1]) * inverse[p : p + 1], 0.0)
         weights_b = weights.astype(bf16)
         d_scores = (weights * (dw - delta[p : p + 1]) * scale).astype(bf16)
-        d_pairs_ref[1 - core[0], :, cols] = jnp.dot(
-            weights_b, d, preferred_element_type=f32
-        ).astype(bf16)
-        d_pairs_ref[core[0], :, cols] = jnp.dot(d_scores, q, preferred_element_type=f32).astype(bf16)
+        d_values = jnp.dot(weights_b, d, preferred_element_type=f32)
+        d_keys = jnp.dot(d_scores, q, preferred_element_type=f32)
+        kept_ref[:, cols] = jnp.where(core[0] == 0, d_keys, d_values).astype(bf16)
+        sent_ref[:, cols] = jnp.where(core[0] == 0, d_values, d_keys).astype(bf16)
         mixed = lax.dot_general(weights_b, v, FIRST, preferred_element_type=f32)
-        mixed_acc[slot, :, cols] += jnp.where(wide, mixed[:rows], mixed[rows:])
+        mixed_now[:, cols] = jnp.where(wide, mixed[:rows], mixed[rows:])
         query = lax.dot_general(d_scores, k, FIRST, preferred_element_type=f32)
-        query_acc[slot, :, cols] += jnp.where(wide, query[:rows], query[rows:])
+        query_now[:, cols] = jnp.where(wide, query[:rows], query[rows:])
+    mixed_acc[slot] += mixed_now[...]
+    query_acc[slot] += query_now[...]
 
     @pl.when(block == 3)
     def _():
@@ -296,21 +366,133 @@
         grads_kernel,
         grid=(4,),
         out_shape=(
-            jax.ShapeDtypeStruct((2, pairs.shape[0], width), bf16),
+            jax.ShapeDtypeStruct((pairs.shape[0], width), bf16),
+            jax.ShapeDtypeStruct((pairs.shape[0], width), bf16),
             jax.ShapeDtypeStruct((H, SLOTS, rows, 128), bf16),
         ),
         in_specs=[SMEM, SMEM, SMEM]
         + block_specs(rows, width)
-        + [pl.BlockSpec((8, 16, 256), lambda i: (0, 0, 0))],
+        + [pl.BlockSpec((128, 1, 256), lambda i: (0, 0, 0))],
         out_specs=(
-            pl.BlockSpec((2, 128, width), lambda i: (0, i, 0)),
+            pl.BlockSpec((128, width), lambda i: (i, 0)),
+            pl.BlockSpec((128, width), lambda i: (i, 0)),
             pl.BlockSpec((H, SLOTS, rows, 128), lambda i: (0, 0, 0, 0)),
         ),
-        scratch_shapes=[pltpu.VMEM((SLOTS, rows, width), f32)] * 2,
+        scratch_shapes=[pltpu.VMEM((SLOTS, rows, width), f32)] * 2
+        + [pltpu.VMEM((rows, width), f32)] * 2,
         cost_estimate=pl.CostEstimate(
             flops=8 * 1024 * 1024 * 1024, bytes_accessed=8 * 1024 * 1024, transcendentals=512 * 1024
         ),
     )(counts, groups, core, queries, d_mixed, pairs, reply)
+
+
+def prepare_kernel(owners, *refs):
+    latents, d_outs, (latents_ref, d_out_ref) = refs[:8], refs[8:16], refs[16:]
+    rows = latents[0].shape[0]
+    for j in range(8):
+        at = pl.ds(pl.multiple_of(owners[j] * rows, rows), rows)
+        latents_ref[at, :] = normalize(latents[j][...])
+        d_out_ref[at, :] = d_outs[j][...]
+
+
+def prepare(owners, latents, d_outs):
+    rows, width = latents[0].shape
+    out = jax.ShapeDtypeStruct((8 * rows, width), bf16)
+    return pl.pallas_call(
+        prepare_kernel,
+        out_shape=(out, out),
+        in_specs=[SMEM] + [VMEM] * 16,
+        out_specs=(VMEM, VMEM),
+        cost_estimate=pl.CostEstimate(
+            flops=4 * 1024 * 1024, bytes_accessed=4 * 1024 * 1024, transcendentals=512
+        ),
+    )(owners, *latents, *d_outs)
+
+
+def by_group_kernel(source_groups, in_ref, out_ref):
+    out_ref[...] = jnp.zeros_like(out_ref)
+    for source in range(in_ref.shape[0]):
+        for slot in range(SLOTS):
+            group = source_groups[source * SLOTS + slot]
+
+            @pl.when(group >= 0)
+            def _():
+                out_ref[group] += in_ref[source, slot].astype(f32)
+
+
+def by_group(source_groups, slotted):
+    return pl.pallas_call(
+        by_group_kernel,
+        out_shape=jax.ShapeDtypeStruct((8,) + slotted.shape[2:], f32),
+        in_specs=[SMEM, VMEM],
+        out_specs=VMEM,
+    )(source_groups, slotted)
+
+
+def owners_kernel(heads_ref, owned_ref, latents_ref, d_out_ref, outproj_ref, out_ref):
+    rows = outproj_ref.shape[0]
+    heads = heads_ref[...]
+    outproj_ref[...] = lax.dot_general(
+        heads, d_out_ref[...], FIRST, preferred_element_type=f32
+    )[:rows]
+    query = lax.dot_general(latents_ref[...], heads, FIRST, preferred_element_type=f32)
+    high = query.astype(bf16).astype(f32)
+    query = jnp.where(low_lanes(query.shape), pltpu.roll(high, 64, 1), query - high).astype(bf16)
+    for at in range(H):
+        out_ref[at, :rows] = owned_ref[...]
+        out_ref[at, rows:] = query[rows * at : rows * at + rows]
+
+
+def owners(heads, owned, normed_latents, d_outs):
+    rows = owned.shape[0]
+    width = d_outs.shape[1]
+    return pl.pallas_call(
+        owners_kernel,
+        out_shape=(
+            jax.ShapeDtypeStruct((rows, width), f32),
+            jax.ShapeDtypeStruct((H, 2 * rows, 128), bf16),
+        ),
+        in_specs=[VMEM] * 4,
+        out_specs=(VMEM, VMEM),
+        cost_estimate=pl.CostEstimate(
+            flops=512 * 1024 * 1024, bytes_accessed=4 * 1024 * 1024, transcendentals=0
+        ),
+    )(heads, owned, normed_latents, d_outs)
+
+
+def finish_kernel(in_ref, latent_ref, d_out_ref, w_query_ref, w_out_ref, *refs):
+    out_ref, d_latents_ref, grad_query_ref, mixed, d_query = refs
+    rows = latent_ref.shape[0]
+    left = low_lanes((rows, 128))
+
+    def parts(head):
+        both = in_ref[head, rows : 2 * rows].astype(f32)
+        return in_ref[head, :rows].astype(f32), both + pltpu.roll(both, 64, 1)
+
+    for p in range(H // 2):
+        cols = slice(128 * p, 128 * p + 128)
+        even, even_grad = parts(2 * p)
+        odd, odd_grad = parts(2 * p + 1)
+        mixed[:, cols] = jnp.where(left, even, pltpu.roll(odd, 64, 1)).astype(bf16)
+        d_query[:, cols] = jnp.where(left, pltpu.roll(even, 64, 1), odd).astype(bf16)
+        grad_query_ref[:, cols] = jnp.where(left, even_grad, odd_grad)
+    latent = latent_ref[...].astype(f32)
+    update = jnp.dot(mixed[...], w_out_ref[...], preferred_element_type=f32)
+    out_ref[...] = (latent + update).astype(bf16)
+    d_normed = lax.dot_general(d_query[...], w_query_ref[...], LAST, preferred_element_type=f32)
+    d_latents_ref[...] = (d_out_ref[...].astype(f32) + rms_back(latent, d_normed)).astype(bf16)
+
+
+def finish(over_seq, latent, d_out, w_query, w_out):
+    rows, width = latent.shape
+    small = jax.ShapeDtypeStruct((rows, width), bf16)
+    return pl.pallas_call(
+        finish_kernel,
+        out_shape=(small, small, jax.ShapeDtypeStruct((rows, width), f32)),
+        in_specs=[VMEM] * 5,
+        out_specs=(VMEM,) * 3,
+        scratch_shapes=[pltpu.VMEM((rows, width), bf16)] * 2,
+    )(over_seq, latent, d_out, w_query, w_out)
 
 
 def local(latents, frames, counts, groups, w_query, w_kv, w_out, d_out):
@@ -324,29 +506,51 @@
 
     latents_all = gather_batch(latents[0])
     d_out_all = gather_batch(d_out[0])
-    normed = normalize(frames).reshape(rows, feature)
-    pairs = jnp.dot(normed, w_kv, preferred_element_type=f32).astype(bf16)
+    normed, pairs = project_pairs(frames.reshape(rows, feature), w_kv)
     places = place_of(groups)
     queries = project(places, latents_all, w_query, True, False)
     d_mixed = project(places, d_out_all, w_out, False, True)
     stats = statistics(counts, groups, queries, d_mixed, pairs)
     normed, stats = lax.optimization_barrier((normed, stats))
     normed_both = jnp.concatenate([normed, other_core(normed)], axis=0)
-    stats = exchange(stats.reshape(128, 256), ALL)
+    stats = exchange(stats, ALL)
     source_groups = lax.dynamic_slice(
-        stats, (batch_at * seq_count, 192), (seq_count, SLOTS)
-    )
-    reply = exchange(totals(stats), ALL).reshape(group_count, seq_count, 256)
-    d_pairs, slotted = gradients(
+        stats, (batch_at * seq_count, 0, 192), (seq_count, 1, SLOTS)
+    ).reshape(seq_count * SLOTS).astype(jnp.int32)
+    all_latents, all_d_out = prepare(
+        jnp.stack([group_at(j) for j in range(8)]), latents_all, d_out_all
+    )
+    reply, all_latents, all_d_out, normed_both = lax.optimization_barrier(
+        (totals(stats), all_latents, all_d_out, normed_both)
+    )
+    reply = exchange(reply, ALL)
+    kept, sent, slotted = gradients(
         counts, groups, core.reshape(1), queries, d_mixed, pairs, reply
     )
-
-    d_half = jnp.concatenate([d_pairs[0], other_core(d_pairs[1])], axis=0)
+    slotted = exchange(slotted, SEQ)
+
+    d_half = jnp.concatenate([kept, other_core(sent)], axis=0)
     term = lax.dot_general(normed_both, d_half, FIRST, preferred_element_type=f32).astype(bf16)
     share_rows = feature // 128
-    term = term.reshape(4, 2, seq_count, share_rows, 8, 128).transpose(0, 2, 1, 3, 4, 5)
-    term = exchange(term.reshape(64, 2 * share_rows, 8, 128), CHIPS)
-    chip_sum = jnp.sum(term.astype(f32), axis=0).reshape(2, share_rows, model_width)
+    term = term.reshape(group_count, 4, 4 * share_rows, 8, 128)
+    z_at = lax.axis_index("z")
+
+    def z_part(step):
+        return lax.dynamic_index_in_dim(term, lax.rem(z_at + step, 4), 1, False)
+
+    ring_sum = z_part(0).astype(f32)
+    for step in range(1, 4):
+        ring_sum = ring_sum + ring_step(z_part(step), "z", step).astype(f32)
+    ring_sum = ring_sum.astype(bf16).reshape(4, 2, 4, share_rows, 8, 128)
+    ring_sum = ring_sum.transpose(0, 2, 1, 3, 4, 5).reshape(16, 2 * share_rows, 8, 128)
+    ring_sum = exchange(ring_sum, ("x", "y"))
+
+    owned = jnp.sum(exchange(by_group(source_groups, slotted), BATCH), axis=0).astype(bf16)
+    heads = share(owned, BATCH, group_count).reshape(group_count * latent_count, 128)
+    grad_outproj, owned_parts = owners(heads, owned, all_latents, all_d_out)
+    over_seq = exchange(owned_parts, SEQ)
+
+    chip_sum = jnp.sum(ring_sum.astype(f32), axis=0).reshape(2, share_rows, model_width)
     kept_sum = lax.dynamic_index_in_dim(chip_sum, core, 0, False)
     got_sum = other_core(lax.dynamic_index_in_dim(chip_sum, 1 - core, 0, False))
     grad_kv = jnp.where(
@@ -354,54 +558,7 @@
         jnp.concatenate([kept_sum, got_sum], axis=1),
         jnp.concatenate([got_sum, kept_sum], axis=1),
     )
-
-    slotted = exchange(slotted, SEQ)
-    chosen = (
-        jnp.arange(group_count, dtype=f32)[:, None, None] == source_groups[None]
-    ).astype(bf16)
-    by_group = jnp.einsum("gsk,sklc->glc", chosen, slotted, preferred_element_type=f32)
-    owned = jnp.sum(exchange(by_group, BATCH), axis=0).astype(bf16)
-    over_batch = share(owned, BATCH, group_count)
-    over_batch = jnp.concatenate(
-        [lax.dynamic_index_in_dim(over_batch, group_at(j), 0, False) for j in range(8)], axis=0
-    )
-    normed_latents = normalize(jnp.concatenate(latents_all, axis=0))
-    query_cols = lax.dot_general(
-        normed_latents, over_batch[:, head_dim:], FIRST, preferred_element_type=f32
-    )
-    query_high = query_cols.astype(bf16)
-    query_low = (query_cols - query_high.astype(f32)).astype(bf16)
-    query_cols = jnp.concatenate([query_high, query_low], axis=1)
-    grad_outproj = lax.dot_general(
-        over_batch[:, :head_dim],
-        jnp.concatenate(d_out_all, axis=0),
-        FIRST,
-        preferred_element_type=f32,
-    )
-    over_seq = exchange(
-        jnp.stack(
-            [
-                jnp.broadcast_to(owned[None], (seq_count,) + owned.shape),
-                query_cols.reshape(seq_count, head_dim, 128),
-            ],
-            axis=1,
-        ),
-        SEQ,
-    )
-
-    def joined(part):
-        return part.transpose(1, 0, 2).reshape(part.shape[1], model_width)
-
-    mixed_b = joined(over_seq[:, 0, :, :head_dim])
-    d_query = joined(over_seq[:, 0, :, head_dim:])
-    grad_query = joined(
-        over_seq[:, 1, :, :head_dim].astype(f32) + over_seq[:, 1, :, head_dim:].astype(f32)
-    )
-    latent = latents[0].astype(f32)
-    cotangent = d_out[0]
-    out = (latent + jnp.dot(mixed_b, w_out, preferred_element_type=f32)).astype(bf16)
-    d_normed = lax.dot_general(d_query, w_query, LAST, preferred_element_type=f32)
-    d_latents = (cotangent.astype(f32) + rms_back(latent, d_normed)).astype(bf16)
+    out, d_latents, grad_query = finish(over_seq, latents[0], d_out[0], w_query, w_out)
     return (out[None], d_latents[None], grad_query, grad_outproj, grad_kv)
 
 

time: 193 us -> 173 us (0.90); the launches traced: 192 us -> 170 us
  local copies, waits for them, and re-layouts: 32.1 us -> 9.1 us
  Pallas kernels: 25.7 us -> 48 us
  matrix products: 20.8 us -> 4.18 us
  blocking collectives: 0 us -> 14.5 us
  waiting for transfers between devices: 52.4 us -> 38.6 us
  starting transfers between devices: 52.7 us -> 49.3 us
  other arithmetic: 7.36 us -> 5.32 us
    pallas_call x1 -> x6, Pallas kernels: 4.85 us -> 27.1 us  [the longest x1 8.94 us: project_pairs(): pl.pallas_call(pairs_kernel, grid=(width // tile,), out_shape=(jax.ShapeD...]
    all_to_all x7 -> x6, waiting for transfers between devices: 52.4 us -> 31.2 us  [exchange(): return lax.all_to_all(values, axes, 0, 0, tiled=True)]
    dot_general x6 -> x0, matrix products: 16.3 us -> none  [the longest x1 6.51 us: local(): pairs = jnp.dot(normed, w_kv, preferred_element_type=f32).astype(bf16)]
    all_to_all x0 -> x1, blocking collectives: none -> 14.5 us  [exchange(): return lax.all_to_all(values, axes, 0, 0, tiled=True)]
    unnamed x90 -> x47, local copies, waits for them, and re-layouts: 16.1 us -> 5.01 us
    ppermute x6 -> x9, waiting for transfers between devices: 0.02 us -> 7.47 us  [ring_step(): return lax.ppermute(values, axis, [(i, (i + step) % 4) for i in range(4)])]
    all_to_all x7 -> x6, starting transfers between devices: 35.7 us -> 29.8 us  [exchange(): return lax.all_to_all(values, axes, 0, 0, tiled=True)]
    reshape x5 -> x1, local copies, waits for them, and re-layouts: 3.55 us -> 0.02 us  [local(): jnp.sum(ring_sum.astype(f32), axis=0).reshape(2, share_rows, model_width)]
  transfers between devices with their start and end apart: 24 -> 26, of which waited for: 7 -> 7; matrix products, arithmetic and copies ran while one was open for 27% -> 7% of each run, Pallas kernels for 2% -> 16%
where the time goes in v3:
time: 173 us; the launch traced here: 170 us
  starting transfers between devices  49.3 us (28%)
  Pallas kernels  48 us (28%)
  waiting for transfers between devices  38.6 us (22%)
  blocking collectives  14.5 us (8%)
  local copies, waits for them, and re-layouts  9.1 us (5%)
  other arithmetic  5.32 us (3%)
  matrix products  4.18 us (2%)
    all_to_all x6, waiting for transfers between devices, exchange(): return lax.all_to_all(values, axes, 0, 0, tiled=True)  31.2 us
    all_to_all x6, starting transfers between devices, exchange(): return lax.all_to_all(values, axes, 0, 0, tiled=True)  29.8 us
    all_to_all x1, blocking collectives, exchange(): return lax.all_to_all(values, axes, 0, 0, tiled=True)  14.5 us
    pallas_call x1, Pallas kernels, gradients(): pl.pallas_call(grads_kernel, grid=(4,), out_shape=(jax.ShapeDtypeStruct((...  11.2 us
    ppermute x9, starting transfers between devices, ring_step(): return lax.ppermute(values, axis, [(i, (i + step) % 4) for i in range(4)])  10.4 us
    ppermute x11, starting transfers between devices, other_core(): return lax.ppermute(values, 'core', [(0, 1), (1, 0)])  9.17 us
    pallas_call x1, Pallas kernels, project_pairs(): pl.pallas_call(pairs_kernel, grid=(width // tile,), out_shape=(jax.ShapeD...  8.94 us
    pallas_call x2, Pallas kernels, project(): pl.pallas_call(functools.partial(project_kernel, norm, transposed), out_s...  7.85 us
  transfers between devices with their start and end apart: 26, of which 7 were waited for; matrix products, arithmetic and copies ran while one was open for 7% of the time, Pallas kernels for 16%

profile of v3, /device:TPU:1, one launch (start us, length us, event | category | flops | bytes accessed | tf_op | source)
XLA Modules:
  0.0 170.0 jit_solution(11529622868645929178)
XLA Ops:
  11.1 2.8 %collective-permute-start.4 = (bf16[64,1024]{1,0:T(8,128)(2,1)S(1)}, bf16[64,1024]{1,0:T(8,128)(2,1)S(1)}, u32[]{:S(2)}, u32[]{:S(2)}) collective-permute-start(bf16[64,1024]{1,0:T(8,128)(2,1)S(1)} %collective-permute-done.refs_1_), channel_id=1, source_target_pairs={{0,16},{16,0},{1,17},{17,1},{2,18},{18,2},{3,19},{19,3},{4,20},{20... | collective-permute-start | bytes 393224 | tf_op jit(solution)/shard_map/ppermute | solution.py:45
  14.0 8.9 %shard_map.119 = (bf16[512,1152]{1,0:T(8,128)(2,1)}, bf16[512,2048]{1,0:T(8,128)(2,1)}) custom-call(bf16[512,1152]{1,0:T(8,128)(2,1)} %bitcast.57, bf16[1152,2048]{1,0:T(8,128)(2,1)} %w_ref.1), custom_call_target="tpu_custom_call" | custom-call | flops 2415919104 | bytes 9437184 | tf_op jit(solution)/shard_map/pallas_call | solution.py:127
  25.8 4.0 %shard_map.120.q_ref = bf16[256,1024]{1,0:T(8,128)(2,1)} custom-call(s32[4]{0:T(128)} %fusion.9.places, bf16[64,1024]{1,0:T(8,128)(2,1)} %bitcast.46, bf16[64,1024]{1,0:T(8,128)(2,1)} %copy-done.5, bf16[64,1024]{1,0:T(8,128)(2,1)} %copy-done.6, bf16[64,1024]{1,0:T(8,128)(2,1)} %copy-done.7, bf16[64,1024]{1,0:T(8,128)(2,1)} %copy-done.8, ...), custom_call_target="tpu_custom_call" | custom-call | flops 536870912 | bytes 4194304 | tf_op jit(solution)/shard_map/pallas_call | solution.py:102
  31.2 3.9 %shard_map.121.d_ref = bf16[256,1024]{1,0:T(8,128)(2,1)} custom-call(s32[4]{0:T(128)} %fusion.9.places, bf16[64,1024]{1,0:T(8,128)(2,1)} %bitcast.52, bf16[64,1024]{1,0:T(8,128)(2,1)} %copy-done.9, bf16[64,1024]{1,0:T(8,128)(2,1)} %copy-done.10, bf16[64,1024]{1,0:T(8,128)(2,1)} %copy-done.11, bf16[64,1024]{1,0:T(8,128)(2,1)} %copy-done.14, ...), custom_call_target="tpu_custom_call" | custom-call | flops 536870912 | bytes 4194304 | tf_op jit(solution)/shard_map/pallas_call | solution.py:102
  35.1 4.9 %shard_map.122 = f32[128,1,256]{2,1,0:T(1,128)} custom-call(s32[4]{0:T(128)} %counts.3, s32[4]{0:T(128)} %groups.3, bf16[256,1024]{1,0:T(8,128)(2,1)} %shard_map.120.q_ref, bf16[256,1024]{1,0:T(8,128)(2,1)} %shard_map.121.d_ref, bf16[512,2048]{1,0:T(8,128)(2,1)} %get-tuple-element.24.pairs_ref), custom_call_target="tpu_custom_call" | custom-call | flops 4294967296 | bytes 4194304 | tf_op jit(solution)/shard_map/pallas_call | solution.py:241
  40.1 10.1 %all-to-all-start = ((f32[128,1,256]{2,1,0:T(1,128)}), f32[128,1,256]{2,1,0:T(1,128)S(1)}, u32[]{:S(2)}, u32[]{:S(2)}) async-start(f32[128,1,256]{2,1,0:T(1,128)} %shard_map.122), calls=%async_computation | async-start | bytes 262144 | tf_op jit(solution)/shard_map/all_to_all | solution.py:37
  50.9 3.3 %shard_map.124 = (bf16[512,1024]{1,0:T(8,128)(2,1)}, bf16[512,1024]{1,0:T(8,128)(2,1)}) custom-call(s32[8]{0:T(128)} %stack.35.owners, bf16[64,1024]{1,0:T(8,128)(2,1)} %bitcast.47, bf16[64,1024]{1,0:T(8,128)(2,1)} %copy-done.5, bf16[64,1024]{1,0:T(8,128)(2,1)} %copy-done.6, bf16[64,1024]{1,0:T(8,128)(2,1)} %copy-done.7, bf16[64,1024]{1,0:T(8,128)(2,1)} %copy-done.8, ...), custom_call_target="tpu_custom_call" | custom-call | flops 4194304 | bytes 4194304 | tf_op jit(solution)/shard_map/pallas_call | solution.py:401
  54.2 6.2 %all-to-all-done.in_ref = f32[128,1,256]{2,1,0:T(1,128)S(1)} async-done(((f32[128,1,256]{2,1,0:T(1,128)}), f32[128,1,256]{2,1,0:T(1,128)S(1)}, u32[]{:S(2)}, u32[]{:S(2)}) %all-to-all-start) | async-done | bytes 131104 | tf_op jit(solution)/shard_map/all_to_all | solution.py:37
  64.4 14.5 %all_to_all.35.reply_ref = f32[128,1,256]{2,1,0:T(1,128)} all-to-all(f32[128,1,256]{2,1,0:T(1,128)S(1)} %copy-done.20), channel_id=1, replica_groups=mesh['x'=4,'core'=2,'z'=4,'y'=4] {'x','core','z','y'}, dimensions={0} | all-to-all | bytes 262144 | tf_op jit(solution)/shard_map/all_to_all | solution.py:37
  78.9 11.2 %shard_map.125 = (bf16[512,1024]{1,0:T(8,128)(2,1)}, bf16[512,1024]{1,0:T(8,128)(2,1)}, bf16[16,3,64,128]{3,2,1,0:T(8,128)(2,1)}) custom-call(s32[4]{0:T(128)} %counts.3, s32[4]{0:T(128)} %groups.3, s32[1]{0:T(128)} %bitcast.3.core, bf16[256,1024]{1,0:T(8,128)(2,1)} %shard_map.120.q_ref, bf16[256,1024]{1,0:T(8,128)(2,1)} %shard_map.121.d_ref, ...), custom_call_target="tpu_custom_call" | custom-call | flops 8589934592 | bytes 8388608 | tf_op jit(solution)/shard_map/pallas_call | solution.py:365
  90.8 3.6 %all-to-all-start.2 = ((bf16[16,3,64,128]{3,2,1,0:T(8,128)(2,1)}), bf16[16,3,64,128]{3,2,1,0:T(8,128)(2,1)S(1)}, u32[]{:S(2)}, u32[]{:S(2)}) async-start(bf16[16,3,64,128]{3,2,1,0:T(8,128)(2,1)} %get-tuple-element.30), calls=%async_computation.2 | async-start | bytes 1572864 | tf_op jit(solution)/shard_map/all_to_all | solution.py:37
  94.5 4.2 %fusion.3 = bf16[144,8,8,128]{3,1,2,0:T(8,128)(2,1)S(1)} fusion(bf16[1024,1152]{1,0:T(8,128)(2,1)S(1)} %pad_maximum_fusion, bf16[512,1024]{1,0:T(8,128)(2,1)} %collective-permute-done.15, bf16[512,1024]{1,0:T(8,128)(2,1)} %get-tuple-element.39), kind=kOutput, calls=%fused_computation.5 | convolution fusion | flops 2421293056 | bytes 6815744 | tf_op jit(solution)/shard_map/dot_general | solution.py:533
  100.5 2.5 %collective-permute-start.18 = (bf16[8,36,8,128]{3,2,1,0:T(8,128)(2,1)}, bf16[8,36,8,128]{3,2,1,0:T(8,128)(2,1)}, u32[]{:S(2)}, u32[]{:S(2)}) collective-permute-start(bf16[8,36,8,128]{3,2,1,0:T(8,128)(2,1)} %get-tuple-element.42), channel_id=1, source_target_pairs={{0,12},{4,0},{8,4},{12,8},{1,13},{5,1},{9,5},{13,9},{2,14},{6,2},{... | collective-permute-start | bytes 1769480 | tf_op jit(solution)/shard_map/ppermute | solution.py:49
  105.6 3.7 %all-to-all-done.2.in_ref = bf16[16,3,64,128]{3,2,1,0:T(8,128)(2,1)S(1)} async-done(((bf16[16,3,64,128]{3,2,1,0:T(8,128)(2,1)}), bf16[16,3,64,128]{3,2,1,0:T(8,128)(2,1)S(1)}, u32[]{:S(2)}, u32[]{:S(2)}) %all-to-all-start.2) | async-done | bytes 786464 | tf_op jit(solution)/shard_map/all_to_all | solution.py:37
  112.5 4.6 %all-to-all-start.3 = ((f32[8,64,128]{2,1,0:T(8,128)}), f32[8,64,128]{2,1,0:T(8,128)S(1)}, u32[]{:S(2)}, u32[]{:S(2)}) async-start(f32[8,64,128]{2,1,0:T(8,128)} %shard_map.126), calls=%async_computation.3 | async-start | bytes 524288 | tf_op jit(solution)/shard_map/all_to_all | solution.py:37
  117.1 6.5 %all-to-all-done.3 = f32[8,64,128]{2,1,0:T(8,128)S(1)} async-done(((f32[8,64,128]{2,1,0:T(8,128)}), f32[8,64,128]{2,1,0:T(8,128)S(1)}, u32[]{:S(2)}, u32[]{:S(2)}) %all-to-all-start.3) | async-done | bytes 262176 | tf_op jit(solution)/shard_map/all_to_all | solution.py:37
  124.3 4.3 %all-to-all-start.4 = ((bf16[8,64,128]{2,1,0:T(8,128)(2,1)}), bf16[8,64,128]{2,1,0:T(8,128)(2,1)S(1)}, u32[]{:S(2)}, u32[]{:S(2)}) async-start(bf16[8,64,128]{2,1,0:T(8,128)(2,1)} %broadcast_in_dim.19), calls=%async_computation.4 | async-start | bytes 262144 | tf_op jit(solution)/shard_map/all_to_all | solution.py:37
  128.6 5.2 %collective-permute-done.16 = bf16[8,36,8,128]{3,2,1,0:T(8,128)(2,1)} collective-permute-done((bf16[8,36,8,128]{3,2,1,0:T(8,128)(2,1)}, bf16[8,36,8,128]{3,2,1,0:T(8,128)(2,1)}, u32[]{:S(2)}, u32[]{:S(2)}) %collective-permute-start.16) | collective-permute-done | bytes 589856 | tf_op jit(solution)/shard_map/ppermute | solution.py:49
  136.4 3.7 %all-to-all-start.6 = ((bf16[16,18,8,128]{3,2,1,0:T(8,128)(2,1)}), bf16[16,18,8,128]{3,2,1,0:T(8,128)(2,1)S(1)}, u32[]{:S(2)}, u32[]{:S(2)}) async-start(bf16[16,18,8,128]{3,2,1,0:T(8,128)(2,1)} %bitcast.21), calls=%async_computation.6 | async-start | bytes 1179648 | tf_op jit(solution)/shard_map/all_to_all | solution.py:37
  140.1 3.1 %shard_map.127 = (f32[64,1024]{1,0:T(8,128)}, bf16[16,128,128]{2,1,0:T(8,128)(2,1)}) custom-call(bf16[512,128]{1,0:T(8,128)(2,1)} %bitcast.56, bf16[64,128]{1,0:T(8,128)(2,1)} %copy-done.21, bf16[512,1024]{1,0:T(8,128)(2,1)} %get-tuple-element.31.latents_ref, bf16[512,1024]{1,0:T(8,128)(2,1)} %get-tuple-element.32.d_out_ref), custom_call_target="tpu_custom_call" | custom-call | flops 536870912 | bytes 4194304 | tf_op jit(solution)/shard_map/pallas_call | solution.py:449
  143.3 7.7 %all-to-all-done.6 = bf16[16,18,8,128]{3,2,1,0:T(8,128)(2,1)S(1)} async-done(((bf16[16,18,8,128]{3,2,1,0:T(8,128)(2,1)}), bf16[16,18,8,128]{3,2,1,0:T(8,128)(2,1)S(1)}, u32[]{:S(2)}, u32[]{:S(2)}) %all-to-all-start.6) | async-done | bytes 589856 | tf_op jit(solution)/shard_map/all_to_all | solution.py:37
  151.0 3.6 %all-to-all-start.5 = ((bf16[16,128,128]{2,1,0:T(8,128)(2,1)}), bf16[16,128,128]{2,1,0:T(8,128)(2,1)S(1)}, u32[]{:S(2)}, u32[]{:S(2)}) async-start(bf16[16,128,128]{2,1,0:T(8,128)(2,1)} %get-tuple-element.33), calls=%async_computation.5 | async-start | bytes 1048576 | tf_op jit(solution)/shard_map/all_to_all | solution.py:37
  157.1 6.9 %all-to-all-done.5.in_ref = bf16[16,128,128]{2,1,0:T(8,128)(2,1)S(1)} async-done(((bf16[16,128,128]{2,1,0:T(8,128)(2,1)}), bf16[16,128,128]{2,1,0:T(8,128)(2,1)S(1)}, u32[]{:S(2)}, u32[]{:S(2)}) %all-to-all-start.5) | async-done | bytes 524320 | tf_op jit(solution)/shard_map/all_to_all | solution.py:37
  164.8 4.5 %shard_map.128 = (bf16[64,1024]{1,0:T(8,128)(2,1)}, bf16[64,1024]{1,0:T(8,128)(2,1)}, f32[64,1024]{1,0:T(8,128)}) custom-call(bf16[16,128,128]{2,1,0:T(8,128)(2,1)} %copy-done.1, bf16[64,1024]{1,0:T(8,128)(2,1)} %bitcast.48, bf16[64,1024]{1,0:T(8,128)(2,1)} %bitcast.54, bf16[1024,1024]{1,0:T(8,128)(2,1)} %w_query_ref.1, bf16[1024,1024]{1,0:T(8,128)(2,1)} %w_out_ref.1), custom_call_target="tpu_custom_call" | custom-call | tf_op jit(solution)/shard_map/pallas_call | solution.py:489
  (101 shorter events, 35.1 us)
Async XLA Ops:
  0.6 7.5 %collective-permute-start = (bf16[64,1024]{1,0:T(8,128)(2,1)}, bf16[64,1024]{1,0:T(8,128)(2,1)S(1)}, u32[]{:S(2)}, u32[]{:S(2)}) collective-permute-start(bf16[64,1024]{1,0:T(8,128)(2,1)} %bitcast.42), channel_id=1, source_target_pairs={{0,32},{32,64},{64,96},{96,0},{1,33},{33,65},{65,97},{97,1},{2,34}... | collective-permute-start | bytes 393224 | tf_op jit(solution)/shard_map/ppermute | solution.py:49
  2.7 8.4 %collective-permute-start.1 = (bf16[64,1024]{1,0:T(8,128)(2,1)}, bf16[64,1024]{1,0:T(8,128)(2,1)S(1)}, u32[]{:S(2)}, u32[]{:S(2)}) collective-permute-start(bf16[64,1024]{1,0:T(8,128)(2,1)} %bitcast.43), channel_id=1, source_target_pairs={{0,64},{32,96},{64,0},{96,32},{1,65},{33,97},{65,1},{97,33},{2,66}... | collective-permute-start | bytes 393224 | tf_op jit(solution)/shard_map/ppermute | solution.py:49
  5.2 5.9 %collective-permute-start.2 = (bf16[64,1024]{1,0:T(8,128)(2,1)}, bf16[64,1024]{1,0:T(8,128)(2,1)S(1)}, u32[]{:S(2)}, u32[]{:S(2)}) collective-permute-start(bf16[64,1024]{1,0:T(8,128)(2,1)} %bitcast.44), channel_id=1, source_target_pairs={{0,96},{32,0},{64,32},{96,64},{1,97},{33,1},{65,33},{97,65},{2,98}... | collective-permute-start | bytes 393224 | tf_op jit(solution)/shard_map/ppermute | solution.py:49
  6.3 7.6 %collective-permute-start.3 = (bf16[64,1024]{1,0:T(8,128)(2,1)}, bf16[64,1024]{1,0:T(8,128)(2,1)S(1)}, u32[]{:S(2)}, u32[]{:S(2)}) collective-permute-start(bf16[64,1024]{1,0:T(8,128)(2,1)} %bitcast.45), channel_id=1, source_target_pairs={{0,16},{16,0},{1,17},{17,1},{2,18},{18,2},{3,19},{19,3},{4,20},{20... | collective-permute-start | bytes 393224 | tf_op jit(solution)/shard_map/ppermute | solution.py:45
  7.9 15.1 %collective-permute-start.7 = (bf16[64,1024]{1,0:T(8,128)(2,1)}, bf16[64,1024]{1,0:T(8,128)(2,1)S(1)}, u32[]{:S(2)}, u32[]{:S(2)}) collective-permute-start(bf16[64,1024]{1,0:T(8,128)(2,1)} %bitcast.49), channel_id=1, source_target_pairs={{0,32},{32,64},{64,96},{96,0},{1,33},{33,65},{65,97},{97,1},{2,34}... | collective-permute-start | bytes 393224 | tf_op jit(solution)/shard_map/ppermute | solution.py:49
  8.2 15.3 %collective-permute-start.8 = (bf16[64,1024]{1,0:T(8,128)(2,1)}, bf16[64,1024]{1,0:T(8,128)(2,1)S(1)}, u32[]{:S(2)}, u32[]{:S(2)}) collective-permute-start(bf16[64,1024]{1,0:T(8,128)(2,1)} %bitcast.50), channel_id=1, source_target_pairs={{0,64},{32,96},{64,0},{96,32},{1,65},{33,97},{65,1},{97,33},{2,66}... | collective-permute-start | bytes 393224 | tf_op jit(solution)/shard_map/ppermute | solution.py:49
  11.1 12.6 %collective-permute-start.9 = (bf16[64,1024]{1,0:T(8,128)(2,1)}, bf16[64,1024]{1,0:T(8,128)(2,1)S(1)}, u32[]{:S(2)}, u32[]{:S(2)}) collective-permute-start(bf16[64,1024]{1,0:T(8,128)(2,1)} %bitcast.51), channel_id=1, source_target_pairs={{0,96},{32,0},{64,32},{96,64},{1,97},{33,1},{65,33},{97,65},{2,98}... | collective-permute-start | bytes 393224 | tf_op jit(solution)/shard_map/ppermute | solution.py:49
  11.1 13.0 %collective-permute-start.4 = (bf16[64,1024]{1,0:T(8,128)(2,1)S(1)}, bf16[64,1024]{1,0:T(8,128)(2,1)S(1)}, u32[]{:S(2)}, u32[]{:S(2)}) collective-permute-start(bf16[64,1024]{1,0:T(8,128)(2,1)S(1)} %collective-permute-done.refs_1_), channel_id=1, source_target_pairs={{0,16},{16,0},{1,17},{17,1},{2,18},{18,2},{3,19},{19,3},{4,20},{20... | collective-permute-start | bytes 393224 | tf_op jit(solution)/shard_map/ppermute | solution.py:45
  13.9 10.3 %collective-permute-start.5 = (bf16[64,1024]{1,0:T(8,128)(2,1)S(1)}, bf16[64,1024]{1,0:T(8,128)(2,1)S(1)}, u32[]{:S(2)}, u32[]{:S(2)}) collective-permute-start(bf16[64,1024]{1,0:T(8,128)(2,1)S(1)} %collective-permute-done.1.refs_2_), channel_id=1, source_target_pairs={{0,16},{16,0},{1,17},{17,1},{2,18},{18,2},{3,19},{19,3},{4,20},{20... | collective-permute-start | bytes 393224 | tf_op jit(solution)/shard_map/ppermute | solution.py:45
  23.0 6.8 %collective-permute-start.10 = (bf16[64,1024]{1,0:T(8,128)(2,1)S(1)}, bf16[64,1024]{1,0:T(8,128)(2,1)S(1)}, u32[]{:S(2)}, u32[]{:S(2)}) collective-permute-start(bf16[64,1024]{1,0:T(8,128)(2,1)S(1)} %bitcast.55), channel_id=1, source_target_pairs={{0,16},{16,0},{1,17},{17,1},{2,18},{18,2},{3,19},{19,3},{4,20},{20... | collective-permute-start | bytes 393224 | tf_op jit(solution)/shard_map/ppermute | solution.py:45
  23.7 6.1 %collective-permute-start.11 = (bf16[64,1024]{1,0:T(8,128)(2,1)S(1)}, bf16[64,1024]{1,0:T(8,128)(2,1)S(1)}, u32[]{:S(2)}, u32[]{:S(2)}) collective-permute-start(bf16[64,1024]{1,0:T(8,128)(2,1)S(1)} %collective-permute-done.7.refs_1_.refs_9_), channel_id=1, source_target_pairs={{0,16},{16,0},{1,17},{17,1},{2,18},{18,2},{3,19},{19,3},{4,20},{20... | collective-permute-start | bytes 393224 | tf_op jit(solution)/shard_map/ppermute | solution.py:45
  24.1 5.7 %collective-permute-start.12 = (bf16[64,1024]{1,0:T(8,128)(2,1)S(1)}, bf16[64,1024]{1,0:T(8,128)(2,1)S(1)}, u32[]{:S(2)}, u32[]{:S(2)}) collective-permute-start(bf16[64,1024]{1,0:T(8,128)(2,1)S(1)} %collective-permute-done.8.refs_2_.refs_10_), channel_id=1, source_target_pairs={{0,16},{16,0},{1,17},{17,1},{2,18},{18,2},{3,19},{19,3},{4,20},{20... | collective-permute-start | bytes 393224 | tf_op jit(solution)/shard_map/ppermute | solution.py:45
  24.2 5.6 %collective-permute-start.13 = (bf16[64,1024]{1,0:T(8,128)(2,1)S(1)}, bf16[64,1024]{1,0:T(8,128)(2,1)S(1)}, u32[]{:S(2)}, u32[]{:S(2)}) collective-permute-start(bf16[64,1024]{1,0:T(8,128)(2,1)S(1)} %collective-permute-done.9.refs_3_.refs_11_), channel_id=1, source_target_pairs={{0,16},{16,0},{1,17},{17,1},{2,18},{18,2},{3,19},{19,3},{4,20},{20... | collective-permute-start | bytes 393224 | tf_op jit(solution)/shard_map/ppermute | solution.py:45
  40.0 22.9 %collective-permute-start.14 = (bf16[512,1152]{1,0:T(8,128)(2,1)S(1)}, bf16[512,1152]{1,0:T(8,128)(2,1)}, u32[]{:S(2)}, u32[]{:S(2)}) collective-permute-start(bf16[512,1152]{1,0:T(8,128)(2,1)S(1)} %copy-done.3), channel_id=1, source_target_pairs={{0,16},{16,0},{1,17},{17,1},{2,18},{18,2},{3,19},{19,3},{4,20},{20... | collective-permute-start | bytes 3538952 | tf_op jit(solution)/shard_map/ppermute | solution.py:45
  40.1 20.3 %all-to-all-start = ((f32[128,1,256]{2,1,0:T(1,128)}), f32[128,1,256]{2,1,0:T(1,128)S(1)}, u32[]{:S(2)}, u32[]{:S(2)}) async-start(f32[128,1,256]{2,1,0:T(1,128)} %shard_map.122), calls=%async_computation | async-start | bytes 262144 | tf_op jit(solution)/shard_map/all_to_all | solution.py:37
  90.8 18.5 %all-to-all-start.2 = ((bf16[16,3,64,128]{3,2,1,0:T(8,128)(2,1)}), bf16[16,3,64,128]{3,2,1,0:T(8,128)(2,1)S(1)}, u32[]{:S(2)}, u32[]{:S(2)}) async-start(bf16[16,3,64,128]{3,2,1,0:T(8,128)(2,1)} %get-tuple-element.30), calls=%async_computation.2 | async-start | bytes 1572864 | tf_op jit(solution)/shard_map/all_to_all | solution.py:37
  100.5 28.1 %collective-permute-start.18 = (bf16[8,36,8,128]{3,2,1,0:T(8,128)(2,1)}, bf16[8,36,8,128]{3,2,1,0:T(8,128)(2,1)}, u32[]{:S(2)}, u32[]{:S(2)}) collective-permute-start(bf16[8,36,8,128]{3,2,1,0:T(8,128)(2,1)} %get-tuple-element.42), channel_id=1, source_target_pairs={{0,12},{4,0},{8,4},{12,8},{1,13},{5,1},{9,5},{13,9},{2,14},{6,2},{... | collective-permute-start | bytes 1769480 | tf_op jit(solution)/shard_map/ppermute | solution.py:49
  103.1 25.6 %collective-permute-start.17 = (bf16[8,36,8,128]{3,2,1,0:T(8,128)(2,1)}, bf16[8,36,8,128]{3,2,1,0:T(8,128)(2,1)}, u32[]{:S(2)}, u32[]{:S(2)}) collective-permute-start(bf16[8,36,8,128]{3,2,1,0:T(8,128)(2,1)} %get-tuple-element.43), channel_id=1, source_target_pairs={{0,8},{4,12},{8,0},{12,4},{1,9},{5,13},{9,1},{13,5},{2,10},{6,14},... | collective-permute-start | bytes 1769480 | tf_op jit(solution)/shard_map/ppermute | solution.py:49
  103.6 30.2 %collective-permute-start.16 = (bf16[8,36,8,128]{3,2,1,0:T(8,128)(2,1)}, bf16[8,36,8,128]{3,2,1,0:T(8,128)(2,1)}, u32[]{:S(2)}, u32[]{:S(2)}) collective-permute-start(bf16[8,36,8,128]{3,2,1,0:T(8,128)(2,1)} %get-tuple-element.41), channel_id=1, source_target_pairs={{0,4},{4,8},{8,12},{12,0},{1,5},{5,9},{9,13},{13,1},{2,6},{6,10},{... | collective-permute-start | bytes 1769480 | tf_op jit(solution)/shard_map/ppermute | solution.py:49
  112.5 11.1 %all-to-all-start.3 = ((f32[8,64,128]{2,1,0:T(8,128)}), f32[8,64,128]{2,1,0:T(8,128)S(1)}, u32[]{:S(2)}, u32[]{:S(2)}) async-start(f32[8,64,128]{2,1,0:T(8,128)} %shard_map.126), calls=%async_computation.3 | async-start | bytes 524288 | tf_op jit(solution)/shard_map/all_to_all | solution.py:37
  124.3 12.1 %all-to-all-start.4 = ((bf16[8,64,128]{2,1,0:T(8,128)(2,1)}), bf16[8,64,128]{2,1,0:T(8,128)(2,1)S(1)}, u32[]{:S(2)}, u32[]{:S(2)}) async-start(bf16[8,64,128]{2,1,0:T(8,128)(2,1)} %broadcast_in_dim.19), calls=%async_computation.4 | async-start | bytes 262144 | tf_op jit(solution)/shard_map/all_to_all | solution.py:37
  136.4 14.6 %all-to-all-start.6 = ((bf16[16,18,8,128]{3,2,1,0:T(8,128)(2,1)}), bf16[16,18,8,128]{3,2,1,0:T(8,128)(2,1)S(1)}, u32[]{:S(2)}, u32[]{:S(2)}) async-start(bf16[16,18,8,128]{3,2,1,0:T(8,128)(2,1)} %bitcast.21), calls=%async_computation.6 | async-start | bytes 1179648 | tf_op jit(solution)/shard_map/all_to_all | solution.py:37
  151.0 13.0 %all-to-all-start.5 = ((bf16[16,128,128]{2,1,0:T(8,128)(2,1)}), bf16[16,128,128]{2,1,0:T(8,128)(2,1)S(1)}, u32[]{:S(2)}, u32[]{:S(2)}) async-start(bf16[16,128,128]{2,1,0:T(8,128)(2,1)} %get-tuple-element.33), calls=%async_computation.5 | async-start | bytes 1048576 | tf_op jit(solution)/shard_map/all_to_all | solution.py:37
  154.7 14.6 %collective-permute-start.19 = (f32[9,1024]{1,0:T(8,128)S(1)}, f32[9,1024]{1,0:T(8,128)S(1)}, u32[]{:S(2)}, u32[]{:S(2)}) collective-permute-start(f32[9,1024]{1,0:T(8,128)S(1)} %get-tuple-element.45), channel_id=1, source_target_pairs={{0,16},{16,0},{1,17},{17,1},{2,18},{18,2},{3,19},{19,3},{4,20},{20... | collective-permute-start | bytes 110600 | tf_op jit(solution)/shard_map/ppermute | solution.py:45
  (25 other events, 123.7 us)

commit v4 on v3

v4 whole, which is shorter than its diff:
```python
import functools

import jax
import jax.numpy as jnp
from jax import lax
from jax.experimental import pallas as pl
from jax.experimental.pallas import tpu as pltpu
from jax.sharding import Mesh, PartitionSpec as P

H = 16
BATCH = ("x", "core")
SEQ = ("z", "y")
CHIPS = ("x", "z", "y")
ALL = BATCH + SEQ
SLOTS = 3
WIDE = 256

epsilon = 1e-06
f32 = jnp.float32
bf16 = jnp.bfloat16


def rms_rows(values):
    return values * lax.rsqrt(jnp.mean(values * values, axis=-1, keepdims=True) + epsilon)


def rms_back(values, grads):
    factor = lax.rsqrt(jnp.mean(values * values, axis=-1, keepdims=True) + epsilon)
    normed = values * factor
    return factor * (grads - normed * jnp.mean(grads * normed, axis=-1, keepdims=True))


def normalize(values):
    return rms_rows(values.astype(f32)).astype(bf16)


def exchange(values, axes):
    return lax.all_to_all(values, axes, 0, 0, tiled=True)


def share(values, axes, count):
    return exchange(jnp.broadcast_to(values[None], (count,) + values.shape), axes)


def other_core(values):
    return lax.ppermute(values, "core", [(0, 1), (1, 0)])


def ring_step(values, axis, step):
    return lax.ppermute(values, axis, [(i, (i + step) % 4) for i in range(4)])


def chip_step(values, step):
    return ring_step(values, "x", step)


def along_chips(values):
    return [values, chip_step(values, 1), chip_step(values, 2), chip_step(values, 3)]


def place_of(group):
    chip = lax.rem(lax.axis_index("x") - group // 2 + 4, 4)
    return jnp.where(group % 2 == lax.axis_index("core"), 0, 4) + chip


def group_at(place):
    chip = lax.rem(lax.axis_index("x") - place % 4 + 4, 4)
    core = lax.axis_index("core")
    return 2 * chip + (core if place < 4 else 1 - core)


SMEM = pl.BlockSpec(memory_space=pltpu.SMEM)
VMEM = pl.BlockSpec(memory_space=pltpu.VMEM)
HBM = pl.BlockSpec(memory_space=pltpu.HBM)
LAST = (((1,), (1,)), ((), ()))
FIRST = (((0,), (0,)), ((), ()))


def room(mebibytes):
    return pltpu.CompilerParams(vmem_limit_bytes=mebibytes * 1024 * 1024)


def pairs_kernel(frames_ref, w_ref, normed_ref, out_ref):
    @pl.when(pl.program_id(0) == 0)
    def _():
        normed_ref[...] = normalize(frames_ref[...])

    out_ref[...] = jnp.dot(normed_ref[...], w_ref[...], preferred_element_type=f32).astype(bf16)


def project_pairs(frames, w_kv):
    rows, feature = frames.shape
    width, tile = w_kv.shape[1], 1024
    return pl.pallas_call(
        pairs_kernel,
        grid=(width // tile,),
        out_shape=(
            jax.ShapeDtypeStruct((rows, feature), bf16),
            jax.ShapeDtypeStruct((rows, width), bf16),
        ),
        in_specs=[
            pl.BlockSpec((rows, feature), lambda i: (0, 0)),
            pl.BlockSpec((feature, tile), lambda i: (0, i)),
        ],
        out_specs=(
            pl.BlockSpec((rows, feature), lambda i: (0, 0)),
            pl.BlockSpec((rows, tile), lambda i: (0, i)),
        ),
        cost_estimate=pl.CostEstimate(
            flops=2 * rows * feature * width, bytes_accessed=9 * 1024 * 1024, transcendentals=0
        ),
    )(frames, w_kv)


def low_lanes(shape):
    return lax.broadcasted_iota(jnp.int32, shape, len(shape) - 1) < 64


def spread(heads, masks):
    return jnp.concatenate([heads * mask for mask in masks], axis=0)


def head_masks():
    head = lax.broadcasted_iota(jnp.int32, (1, WIDE), 1) // 64
    return [jnp.where(head == at, 1.0, 0.0).astype(bf16) for at in range(WIDE // 64)]


def own_heads(product, rows):
    head = lax.broadcasted_iota(jnp.int32, (rows, WIDE), 1) // 64
    result = product[:rows]
    for at in range(1, WIDE // 64):
        result = jnp.where(head == at, product[at * rows : at * rows + rows], result)
    return result


def slots_of(groups):
    slots, used = [0], 1
    for i in range(1, 4):
        slot = used
        fresh = True
        for j in reversed(range(i)):
            slot = jnp.where(groups[i] == groups[j], slots[j], slot)
            fresh = fresh & (groups[i] != groups[j])
        slots.append(slot)
        used = used + jnp.where(fresh, 1, 0)
    return slots


def attend_kernel(counts, groups, places, *refs):
    pieces, (wq_in, wo_in, pairs_in, q_out, d_out, out_ref), scratch = refs[:8], refs[8:14], refs[14:]
    picked, wq, wo, pairs_ref, q_ref, d_ref, top_ref, total_ref, moment_ref, sems = scratch
    copies = [
        pltpu.make_async_copy(wq_in, wq, sems.at[0]),
        pltpu.make_async_copy(wo_in, wo, sems.at[1]),
        pltpu.make_async_copy(pairs_in, pairs_ref, sems.at[2]),
        pltpu.make_async_copy(q_ref, q_out, sems.at[3]),
        pltpu.make_async_copy(d_ref, d_out, sems.at[4]),
    ]
    for copy in copies[:3]:
        copy.start()
    rows, width = pieces[0].shape[1:]
    blocks = q_ref.shape[0] // rows
    for i in range(blocks):
        for j in range(8):

            @pl.when(places[i] == j)
            def _():
                picked[0, i * rows : (i + 1) * rows, :] = normalize(pieces[j][0])
                picked[1, i * rows : (i + 1) * rows, :] = pieces[j][1]

    copies[0].wait()
    for at in range(0, width, 256):
        tile = slice(at, at + 256)
        q_ref[:, tile] = jnp.dot(picked[0], wq[:, tile], preferred_element_type=f32).astype(bf16)
    copies[3].start()
    copies[1].wait()
    for at in range(0, width, 256):
        tile = slice(at, at + 256)
        d_ref[:, tile] = lax.dot_general(
            picked[1], wo[tile, :], LAST, preferred_element_type=f32
        ).astype(bf16)
    copies[4].start()
    copies[2].wait()

    masks = head_masks()
    scale = (width // H) ** (-0.5)
    position = lax.broadcasted_iota(jnp.int32, (128, WIDE), 0)

    def one_block(block, carry):
        usable = position < counts[block]
        here = pl.ds(pl.multiple_of(block * rows, rows), rows)
        there = pl.ds(pl.multiple_of(block * 128, 128), 128)
        for at in range(0, width, WIDE):
            cols = slice(at, at + WIDE)
            value_cols = slice(width + at, width + at + WIDE)
            s = lax.dot_general(
                pairs_ref[there, cols],
                spread(q_ref[here, cols], masks),
                LAST,
                preferred_element_type=f32,
            )
            s = jnp.where(usable, s * scale, -1e30)
            top = jnp.max(s, axis=0, keepdims=True)
            raw = jnp.where(usable, jnp.exp(s - top), 0.0)
            dw = lax.dot_general(
                pairs_ref[there, value_cols],
                spread(d_ref[here, cols], masks),
                LAST,
                preferred_element_type=f32,
            )
            total = jnp.sum(raw, axis=0, keepdims=True)
            moment = jnp.sum(raw * dw, axis=0, keepdims=True)
            for part in range(0, WIDE, 128):
                p = (at + part) // 128
                top_ref[block, p : p + 1, :] = top[:, part : part + 128]
                total_ref[block, p : p + 1, :] = total[:, part : part + 128]
                moment_ref[block, p : p + 1, :] = moment[:, part : part + 128]
        return carry

    lax.fori_loop(0, blocks, one_block, 0)
    own = [groups[i] for i in range(blocks)]
    slots = slots_of(own)
    left = low_lanes((8, 128))
    lane = lax.broadcasted_iota(jnp.int32, (8, 128), 1)
    note = jnp.full((8, 128), -1.0, f32)
    for i in range(blocks):
        note = jnp.where(lane == 64 + slots[i], own[i].astype(f32), note)
    for g in range(8):
        tops = [jnp.where(own[i] == g, top_ref[i], -1e30) for i in range(blocks)]
        top = functools.reduce(jnp.maximum, tops)
        total = jnp.zeros((8, 128), f32)
        moment = jnp.zeros((8, 128), f32)
        for i in range(blocks):
            factor = jnp.where(own[i] == g, jnp.exp(tops[i] - top), 0.0)
            total = total + factor * total_ref[i]
            moment = moment + factor * moment_ref[i]
        parts = (
            (jnp.where(left, top, pltpu.roll(total, 64, 1)), jnp.where(left, moment, note)),
            (
                jnp.where(left, pltpu.roll(top, 64, 1), total),
                jnp.where(left, pltpu.roll(moment, 64, 1), note),
            ),
        )
        for odd in range(2):
            for p in range(8):
                at = 16 * g + 8 * odd + p
                out_ref[at, :, 0:128] = parts[odd][0][p : p + 1]
                out_ref[at, :, 128:256] = parts[odd][1][p : p + 1]
    copies[3].wait()
    copies[4].wait()


def attend(counts, groups, places, pieces, w_query, w_out, pairs):
    rows, width = pieces[0].shape[1:]
    small = jax.ShapeDtypeStruct((groups.shape[0] * rows, width), bf16)
    return pl.pallas_call(
        attend_kernel,
        out_shape=(small, small, jax.ShapeDtypeStruct((128, 1, 256), f32)),
        in_specs=[SMEM] * 3 + [VMEM] * 8 + [HBM] * 3,
        out_specs=(HBM, HBM, VMEM),
        scratch_shapes=[
            pltpu.VMEM((2,) + small.shape, bf16),
            pltpu.VMEM(w_query.shape, bf16),
            pltpu.VMEM(w_out.shape, bf16),
            pltpu.VMEM(pairs.shape, bf16),
            pltpu.VMEM(small.shape, bf16),
            pltpu.VMEM(small.shape, bf16),
        ]
        + [pltpu.VMEM((groups.shape[0], 8, 128), f32)] * 3
        + [pltpu.SemaphoreType.DMA((5,))],
        cost_estimate=pl.CostEstimate(
            flops=6 * 1024 * 1024 * 1024,
            bytes_accessed=10 * 1024 * 1024,
            transcendentals=512 * 1024,
        ),
    )(counts, groups, places, *pieces, w_query, w_out, pairs)


def block_specs(latent_count, width):
    return [
        pl.BlockSpec((latent_count, width), lambda i: (i, 0)),
        pl.BlockSpec((latent_count, width), lambda i: (i, 0)),
        pl.BlockSpec((128, 2 * width), lambda i: (i, 0)),
    ]


def totals_kernel(in_ref, out_ref):
    left = low_lanes((1, 128))
    first = in_ref[:, 0, 0:128]
    top = jnp.max(first, axis=0, keepdims=True)
    top = jnp.where(left, top, pltpu.roll(top, 64, 1))
    factor = jnp.exp(jnp.where(left, first, pltpu.roll(first, 64, 1)) - top)
    total = jnp.sum(factor * first, axis=0, keepdims=True)
    inverse = 1.0 / jnp.where(left, pltpu.roll(total, 64, 1), total)
    delta = jnp.sum(factor * in_ref[:, 0, 128:256], axis=0, keepdims=True) * inverse
    reply = jnp.concatenate(
        [jnp.where(left, top, inverse), jnp.where(left, delta, 0.0)], axis=1
    )
    for at in range(in_ref.shape[0]):
        out_ref[at] = reply


def totals(stats):
    return pl.pallas_call(
        totals_kernel,
        out_shape=jax.ShapeDtypeStruct(stats.shape, f32),
        in_specs=[VMEM],
        out_specs=VMEM,
        compiler_params=room(4),
    )(stats)


def grads_kernel(
    counts,
    groups,
    core,
    q_ref,
    d_ref,
    pairs_ref,
    reply_ref,
    kept_ref,
    sent_ref,
    slotted_ref,
    mixed_acc,
    query_acc,
    mixed_now,
    query_now,
):
    block = pl.program_id(0)
    masks = head_masks()
    rows, width = q_ref.shape
    scale = (width // H) ** (-0.5)
    usable = lax.broadcasted_iota(jnp.int32, (128, WIDE), 0) < counts[block]
    left = low_lanes((8, 128))
    wide = low_lanes((rows, 128))

    @pl.when(block == 0)
    def _():
        mixed_acc[...] = jnp.zeros_like(mixed_acc)
        query_acc[...] = jnp.zeros_like(query_acc)

    slots = slots_of([groups[i] for i in range(4)])
    slot = slots[0]
    for i in range(1, 4):
        slot = jnp.where(block == i, slots[i], slot)
    group = groups[block]
    def reply_rows(odd, cols):
        first = 16 * group + 8 * odd
        return jnp.concatenate([reply_ref[first + p, :, cols] for p in range(8)], axis=0)

    def row(pairs, at):
        first = at // 128
        return jnp.concatenate([pairs[p : p + 1] for p in range(first, first + WIDE // 128)], axis=1)

    even = reply_rows(0, slice(0, 128))
    odd = reply_rows(1, slice(0, 128))
    top = jnp.where(left, even, pltpu.roll(odd, 64, 1))
    inverse = jnp.where(left, pltpu.roll(even, 64, 1), odd)
    delta = jnp.where(
        left, reply_rows(0, slice(128, 256)), pltpu.roll(reply_rows(1, slice(128, 256)), 64, 1)
    )
    for at in range(0, width, WIDE):
        cols = slice(at, at + WIDE)
        value_cols = slice(width + at, width + at + WIDE)
        q = spread(q_ref[:, cols], masks)
        d = spread(d_ref[:, cols], masks)
        k = pairs_ref[:, cols]
        v = pairs_ref[:, value_cols]
        s = lax.dot_general(k, q, LAST, preferred_element_type=f32) * scale
        dw = lax.dot_general(v, d, LAST, preferred_element_type=f32)
        weights = jnp.where(usable, jnp.exp(s - row(top, at)) * row(inverse, at), 0.0)
        weights_b = weights.astype(bf16)
        d_scores = (weights * (dw - row(delta, at)) * scale).astype(bf16)
        d_values = jnp.dot(weights_b, d, preferred_element_type=f32)
        d_keys = jnp.dot(d_scores, q, preferred_element_type=f32)
        kept_ref[:, cols] = jnp.where(core[0] == 0, d_keys, d_values).astype(bf16)
        sent_ref[:, cols] = jnp.where(core[0] == 0, d_values, d_keys).astype(bf16)
        mixed = lax.dot_general(weights_b, v, FIRST, preferred_element_type=f32)
        mixed_now[:, cols] = own_heads(mixed, rows)
        query = lax.dot_general(d_scores, k, FIRST, preferred_element_type=f32)
        query_now[:, cols] = own_heads(query, rows)
    mixed_acc[slot] += mixed_now[...]
    query_acc[slot] += query_now[...]

    @pl.when(block == 3)
    def _():
        for at in range(SLOTS):
            for p in range(width // 128):
                cols = slice(128 * p, 128 * p + 128)
                mixed = mixed_acc[at, :, cols]
                query = query_acc[at, :, cols]
                slotted_ref[2 * p, at] = jnp.where(
                    wide, mixed, pltpu.roll(query, 64, 1)
                ).astype(bf16)
                slotted_ref[2 * p + 1, at] = jnp.where(
                    wide, pltpu.roll(mixed, 64, 1), query
                ).astype(bf16)


def gradients(counts, groups, core, queries, d_mixed, pairs, reply):
    width = queries.shape[1]
    rows = queries.shape[0] // 4
    return pl.pallas_call(
        grads_kernel,
        grid=(4,),
        out_shape=(
            jax.ShapeDtypeStruct((pairs.shape[0], width), bf16),
            jax.ShapeDtypeStruct((pairs.shape[0], width), bf16),
            jax.ShapeDtypeStruct((H, SLOTS, rows, 128), bf16),
        ),
        in_specs=[SMEM, SMEM, SMEM]
        + block_specs(rows, width)
        + [pl.BlockSpec((128, 1, 256), lambda i: (0, 0, 0))],
        out_specs=(
            pl.BlockSpec((128, width), lambda i: (i, 0)),
            pl.BlockSpec((128, width), lambda i: (i, 0)),
            pl.BlockSpec((H, SLOTS, rows, 128), lambda i: (0, 0, 0, 0)),
        ),
        scratch_shapes=[pltpu.VMEM((SLOTS, rows, width), f32)] * 2
        + [pltpu.VMEM((rows, width), f32)] * 2,
        cost_estimate=pl.CostEstimate(
            flops=8 * 1024 * 1024 * 1024, bytes_accessed=8 * 1024 * 1024, transcendentals=512 * 1024
        ),
    )(counts, groups, core, queries, d_mixed, pairs, reply)


def prepare_kernel(owners, *refs):
    pieces, (latents_ref, d_out_ref) = refs[:8], refs[8:]
    rows = pieces[0].shape[1]
    for j in range(8):
        at = pl.ds(pl.multiple_of(owners[j] * rows, rows), rows)
        latents_ref[at, :] = normalize(pieces[j][0])
        d_out_ref[at, :] = pieces[j][1]


def prepare(owners, pieces):
    rows, width = pieces[0].shape[1:]
    out = jax.ShapeDtypeStruct((8 * rows, width), bf16)
    return pl.pallas_call(
        prepare_kernel,
        out_shape=(out, out),
        in_specs=[SMEM] + [VMEM] * 8,
        out_specs=(VMEM, VMEM),
        cost_estimate=pl.CostEstimate(
            flops=4 * 1024 * 1024, bytes_accessed=4 * 1024 * 1024, transcendentals=512
        ),
    )(owners, *pieces)


def owners_kernel(heads_ref, owned_ref, latents_ref, d_out_ref, outproj_ref, out_ref):
    rows = outproj_ref.shape[0]
    heads = heads_ref[...]
    outproj_ref[...] = lax.dot_general(
        heads, d_out_ref[...], FIRST, preferred_element_type=f32
    )[:rows]
    query = lax.dot_general(latents_ref[...], heads, FIRST, preferred_element_type=f32)
    high = query.astype(bf16).astype(f32)
    query = jnp.where(low_lanes(query.shape), pltpu.roll(high, 64, 1), query - high).astype(bf16)
    for at in range(H):
        out_ref[at, :rows] = owned_ref[...]
        out_ref[at, rows:] = query[rows * at : rows * at + rows]


def owners(heads, owned, normed_latents, d_outs):
    rows = owned.shape[0]
    width = d_outs.shape[1]
    return pl.pallas_call(
        owners_kernel,
        out_shape=(
            jax.ShapeDtypeStruct((rows, width), f32),
            jax.ShapeDtypeStruct((H, 2 * rows, 128), bf16),
        ),
        in_specs=[VMEM] * 4,
        out_specs=(VMEM, VMEM),
        cost_estimate=pl.CostEstimate(
            flops=512 * 1024 * 1024, bytes_accessed=4 * 1024 * 1024, transcendentals=0
        ),
    )(heads, owned, normed_latents, d_outs)


def finish_kernel(in_ref, latent_ref, d_out_ref, w_query_ref, w_out_in, *refs):
    out_ref, d_latents_ref, grad_query_ref, mixed, d_query, w_out_ref, sem = refs
    copy = pltpu.make_async_copy(w_out_in, w_out_ref, sem)
    copy.start()
    rows = latent_ref.shape[0]
    left = low_lanes((rows, 128))

    def parts(head):
        both = in_ref[head, rows : 2 * rows].astype(f32)
        return in_ref[head, :rows].astype(f32), both + pltpu.roll(both, 64, 1)

    for p in range(H // 2):
        cols = slice(128 * p, 128 * p + 128)
        even, even_grad = parts(2 * p)
        odd, odd_grad = parts(2 * p + 1)
        mixed[:, cols] = jnp.where(left, even, pltpu.roll(odd, 64, 1)).astype(bf16)
        d_query[:, cols] = jnp.where(left, pltpu.roll(even, 64, 1), odd).astype(bf16)
        grad_query_ref[:, cols] = jnp.where(left, even_grad, odd_grad)
    latent = latent_ref[...].astype(f32)
    d_normed = lax.dot_general(d_query[...], w_query_ref[...], LAST, preferred_element_type=f32)
    d_latents_ref[...] = (d_out_ref[...].astype(f32) + rms_back(latent, d_normed)).astype(bf16)
    copy.wait()
    update = jnp.dot(mixed[...], w_out_ref[...], preferred_element_type=f32)
    out_ref[...] = (latent + update).astype(bf16)


def finish(over_seq, latent, d_out, w_query, w_out):
    rows, width = latent.shape
    small = jax.ShapeDtypeStruct((rows, width), bf16)
    return pl.pallas_call(
        finish_kernel,
        out_shape=(small, small, jax.ShapeDtypeStruct((rows, width), f32)),
        in_specs=[VMEM] * 4 + [HBM],
        out_specs=(VMEM,) * 3,
        compiler_params=room(12),
        scratch_shapes=[pltpu.VMEM((rows, width), bf16)] * 2
        + [pltpu.VMEM(w_out.shape, bf16), pltpu.SemaphoreType.DMA],
    )(over_seq, latent, d_out, w_query, w_out)


def local(latents, frames, counts, groups, w_query, w_kv, w_out, d_out):
    blocks, block_rows, feature = frames.shape
    latent_count, model_width = latents.shape[1:]
    head_dim = model_width // H
    group_count, seq_count = 8, 16
    rows = blocks * block_rows
    core = lax.axis_index("core")
    batch_at = lax.axis_index(BATCH)

    near = along_chips(jnp.concatenate([latents, d_out], axis=0))
    normed, pairs = project_pairs(frames.reshape(rows, feature), w_kv)
    near, normed, pairs = lax.optimization_barrier((near, normed, pairs))
    pieces = near + [other_core(piece) for piece in near]
    queries, d_mixed, stats = attend(
        counts, groups, place_of(groups), pieces, w_query, w_out, pairs
    )
    sources = jnp.stack([group_at(j) for j in range(8)])
    normed, sources, stats = lax.optimization_barrier((normed, sources, stats))
    all_latents, all_d_out = prepare(sources, pieces)
    normed = jnp.concatenate([normed, other_core(normed)], axis=0)
    stats = exchange(stats, ALL)
    source_groups = lax.dynamic_slice(
        stats, (batch_at * seq_count, 0, 192), (seq_count, 1, SLOTS)
    )
    chosen = (
        jnp.arange(group_count, dtype=f32)[:, None, None] == source_groups.reshape(1, seq_count, SLOTS)
    ).astype(bf16)
    reply = exchange(totals(stats), ALL)
    reply, all_latents, all_d_out, normed, chosen = lax.optimization_barrier(
        (reply, all_latents, all_d_out, normed, chosen)
    )
    kept, sent, slotted = gradients(
        counts, groups, core.reshape(1), queries, d_mixed, pairs, reply
    )
    slotted = exchange(slotted, SEQ)

    d_half = jnp.concatenate([kept, other_core(sent)], axis=0)
    term = lax.dot_general(normed, d_half, FIRST, preferred_element_type=f32).astype(bf16)
    share_rows = feature // 128
    term = term.reshape(group_count, 4, 4 * share_rows, 8, 128)
    z_at = lax.axis_index("z")

    def z_part(step):
        return lax.dynamic_index_in_dim(term, lax.rem(z_at + step, 4), 1, False)

    got = [ring_step(z_part(step), "z", step) for step in range(1, 4)]
    by_group = jnp.einsum("gsk,sklc->glc", chosen, slotted, preferred_element_type=f32)
    owned = jnp.sum(exchange(by_group, BATCH), axis=0).astype(bf16)
    heads = share(owned, BATCH, group_count).reshape(group_count * latent_count, 128)
    heads, got = lax.optimization_barrier((heads, got))
    ring_sum = sum([part.astype(f32) for part in got], z_part(0).astype(f32))
    ring_sum = ring_sum.astype(bf16).reshape(4, 2, 4, share_rows, 8, 128)
    ring_sum = ring_sum.transpose(0, 2, 1, 3, 4, 5).reshape(16, 2 * share_rows, 8, 128)
    grad_outproj, owned_parts = owners(heads, owned, all_latents, all_d_out)
    over_seq = exchange(owned_parts, SEQ)
    ring_sum, over_seq = lax.optimization_barrier((ring_sum, over_seq))
    ring_sum = exchange(ring_sum, ("x", "y"))
    out, d_latents, grad_query = finish(over_seq, latents[0], d_out[0], w_query, w_out)
    ring_sum, out, d_latents, grad_query = lax.optimization_barrier(
        (ring_sum, out, d_latents, grad_query)
    )

    chip_sum = jnp.sum(ring_sum.astype(f32), axis=0).reshape(2, share_rows, model_width)
    kept_sum = lax.dynamic_index_in_dim(chip_sum, core, 0, False)
    got_sum = other_core(lax.dynamic_index_in_dim(chip_sum, 1 - core, 0, False))
    grad_kv = jnp.where(
        core == 0,
        jnp.concatenate([kept_sum, got_sum], axis=1),
        jnp.concatenate([got_sum, kept_sum], axis=1),
    )
    return (out[None], d_latents[None], grad_query, grad_outproj, grad_kv)


def solution(mesh):
    chips = Mesh(mesh.devices.reshape(4, 2, 4, 4), ("x", "core", "z", "y"))
    in_specs = (
        P(BATCH, None, None),
        P(ALL, None, None),
        P(ALL),
        P(ALL),
        P(),
        P(),
        P(),
        P(BATCH, None, None),
    )
    out_specs = (
        P(BATCH, None, None),
        P(BATCH, None, None),
        P(SEQ, None),
        P(SEQ, None),
        P(ALL, None),
    )
    return jax.shard_map(local, mesh=chips, in_specs=in_specs, out_specs=out_specs, check_vma=False)
```

time: 173 us -> 157 us (0.908); the launches traced: 170 us -> 156 us
  Pallas kernels: 48 us -> 32.2 us
  starting transfers between devices: 49.3 us -> 44.2 us
  blocking collectives: 14.5 us -> 19.5 us
    pallas_call x4 -> x1, Pallas kernels: 15.1 us -> 7.61 us  [attend(): pl.pallas_call(attend_kernel, out_shape=(small, small, jax.ShapeDtypeStru...]
    all_to_all x1 -> x2, blocking collectives: 14.5 us -> 19.5 us  [exchange(): return lax.all_to_all(values, axes, 0, 0, tiled=True)]
    pallas_call x1, Pallas kernels: 11.2 us -> 8.53 us  [gradients(): pl.pallas_call(grads_kernel, grid=(4,), out_shape=(jax.ShapeDtypeStruct((...]
    all_to_all x6 -> x5, starting transfers between devices: 29.8 us -> 27.2 us  [exchange(): return lax.all_to_all(values, axes, 0, 0, tiled=True)]
    pallas_call x1, Pallas kernels: 8.94 us -> 6.44 us  [project_pairs(): pl.pallas_call(pairs_kernel, grid=(width // tile,), out_shape=(jax.ShapeD...]
    pallas_call x1, Pallas kernels: 4.55 us -> 2.19 us  [finish(): pl.pallas_call(finish_kernel, out_shape=(small, small, jax.ShapeDtypeStru...]
    ppermute x11 -> x7, starting transfers between devices: 9.17 us -> 6.98 us  [other_core(): return lax.ppermute(values, 'core', [(0, 1), (1, 0)])]
    unnamed x47 -> x40, local copies, waits for them, and re-layouts: 5.01 us -> 5.68 us
  transfers between devices with their start and end apart: 26 -> 18, of which waited for: 7 -> 11; matrix products, arithmetic and copies ran while one was open for 7% -> 8% of each run, Pallas kernels for 16% -> 8%
where the time goes in v4:
time: 157 us; the launch traced here: 156 us
  starting transfers between devices  44.2 us (28%)
  waiting for transfers between devices  40.3 us (26%)
  Pallas kernels  32.2 us (21%)
  blocking collectives  19.5 us (12%)
  local copies, waits for them, and re-layouts  9.59 us (6%)
  other arithmetic  4.83 us (3%)
  matrix products  4.78 us (3%)
    all_to_all x5, waiting for transfers between devices, exchange(): return lax.all_to_all(values, axes, 0, 0, tiled=True)  31.8 us
    all_to_all x5, starting transfers between devices, exchange(): return lax.all_to_all(values, axes, 0, 0, tiled=True)  27.2 us
    all_to_all x2, blocking collectives, exchange(): return lax.all_to_all(values, axes, 0, 0, tiled=True)  19.5 us
    ppermute x6, starting transfers between devices, ring_step(): return lax.ppermute(values, axis, [(i, (i + step) % 4) for i in range(4)])  9.97 us
    pallas_call x1, Pallas kernels, gradients(): pl.pallas_call(grads_kernel, grid=(4,), out_shape=(jax.ShapeDtypeStruct((...  8.53 us
    pallas_call x1, Pallas kernels, attend(): pl.pallas_call(attend_kernel, out_shape=(small, small, jax.ShapeDtypeStru...  7.61 us
    ppermute x6, waiting for transfers between devices, ring_step(): return lax.ppermute(values, axis, [(i, (i + step) % 4) for i in range(4)])  7.1 us
    ppermute x7, starting transfers between devices, other_core(): return lax.ppermute(values, 'core', [(0, 1), (1, 0)])  6.98 us
  transfers between devices with their start and end apart: 18, of which 11 were waited for; matrix products, arithmetic and copies ran while one was open for 8% of the time, Pallas kernels for 8%

profile of v4, /device:TPU:1, one launch (start us, length us, event | category | flops | bytes accessed | tf_op | source)
XLA Modules:
  0.0 156.4 jit_solution(11232761182157688039)
XLA Ops:
  2.5 2.1 %collective-permute-start = (bf16[2,64,1024]{2,1,0:T(8,128)(2,1)S(1)}, bf16[2,64,1024]{2,1,0:T(8,128)(2,1)S(1)}, u32[]{:S(2)}, u32[]{:S(2)}) collective-permute-start(bf16[2,64,1024]{2,1,0:T(8,128)(2,1)S(1)} %constant_dynamic-update-slice_fusion.refs_0_), channel_id=1, source_target_pairs={{0,32},{32,64},{64,96},{96,0},{1,33},{33,65},{65,97},{97,1},{2,34}... | collective-permute-start | bytes 786440 | tf_op jit(solution)/shard_map/ppermute | solution.py:50
  4.6 2.5 %collective-permute-start.1 = (bf16[2,64,1024]{2,1,0:T(8,128)(2,1)S(1)}, bf16[2,64,1024]{2,1,0:T(8,128)(2,1)S(1)}, u32[]{:S(2)}, u32[]{:S(2)}) collective-permute-start(bf16[2,64,1024]{2,1,0:T(8,128)(2,1)S(1)} %constant_dynamic-update-slice_fusion.refs_0_), channel_id=1, source_target_pairs={{0,64},{32,96},{64,0},{96,32},{1,65},{33,97},{65,1},{97,33},{2,66}... | collective-permute-start | bytes 786440 | tf_op jit(solution)/shard_map/ppermute | solution.py:50
  8.2 6.4 %shard_map.119 = (bf16[512,1152]{1,0:T(8,128)(2,1)}, bf16[512,2048]{1,0:T(8,128)(2,1)}) custom-call(bf16[512,1152]{1,0:T(8,128)(2,1)} %bitcast.53, bf16[1152,2048]{1,0:T(8,128)(2,1)} %w_ref.1), custom_call_target="tpu_custom_call" | custom-call | flops 2415919104 | bytes 9437184 | tf_op jit(solution)/shard_map/pallas_call | solution.py:94
  14.6 3.7 %collective-permute-done.1.refs_2_ = bf16[2,64,1024]{2,1,0:T(8,128)(2,1)S(1)} collective-permute-done((bf16[2,64,1024]{2,1,0:T(8,128)(2,1)S(1)}, bf16[2,64,1024]{2,1,0:T(8,128)(2,1)S(1)}, u32[]{:S(2)}, u32[]{:S(2)}) %collective-permute-start.1) | collective-permute-done | bytes 262176 | tf_op jit(solution)/shard_map/ppermute | solution.py:50
  23.3 7.6 %shard_map.120 = (bf16[256,1024]{1,0:T(8,128)(2,1)}, bf16[256,1024]{1,0:T(8,128)(2,1)}, f32[128,1,256]{2,1,0:T(1,128)}) custom-call(s32[4]{0:T(128)} %counts.3, s32[4]{0:T(128)} %groups.3, s32[4]{0:T(128)} %fusion.12.places, bf16[2,64,1024]{2,1,0:T(8,128)(2,1)} %copy-done.6, bf16[2,64,1024]{2,1,0:T(8,128)(2,1)} %copy-done.10, ...), custom_call_target="tpu_custom_call" | custom-call | flops 6442450944 | bytes 10485760 | tf_op jit(solution)/shard_map/pallas_call | solution.py:256
  31.5 9.7 %all-to-all-start = ((f32[128,1,256]{2,1,0:T(1,128)}), f32[128,1,256]{2,1,0:T(1,128)S(1)}, u32[]{:S(2)}, u32[]{:S(2)}) async-start(f32[128,1,256]{2,1,0:T(1,128)} %get-tuple-element.53), calls=%async_computation | async-start | bytes 262144 | tf_op jit(solution)/shard_map/all_to_all | solution.py:38
  41.2 3.2 %shard_map.122 = (bf16[512,1024]{1,0:T(8,128)(2,1)}, bf16[512,1024]{1,0:T(8,128)(2,1)}) custom-call(s32[8]{0:T(128)} %stack.35.owners, bf16[2,64,1024]{2,1,0:T(8,128)(2,1)} %copy-done.6, bf16[2,64,1024]{2,1,0:T(8,128)(2,1)} %copy-done.10, bf16[2,64,1024]{2,1,0:T(8,128)(2,1)} %copy-done.11, bf16[2,64,1024]{2,1,0:T(8,128)(2,1)} %copy-done.12, ...), custom_call_target="tpu_custom_call" | custom-call | flops 4194304 | bytes 4194304 | tf_op jit(solution)/shard_map/pallas_call | solution.py:439
  44.4 7.0 %all-to-all-done.in_ref = f32[128,1,256]{2,1,0:T(1,128)S(1)} async-done(((f32[128,1,256]{2,1,0:T(1,128)}), f32[128,1,256]{2,1,0:T(1,128)S(1)}, u32[]{:S(2)}, u32[]{:S(2)}) %all-to-all-start) | async-done | bytes 131104 | tf_op jit(solution)/shard_map/all_to_all | solution.py:38
  52.3 4.8 %all-to-all-start.1 = ((f32[128,1,256]{2,1,0:T(1,128)}), f32[128,1,256]{2,1,0:T(1,128)}, u32[]{:S(2)}, u32[]{:S(2)}) async-start(f32[128,1,256]{2,1,0:T(1,128)} %shard_map.121), calls=%async_computation.1 | async-start | bytes 262144 | tf_op jit(solution)/shard_map/all_to_all | solution.py:38
  58.8 8.5 %all-to-all-done.1.reply_ref = f32[128,1,256]{2,1,0:T(1,128)} async-done(((f32[128,1,256]{2,1,0:T(1,128)}), f32[128,1,256]{2,1,0:T(1,128)}, u32[]{:S(2)}, u32[]{:S(2)}) %all-to-all-start.1) | async-done | bytes 131104 | tf_op jit(solution)/shard_map/all_to_all | solution.py:38
  67.3 8.5 %shard_map.123 = (bf16[512,1024]{1,0:T(8,128)(2,1)}, bf16[512,1024]{1,0:T(8,128)(2,1)}, bf16[16,3,64,128]{3,2,1,0:T(8,128)(2,1)}) custom-call(s32[4]{0:T(128)} %counts.3, s32[4]{0:T(128)} %groups.3, s32[1]{0:T(128)} %bitcast.10.core, bf16[256,1024]{1,0:T(8,128)(2,1)} %get-tuple-element.59.q_ref, bf16[256,1024]{1,0:T(8,128)(2,1)} %get-tuple-element.60.d_ref, ...), custom_call_target="tpu_custom_call" | custom-call | flops 8589934592 | bytes 8388608 | tf_op jit(solution)/shard_map/pallas_call | solution.py:403
  76.4 3.8 %all-to-all-start.2 = ((bf16[16,3,64,128]{3,2,1,0:T(8,128)(2,1)}), bf16[16,3,64,128]{3,2,1,0:T(8,128)(2,1)S(1)}, u32[]{:S(2)}, u32[]{:S(2)}) async-start(bf16[16,3,64,128]{3,2,1,0:T(8,128)(2,1)} %get-tuple-element.65), calls=%async_computation.2 | async-start | bytes 1572864 | tf_op jit(solution)/shard_map/all_to_all | solution.py:38
  80.2 4.2 %fusion.3 = bf16[144,8,8,128]{3,1,2,0:T(8,128)(2,1)S(1)} fusion(bf16[1024,1152]{1,0:T(8,128)(2,1)S(1)} %pad_maximum_fusion, bf16[512,1024]{1,0:T(8,128)(2,1)} %collective-permute-done.8, bf16[512,1024]{1,0:T(8,128)(2,1)} %get-tuple-element.62), kind=kOutput, calls=%fused_computation.5 | convolution fusion | flops 2421293056 | bytes 6815744 | tf_op jit(solution)/shard_map/dot_general | solution.py:558
  87.8 2.8 %collective-permute-start.10 = (bf16[8,36,8,128]{3,2,1,0:T(8,128)(2,1)}, bf16[8,36,8,128]{3,2,1,0:T(8,128)(2,1)S(1)}, u32[]{:S(2)}, u32[]{:S(2)}) collective-permute-start(bf16[8,36,8,128]{3,2,1,0:T(8,128)(2,1)} %get-tuple-element.84), channel_id=1, source_target_pairs={{0,8},{4,12},{8,0},{12,4},{1,9},{5,13},{9,1},{13,5},{2,10},{6,14},... | collective-permute-start | bytes 1769480 | tf_op jit(solution)/shard_map/ppermute | solution.py:50
  92.0 3.0 %all-to-all-done.2 = bf16[16,3,64,128]{3,2,1,0:T(8,128)(2,1)S(1)} async-done(((bf16[16,3,64,128]{3,2,1,0:T(8,128)(2,1)}), bf16[16,3,64,128]{3,2,1,0:T(8,128)(2,1)S(1)}, u32[]{:S(2)}, u32[]{:S(2)}) %all-to-all-start.2) | async-done | bytes 786464 | tf_op jit(solution)/shard_map/all_to_all | solution.py:38
  95.7 10.4 %all_to_all.35 = f32[8,64,128]{2,1,0:T(8,128)S(1)} all-to-all(f32[8,64,128]{2,1,0:T(8,128)S(1)} %copy.24), channel_id=1, replica_groups=mesh['x'=4,'core'=2,'z'=4,'y'=4] {'x','core'}, dimensions={0} | all-to-all | bytes 524288 | tf_op jit(solution)/shard_map/all_to_all | solution.py:38
  106.2 9.1 %all_to_all.36 = bf16[8,64,128]{2,1,0:T(8,128)(2,1)} all-to-all(bf16[8,64,128]{2,1,0:T(8,128)(2,1)S(1)} %broadcast_in_dim.20), channel_id=1, replica_groups=mesh['x'=4,'core'=2,'z'=4,'y'=4] {'x','core'}, dimensions={0} | all-to-all | bytes 262144 | tf_op jit(solution)/shard_map/all_to_all | solution.py:38
  118.6 3.3 %shard_map.124 = (f32[64,1024]{1,0:T(8,128)}, bf16[16,128,128]{2,1,0:T(8,128)(2,1)}) custom-call(bf16[512,128]{1,0:T(8,128)(2,1)} %bitcast.51, bf16[64,128]{1,0:T(8,128)(2,1)} %copy-done.17, bf16[512,1024]{1,0:T(8,128)(2,1)} %get-tuple-element.70.latents_ref, bf16[512,1024]{1,0:T(8,128)(2,1)} %get-tuple-element.71.d_out_ref), custom_call_target="tpu_custom_call" | custom-call | flops 536870912 | bytes 4194304 | tf_op jit(solution)/shard_map/pallas_call | solution.py:467
  122.0 5.4 %all-to-all-start.5 = ((bf16[16,128,128]{2,1,0:T(8,128)(2,1)}), bf16[16,128,128]{2,1,0:T(8,128)(2,1)S(1)}, u32[]{:S(2)}, u32[]{:S(2)}) async-start(bf16[16,128,128]{2,1,0:T(8,128)(2,1)} %get-tuple-element.72), calls=%async_computation.5 | async-start | bytes 1048576 | tf_op jit(solution)/shard_map/all_to_all | solution.py:38
  130.3 7.6 %all-to-all-done.5.in_ref = bf16[16,128,128]{2,1,0:T(8,128)(2,1)S(1)} async-done(((bf16[16,128,128]{2,1,0:T(8,128)(2,1)}), bf16[16,128,128]{2,1,0:T(8,128)(2,1)S(1)}, u32[]{:S(2)}, u32[]{:S(2)}) %all-to-all-start.5) | async-done | bytes 524320 | tf_op jit(solution)/shard_map/all_to_all | solution.py:38
  137.9 3.6 %all-to-all-start.6 = ((bf16[16,18,8,128]{3,2,1,0:T(8,128)(2,1)}), bf16[16,18,8,128]{3,2,1,0:T(8,128)(2,1)S(1)}, u32[]{:S(2)}, u32[]{:S(2)}) async-start(bf16[16,18,8,128]{3,2,1,0:T(8,128)(2,1)} %bitcast.21), calls=%async_computation.6 | async-start | bytes 1179648 | tf_op jit(solution)/shard_map/all_to_all | solution.py:38
  143.1 2.2 %shard_map.125 = (bf16[64,1024]{1,0:T(8,128)(2,1)}, bf16[64,1024]{1,0:T(8,128)(2,1)}, f32[64,1024]{1,0:T(8,128)}) custom-call(bf16[16,128,128]{2,1,0:T(8,128)(2,1)S(1)} %all-to-all-done.5.in_ref, bf16[64,1024]{1,0:T(8,128)(2,1)S(1)} %bitcast.46, bf16[64,1024]{1,0:T(8,128)(2,1)S(1)} %bitcast.47, bf16[1024,1024]{1,0:T(8,128)(2,1)S(1)} %copy-done, ...), custom_call_target="tpu_custom_call" | custom-call | tf_op jit(solution)/shard_map/pallas_call | solution.py:510
  145.3 5.7 %all-to-all-done.6 = bf16[16,18,8,128]{3,2,1,0:T(8,128)(2,1)S(1)} async-done(((bf16[16,18,8,128]{3,2,1,0:T(8,128)(2,1)}), bf16[16,18,8,128]{3,2,1,0:T(8,128)(2,1)S(1)}, u32[]{:S(2)}, u32[]{:S(2)}) %all-to-all-start.6) | async-done | bytes 589856 | tf_op jit(solution)/shard_map/all_to_all | solution.py:38
  151.1 3.7 %collective-permute-start.12 = (f32[9,1024]{1,0:T(8,128)S(1)}, f32[9,1024]{1,0:T(8,128)S(1)}, u32[]{:S(2)}, u32[]{:S(2)}) collective-permute-start(f32[9,1024]{1,0:T(8,128)S(1)} %get-tuple-element.87), channel_id=1, source_target_pairs={{0,16},{16,0},{1,17},{17,1},{2,18},{18,2},{3,19},{19,3},{4,20},{20... | collective-permute-start | bytes 110600 | tf_op jit(solution)/shard_map/ppermute | solution.py:46
  (80 shorter events, 26.7 us)
Async XLA Ops:
  2.5 15.9 %copy-start.6 = (bf16[2,64,1024]{2,1,0:T(8,128)(2,1)}, bf16[2,64,1024]{2,1,0:T(8,128)(2,1)S(1)}, u32[]{:S(2)}) copy-start(bf16[2,64,1024]{2,1,0:T(8,128)(2,1)S(1)} %constant_dynamic-update-slice_fusion.refs_0_) | copy-start | bytes 786436
  2.5 12.2 %collective-permute-start = (bf16[2,64,1024]{2,1,0:T(8,128)(2,1)S(1)}, bf16[2,64,1024]{2,1,0:T(8,128)(2,1)S(1)}, u32[]{:S(2)}, u32[]{:S(2)}) collective-permute-start(bf16[2,64,1024]{2,1,0:T(8,128)(2,1)S(1)} %constant_dynamic-update-slice_fusion.refs_0_), channel_id=1, source_target_pairs={{0,32},{32,64},{64,96},{96,0},{1,33},{33,65},{65,97},{97,1},{2,34}... | collective-permute-start | bytes 786440 | tf_op jit(solution)/shard_map/ppermute | solution.py:50
  4.6 13.8 %collective-permute-start.1 = (bf16[2,64,1024]{2,1,0:T(8,128)(2,1)S(1)}, bf16[2,64,1024]{2,1,0:T(8,128)(2,1)S(1)}, u32[]{:S(2)}, u32[]{:S(2)}) collective-permute-start(bf16[2,64,1024]{2,1,0:T(8,128)(2,1)S(1)} %constant_dynamic-update-slice_fusion.refs_0_), channel_id=1, source_target_pairs={{0,64},{32,96},{64,0},{96,32},{1,65},{33,97},{65,1},{97,33},{2,66}... | collective-permute-start | bytes 786440 | tf_op jit(solution)/shard_map/ppermute | solution.py:50
  7.0 11.3 %collective-permute-start.2 = (bf16[2,64,1024]{2,1,0:T(8,128)(2,1)S(1)}, bf16[2,64,1024]{2,1,0:T(8,128)(2,1)S(1)}, u32[]{:S(2)}, u32[]{:S(2)}) collective-permute-start(bf16[2,64,1024]{2,1,0:T(8,128)(2,1)S(1)} %constant_dynamic-update-slice_fusion.refs_0_), channel_id=1, source_target_pairs={{0,96},{32,0},{64,32},{96,64},{1,97},{33,1},{65,33},{97,65},{2,98}... | collective-permute-start | bytes 786440 | tf_op jit(solution)/shard_map/ppermute | solution.py:50
  8.2 13.0 %copy-start.18 = (s32[4]{0:T(128)S(1)}, s32[4]{0:T(128)}, u32[]{:S(2)}) copy-start(s32[4]{0:T(128)} %groups.3) | copy-start | bytes 52
  18.4 3.3 %collective-permute-start.3 = (bf16[2,64,1024]{2,1,0:T(8,128)(2,1)S(1)}, bf16[2,64,1024]{2,1,0:T(8,128)(2,1)S(1)}, u32[]{:S(2)}, u32[]{:S(2)}) collective-permute-start(bf16[2,64,1024]{2,1,0:T(8,128)(2,1)S(1)} %constant_dynamic-update-slice_fusion.refs_0_), channel_id=1, source_target_pairs={{0,16},{16,0},{1,17},{17,1},{2,18},{18,2},{3,19},{19,3},{4,20},{20... | collective-permute-start | bytes 786440 | tf_op jit(solution)/shard_map/ppermute | solution.py:46
  20.0 1.7 %collective-permute-start.4 = (bf16[2,64,1024]{2,1,0:T(8,128)(2,1)S(1)}, bf16[2,64,1024]{2,1,0:T(8,128)(2,1)S(1)}, u32[]{:S(2)}, u32[]{:S(2)}) collective-permute-start(bf16[2,64,1024]{2,1,0:T(8,128)(2,1)S(1)} %collective-permute-done.refs_1_), channel_id=1, source_target_pairs={{0,16},{16,0},{1,17},{17,1},{2,18},{18,2},{3,19},{19,3},{4,20},{20... | collective-permute-start | bytes 786440 | tf_op jit(solution)/shard_map/ppermute | solution.py:46
  20.1 1.8 %collective-permute-start.5 = (bf16[2,64,1024]{2,1,0:T(8,128)(2,1)S(1)}, bf16[2,64,1024]{2,1,0:T(8,128)(2,1)S(1)}, u32[]{:S(2)}, u32[]{:S(2)}) collective-permute-start(bf16[2,64,1024]{2,1,0:T(8,128)(2,1)S(1)} %collective-permute-done.1.refs_2_), channel_id=1, source_target_pairs={{0,16},{16,0},{1,17},{17,1},{2,18},{18,2},{3,19},{19,3},{4,20},{20... | collective-permute-start | bytes 786440 | tf_op jit(solution)/shard_map/ppermute | solution.py:46
  20.5 1.8 %collective-permute-start.6 = (bf16[2,64,1024]{2,1,0:T(8,128)(2,1)S(1)}, bf16[2,64,1024]{2,1,0:T(8,128)(2,1)S(1)}, u32[]{:S(2)}, u32[]{:S(2)}) collective-permute-start(bf16[2,64,1024]{2,1,0:T(8,128)(2,1)S(1)} %collective-permute-done.2.refs_3_), channel_id=1, source_target_pairs={{0,16},{16,0},{1,17},{17,1},{2,18},{18,2},{3,19},{19,3},{4,20},{20... | collective-permute-start | bytes 786440 | tf_op jit(solution)/shard_map/ppermute | solution.py:46
  31.0 26.4 %collective-permute-start.7 = (bf16[512,1152]{1,0:T(8,128)(2,1)S(1)}, bf16[512,1152]{1,0:T(8,128)(2,1)}, u32[]{:S(2)}, u32[]{:S(2)}) collective-permute-start(bf16[512,1152]{1,0:T(8,128)(2,1)S(1)} %copy-done.5), channel_id=1, source_target_pairs={{0,16},{16,0},{1,17},{17,1},{2,18},{18,2},{3,19},{19,3},{4,20},{20... | collective-permute-start | bytes 3538952 | tf_op jit(solution)/shard_map/ppermute | solution.py:46
  31.5 19.9 %all-to-all-start = ((f32[128,1,256]{2,1,0:T(1,128)}), f32[128,1,256]{2,1,0:T(1,128)S(1)}, u32[]{:S(2)}, u32[]{:S(2)}) async-start(f32[128,1,256]{2,1,0:T(1,128)} %get-tuple-element.53), calls=%async_computation | async-start | bytes 262144 | tf_op jit(solution)/shard_map/all_to_all | solution.py:38
  52.3 15.0 %all-to-all-start.1 = ((f32[128,1,256]{2,1,0:T(1,128)}), f32[128,1,256]{2,1,0:T(1,128)}, u32[]{:S(2)}, u32[]{:S(2)}) async-start(f32[128,1,256]{2,1,0:T(1,128)} %shard_map.121), calls=%async_computation.1 | async-start | bytes 262144 | tf_op jit(solution)/shard_map/all_to_all | solution.py:38
  75.9 4.3 %collective-permute-start.8 = (bf16[512,1024]{1,0:T(8,128)(2,1)}, bf16[512,1024]{1,0:T(8,128)(2,1)}, u32[]{:S(2)}, u32[]{:S(2)}) collective-permute-start(bf16[512,1024]{1,0:T(8,128)(2,1)} %get-tuple-element.63), channel_id=1, source_target_pairs={{0,16},{16,0},{1,17},{17,1},{2,18},{18,2},{3,19},{19,3},{4,20},{20... | collective-permute-start | bytes 3145736 | tf_op jit(solution)/shard_map/ppermute | solution.py:46
  76.4 18.6 %all-to-all-start.2 = ((bf16[16,3,64,128]{3,2,1,0:T(8,128)(2,1)}), bf16[16,3,64,128]{3,2,1,0:T(8,128)(2,1)S(1)}, u32[]{:S(2)}, u32[]{:S(2)}) async-start(bf16[16,3,64,128]{3,2,1,0:T(8,128)(2,1)} %get-tuple-element.65), calls=%async_computation.2 | async-start | bytes 1572864 | tf_op jit(solution)/shard_map/all_to_all | solution.py:38
  87.8 27.5 %collective-permute-start.10 = (bf16[8,36,8,128]{3,2,1,0:T(8,128)(2,1)}, bf16[8,36,8,128]{3,2,1,0:T(8,128)(2,1)S(1)}, u32[]{:S(2)}, u32[]{:S(2)}) collective-permute-start(bf16[8,36,8,128]{3,2,1,0:T(8,128)(2,1)} %get-tuple-element.84), channel_id=1, source_target_pairs={{0,8},{4,12},{8,0},{12,4},{1,9},{5,13},{9,1},{13,5},{2,10},{6,14},... | collective-permute-start | bytes 1769480 | tf_op jit(solution)/shard_map/ppermute | solution.py:50
  90.6 26.3 %collective-permute-start.11 = (bf16[8,36,8,128]{3,2,1,0:T(8,128)(2,1)}, bf16[8,36,8,128]{3,2,1,0:T(8,128)(2,1)S(1)}, u32[]{:S(2)}, u32[]{:S(2)}) collective-permute-start(bf16[8,36,8,128]{3,2,1,0:T(8,128)(2,1)} %get-tuple-element.83), channel_id=1, source_target_pairs={{0,12},{4,0},{8,4},{12,8},{1,13},{5,1},{9,5},{13,9},{2,14},{6,2},{... | collective-permute-start | bytes 1769480 | tf_op jit(solution)/shard_map/ppermute | solution.py:50
  91.4 27.2 %collective-permute-start.9 = (bf16[8,36,8,128]{3,2,1,0:T(8,128)(2,1)}, bf16[8,36,8,128]{3,2,1,0:T(8,128)(2,1)S(1)}, u32[]{:S(2)}, u32[]{:S(2)}) collective-permute-start(bf16[8,36,8,128]{3,2,1,0:T(8,128)(2,1)} %get-tuple-element.85), channel_id=1, source_target_pairs={{0,4},{4,8},{8,12},{12,0},{1,5},{5,9},{9,13},{13,1},{2,6},{6,10},{... | collective-permute-start | bytes 1769480 | tf_op jit(solution)/shard_map/ppermute | solution.py:50
  106.1 12.5 %copy-start.17 = (bf16[64,128]{1,0:T(8,128)(2,1)}, bf16[64,128]{1,0:T(8,128)(2,1)S(1)}, u32[]{:S(2)}) copy-start(bf16[64,128]{1,0:T(8,128)(2,1)S(1)} %reduce_sum.18.owned_ref) | copy-start | bytes 49156
  122.0 15.9 %all-to-all-start.5 = ((bf16[16,128,128]{2,1,0:T(8,128)(2,1)}), bf16[16,128,128]{2,1,0:T(8,128)(2,1)S(1)}, u32[]{:S(2)}, u32[]{:S(2)}) async-start(bf16[16,128,128]{2,1,0:T(8,128)(2,1)} %get-tuple-element.72), calls=%async_computation.5 | async-start | bytes 1048576 | tf_op jit(solution)/shard_map/all_to_all | solution.py:38
  127.4 14.2 %copy-start = (bf16[1024,1024]{1,0:T(8,128)(2,1)S(1)}, bf16[1024,1024]{1,0:T(8,128)(2,1)}, u32[]{:S(2)}) copy-start(bf16[1024,1024]{1,0:T(8,128)(2,1)} %w_query_ref.1) | copy-start | bytes 6291460
  127.4 14.2 %copy-start.2 = (bf16[1,64,1024]{2,1,0:T(8,128)(2,1)S(1)}, bf16[1,64,1024]{2,1,0:T(8,128)(2,1)}, u32[]{:S(2)}) copy-start(bf16[1,64,1024]{2,1,0:T(8,128)(2,1)} %param.8) | copy-start | bytes 393220
  127.4 14.1 %copy-start.3 = (bf16[1,64,1024]{2,1,0:T(8,128)(2,1)S(1)}, bf16[1,64,1024]{2,1,0:T(8,128)(2,1)}, u32[]{:S(2)}) copy-start(bf16[1,64,1024]{2,1,0:T(8,128)(2,1)} %param.15) | copy-start | bytes 393220
  137.9 13.1 %all-to-all-start.6 = ((bf16[16,18,8,128]{3,2,1,0:T(8,128)(2,1)}), bf16[16,18,8,128]{3,2,1,0:T(8,128)(2,1)S(1)}, u32[]{:S(2)}, u32[]{:S(2)}) async-start(bf16[16,18,8,128]{3,2,1,0:T(8,128)(2,1)} %bitcast.21), calls=%async_computation.6 | async-start | bytes 1179648 | tf_op jit(solution)/shard_map/all_to_all | solution.py:38
  151.1 4.6 %collective-permute-start.12 = (f32[9,1024]{1,0:T(8,128)S(1)}, f32[9,1024]{1,0:T(8,128)S(1)}, u32[]{:S(2)}, u32[]{:S(2)}) collective-permute-start(f32[9,1024]{1,0:T(8,128)S(1)} %get-tuple-element.87), channel_id=1, source_target_pairs={{0,16},{16,0},{1,17},{17,1},{2,18},{18,2},{3,19},{19,3},{4,20},{20... | collective-permute-start | bytes 110600 | tf_op jit(solution)/shard_map/ppermute | solution.py:46
  (13 other events, 56.6 us)

commit v5 on v4

--- a/solution.py
+++ b/solution.py
@@ -14,6 +14,7 @@
 ALL = BATCH + SEQ
 SLOTS = 3
 WIDE = 256
+PER_STEP = 2
 
 epsilon = 1e-06
 f32 = jnp.float32
@@ -217,7 +218,7 @@
                 moment_ref[block, p : p + 1, :] = moment[:, part : part + 128]
         return carry
 
-    lax.fori_loop(0, blocks, one_block, 0)
+    lax.fori_loop(0, blocks, one_block, 0, unroll=2)
     own = [groups[i] for i in range(blocks)]
     slots = slots_of(own)
     left = low_lanes((8, 128))
@@ -278,10 +279,51 @@
 
 def block_specs(latent_count, width):
     return [
-        pl.BlockSpec((latent_count, width), lambda i: (i, 0)),
-        pl.BlockSpec((latent_count, width), lambda i: (i, 0)),
-        pl.BlockSpec((128, 2 * width), lambda i: (i, 0)),
+        pl.BlockSpec((PER_STEP * latent_count, width), lambda i: (i, 0)),
+        pl.BlockSpec((PER_STEP * latent_count, width), lambda i: (i, 0)),
+        pl.BlockSpec((PER_STEP * 128, 2 * width), lambda i: (i, 0)),
     ]
+
+
+def products_kernel(q_ref, d_ref, pairs_ref, scores_ref, d_weights_ref):
+    masks = head_masks()
+    width = q_ref.shape[1]
+    rows = q_ref.shape[0] // PER_STEP
+    scale = (width // H) ** (-0.5)
+    for sub in range(PER_STEP):
+        here = slice(sub * rows, sub * rows + rows)
+        there = slice(sub * 128, sub * 128 + 128)
+        for at in range(0, width, WIDE):
+            cols = slice(at, at + WIDE)
+            value_cols = slice(width + at, width + at + WIDE)
+            scores_ref[there, cols] = scale * lax.dot_general(
+                pairs_ref[there, cols],
+                spread(q_ref[here, cols], masks),
+                LAST,
+                preferred_element_type=f32,
+            )
+            d_weights_ref[there, cols] = lax.dot_general(
+                pairs_ref[there, value_cols],
+                spread(d_ref[here, cols], masks),
+                LAST,
+                preferred_element_type=f32,
+            )
+
+
+def products(queries, d_mixed, pairs):
+    width = queries.shape[1]
+    out = jax.ShapeDtypeStruct((pairs.shape[0], width), f32)
+    spec = pl.BlockSpec((PER_STEP * 128, width), lambda i: (i, 0))
+    return pl.pallas_call(
+        products_kernel,
+        grid=(4 // PER_STEP,),
+        out_shape=(out, out),
+        in_specs=block_specs(queries.shape[0] // 4, width),
+        out_specs=(spec, spec),
+        cost_estimate=pl.CostEstimate(
+            flops=2 * 1024 * 1024 * 1024, bytes_accessed=8 * 1024 * 1024, transcendentals=0
+        ),
+    )(queries, d_mixed, pairs)
 
 
 def totals_kernel(in_ref, out_ref):
@@ -317,6 +359,8 @@
     q_ref,
     d_ref,
     pairs_ref,
+    scores_ref,
+    d_weights_ref,
     reply_ref,
     kept_ref,
     sent_ref,
@@ -326,63 +370,71 @@
     mixed_now,
     query_now,
 ):
-    block = pl.program_id(0)
+    step = pl.program_id(0)
     masks = head_masks()
-    rows, width = q_ref.shape
+    width = q_ref.shape[1]
+    rows = q_ref.shape[0] // PER_STEP
     scale = (width // H) ** (-0.5)
-    usable = lax.broadcasted_iota(jnp.int32, (128, WIDE), 0) < counts[block]
+    position = lax.broadcasted_iota(jnp.int32, (128, WIDE), 0)
     left = low_lanes((8, 128))
     wide = low_lanes((rows, 128))
 
-    @pl.when(block == 0)
+    @pl.when(step == 0)
     def _():
         mixed_acc[...] = jnp.zeros_like(mixed_acc)
         query_acc[...] = jnp.zeros_like(query_acc)
 
-    slots = slots_of([groups[i] for i in range(4)])
-    slot = slots[0]
-    for i in range(1, 4):
-        slot = jnp.where(block == i, slots[i], slot)
-    group = groups[block]
-    def reply_rows(odd, cols):
-        first = 16 * group + 8 * odd
-        return jnp.concatenate([reply_ref[first + p, :, cols] for p in range(8)], axis=0)
-
     def row(pairs, at):
         first = at // 128
         return jnp.concatenate([pairs[p : p + 1] for p in range(first, first + WIDE // 128)], axis=1)
 
-    even = reply_rows(0, slice(0, 128))
-    odd = reply_rows(1, slice(0, 128))
-    top = jnp.where(left, even, pltpu.roll(odd, 64, 1))
-    inverse = jnp.where(left, pltpu.roll(even, 64, 1), odd)
-    delta = jnp.where(
-        left, reply_rows(0, slice(128, 256)), pltpu.roll(reply_rows(1, slice(128, 256)), 64, 1)
-    )
-    for at in range(0, width, WIDE):
-        cols = slice(at, at + WIDE)
-        value_cols = slice(width + at, width + at + WIDE)
-        q = spread(q_ref[:, cols], masks)
-        d = spread(d_ref[:, cols], masks)
-        k = pairs_ref[:, cols]
-        v = pairs_ref[:, value_cols]
-        s = lax.dot_general(k, q, LAST, preferred_element_type=f32) * scale
-        dw = lax.dot_general(v, d, LAST, preferred_element_type=f32)
-        weights = jnp.where(usable, jnp.exp(s - row(top, at)) * row(inverse, at), 0.0)
-        weights_b = weights.astype(bf16)
-        d_scores = (weights * (dw - row(delta, at)) * scale).astype(bf16)
-        d_values = jnp.dot(weights_b, d, preferred_element_type=f32)
-        d_keys = jnp.dot(d_scores, q, preferred_element_type=f32)
-        kept_ref[:, cols] = jnp.where(core[0] == 0, d_keys, d_values).astype(bf16)
-        sent_ref[:, cols] = jnp.where(core[0] == 0, d_values, d_keys).astype(bf16)
-        mixed = lax.dot_general(weights_b, v, FIRST, preferred_element_type=f32)
-        mixed_now[:, cols] = own_heads(mixed, rows)
-        query = lax.dot_general(d_scores, k, FIRST, preferred_element_type=f32)
-        query_now[:, cols] = own_heads(query, rows)
-    mixed_acc[slot] += mixed_now[...]
-    query_acc[slot] += query_now[...]
-
-    @pl.when(block == 3)
+    slots = slots_of([groups[i] for i in range(4)])
+    for sub in range(PER_STEP):
+        block = step * PER_STEP + sub
+        here = slice(sub * rows, sub * rows + rows)
+        there = slice(sub * 128, sub * 128 + 128)
+        usable = position < counts[block]
+        group = groups[block]
+
+        def reply_rows(odd, cols):
+            first = 16 * group + 8 * odd
+            return jnp.concatenate([reply_ref[first + p, :, cols] for p in range(8)], axis=0)
+
+        even = reply_rows(0, slice(0, 128))
+        odd = reply_rows(1, slice(0, 128))
+        top = jnp.where(left, even, pltpu.roll(odd, 64, 1))
+        inverse = jnp.where(left, pltpu.roll(even, 64, 1), odd)
+        delta = jnp.where(
+            left, reply_rows(0, slice(128, 256)), pltpu.roll(reply_rows(1, slice(128, 256)), 64, 1)
+        )
+        for at in range(0, width, WIDE):
+            cols = slice(at, at + WIDE)
+            value_cols = slice(width + at, width + at + WIDE)
+            q = spread(q_ref[here, cols], masks)
+            d = spread(d_ref[here, cols], masks)
+            k = pairs_ref[there, cols]
+            v = pairs_ref[there, value_cols]
+            s = scores_ref[there, cols]
+            dw = d_weights_ref[there, cols]
+            weights = jnp.where(usable, jnp.exp(s - row(top, at)) * row(inverse, at), 0.0)
+            weights_b = weights.astype(bf16)
+            d_scores = (weights * (dw - row(delta, at)) * scale).astype(bf16)
+            d_values = jnp.dot(weights_b, d, preferred_element_type=f32)
+            d_keys = jnp.dot(d_scores, q, preferred_element_type=f32)
+            kept_ref[there, cols] = jnp.where(core[0] == 0, d_keys, d_values).astype(bf16)
+            sent_ref[there, cols] = jnp.where(core[0] == 0, d_values, d_keys).astype(bf16)
+            mixed = lax.dot_general(weights_b, v, FIRST, preferred_element_type=f32)
+            mixed_now[sub, :, cols] = own_heads(mixed, rows)
+            query = lax.dot_general(d_scores, k, FIRST, preferred_element_type=f32)
+            query_now[sub, :, cols] = own_heads(query, rows)
+    for sub in range(PER_STEP):
+        slot = slots[sub]
+        for at in range(1, 4 // PER_STEP):
+            slot = jnp.where(step == at, slots[at * PER_STEP + sub], slot)
+        mixed_acc[slot] += mixed_now[sub]
+        query_acc[slot] += query_now[sub]
+
+    @pl.when(step == 4 // PER_STEP - 1)
     def _():
         for at in range(SLOTS):
             for p in range(width // 128):
@@ -397,12 +449,12 @@
                 ).astype(bf16)
 
 
-def gradients(counts, groups, core, queries, d_mixed, pairs, reply):
+def gradients(counts, groups, core, queries, d_mixed, pairs, scores, d_weights, reply):
     width = queries.shape[1]
     rows = queries.shape[0] // 4
     return pl.pallas_call(
         grads_kernel,
-        grid=(4,),
+        grid=(4 // PER_STEP,),
         out_shape=(
             jax.ShapeDtypeStruct((pairs.shape[0], width), bf16),
             jax.ShapeDtypeStruct((pairs.shape[0], width), bf16),
@@ -410,18 +462,19 @@
         ),
         in_specs=[SMEM, SMEM, SMEM]
         + block_specs(rows, width)
+        + [pl.BlockSpec((PER_STEP * 128, width), lambda i: (i, 0))] * 2
         + [pl.BlockSpec((128, 1, 256), lambda i: (0, 0, 0))],
         out_specs=(
-            pl.BlockSpec((128, width), lambda i: (i, 0)),
-            pl.BlockSpec((128, width), lambda i: (i, 0)),
+            pl.BlockSpec((PER_STEP * 128, width), lambda i: (i, 0)),
+            pl.BlockSpec((PER_STEP * 128, width), lambda i: (i, 0)),
             pl.BlockSpec((H, SLOTS, rows, 128), lambda i: (0, 0, 0, 0)),
         ),
         scratch_shapes=[pltpu.VMEM((SLOTS, rows, width), f32)] * 2
-        + [pltpu.VMEM((rows, width), f32)] * 2,
+        + [pltpu.VMEM((PER_STEP, rows, width), f32)] * 2,
         cost_estimate=pl.CostEstimate(
             flops=8 * 1024 * 1024 * 1024, bytes_accessed=8 * 1024 * 1024, transcendentals=512 * 1024
         ),
-    )(counts, groups, core, queries, d_mixed, pairs, reply)
+    )(counts, groups, core, queries, d_mixed, pairs, scores, d_weights, reply)
 
 
 def prepare_kernel(owners, *refs):
@@ -454,11 +507,15 @@
         heads, d_out_ref[...], FIRST, preferred_element_type=f32
     )[:rows]
     query = lax.dot_general(latents_ref[...], heads, FIRST, preferred_element_type=f32)
-    high = query.astype(bf16).astype(f32)
-    query = jnp.where(low_lanes(query.shape), pltpu.roll(high, 64, 1), query - high).astype(bf16)
+    other = pltpu.roll(query, 64, 1)
+    half = rows // 2
+    left = low_lanes((half, 128))
     for at in range(H):
+        first, second = rows * at, rows * at + half
         out_ref[at, :rows] = owned_ref[...]
-        out_ref[at, rows:] = query[rows * at : rows * at + rows]
+        out_ref[at, rows:] = jnp.where(
+            left, other[first : first + half], query[second : second + half]
+        ).astype(bf16)
 
 
 def owners(heads, owned, normed_latents, d_outs):
@@ -468,7 +525,7 @@
         owners_kernel,
         out_shape=(
             jax.ShapeDtypeStruct((rows, width), f32),
-            jax.ShapeDtypeStruct((H, 2 * rows, 128), bf16),
+            jax.ShapeDtypeStruct((H, rows + rows // 2, 128), bf16),
         ),
         in_specs=[VMEM] * 4,
         out_specs=(VMEM, VMEM),
@@ -486,16 +543,19 @@
     left = low_lanes((rows, 128))
 
     def parts(head):
-        both = in_ref[head, rows : 2 * rows].astype(f32)
-        return in_ref[head, :rows].astype(f32), both + pltpu.roll(both, 64, 1)
+        both = in_ref[head, rows:].astype(f32)
+        return in_ref[head, :rows].astype(f32), both, pltpu.roll(both, 64, 1)
 
     for p in range(H // 2):
         cols = slice(128 * p, 128 * p + 128)
-        even, even_grad = parts(2 * p)
-        odd, odd_grad = parts(2 * p + 1)
+        even, even_grad, even_turned = parts(2 * p)
+        odd, odd_grad, odd_turned = parts(2 * p + 1)
         mixed[:, cols] = jnp.where(left, even, pltpu.roll(odd, 64, 1)).astype(bf16)
         d_query[:, cols] = jnp.where(left, pltpu.roll(even, 64, 1), odd).astype(bf16)
-        grad_query_ref[:, cols] = jnp.where(left, even_grad, odd_grad)
+        half = rows // 2
+        narrow = left[:half]
+        grad_query_ref[:half, cols] = jnp.where(narrow, even_grad, odd_turned)
+        grad_query_ref[half:, cols] = jnp.where(narrow, even_turned, odd_grad)
     latent = latent_ref[...].astype(f32)
     d_normed = lax.dot_general(d_query[...], w_query_ref[...], LAST, preferred_element_type=f32)
     d_latents_ref[...] = (d_out_ref[...].astype(f32) + rms_back(latent, d_normed)).astype(bf16)
@@ -529,14 +589,14 @@
 
     near = along_chips(jnp.concatenate([latents, d_out], axis=0))
     normed, pairs = project_pairs(frames.reshape(rows, feature), w_kv)
-    near, normed, pairs = lax.optimization_barrier((near, normed, pairs))
+    near = [lax.optimization_barrier((piece, normed, pairs))[0] for piece in near]
     pieces = near + [other_core(piece) for piece in near]
     queries, d_mixed, stats = attend(
         counts, groups, place_of(groups), pieces, w_query, w_out, pairs
     )
     sources = jnp.stack([group_at(j) for j in range(8)])
-    normed, sources, stats = lax.optimization_barrier((normed, sources, stats))
-    all_latents, all_d_out = prepare(sources, pieces)
+    normed, stats, queries, d_mixed = lax.optimization_barrier((normed, stats, queries, d_mixed))
+    scores, d_weights = products(queries, d_mixed, pairs)
     normed = jnp.concatenate([normed, other_core(normed)], axis=0)
     stats = exchange(stats, ALL)
     source_groups = lax.dynamic_slice(
@@ -545,12 +605,14 @@
     chosen = (
         jnp.arange(group_count, dtype=f32)[:, None, None] == source_groups.reshape(1, seq_count, SLOTS)
     ).astype(bf16)
-    reply = exchange(totals(stats), ALL)
-    reply, all_latents, all_d_out, normed, chosen = lax.optimization_barrier(
-        (reply, all_latents, all_d_out, normed, chosen)
+    reply, sources = lax.optimization_barrier((totals(stats), sources))
+    all_latents, all_d_out = prepare(sources, pieces)
+    reply = exchange(reply, ALL)
+    reply, all_latents, all_d_out, normed, chosen, scores, d_weights = lax.optimization_barrier(
+        (reply, all_latents, all_d_out, normed, chosen, scores, d_weights)
     )
     kept, sent, slotted = gradients(
-        counts, groups, core.reshape(1), queries, d_mixed, pairs, reply
+        counts, groups, core.reshape(1), queries, d_mixed, pairs, scores, d_weights, reply
     )
     slotted = exchange(slotted, SEQ)
 
@@ -563,31 +625,26 @@
     def z_part(step):
         return lax.dynamic_index_in_dim(term, lax.rem(z_at + step, 4), 1, False)
 
-    got = [ring_step(z_part(step), "z", step) for step in range(1, 4)]
+    parts = lax.optimization_barrier([z_part(step) for step in range(4)])
+    got = [ring_step(parts[step], "z", step) for step in range(1, 4)]
     by_group = jnp.einsum("gsk,sklc->glc", chosen, slotted, preferred_element_type=f32)
     owned = jnp.sum(exchange(by_group, BATCH), axis=0).astype(bf16)
     heads = share(owned, BATCH, group_count).reshape(group_count * latent_count, 128)
-    heads, got = lax.optimization_barrier((heads, got))
-    ring_sum = sum([part.astype(f32) for part in got], z_part(0).astype(f32))
-    ring_sum = ring_sum.astype(bf16).reshape(4, 2, 4, share_rows, 8, 128)
-    ring_sum = ring_sum.transpose(0, 2, 1, 3, 4, 5).reshape(16, 2 * share_rows, 8, 128)
     grad_outproj, owned_parts = owners(heads, owned, all_latents, all_d_out)
+    owned_parts, got = lax.optimization_barrier((owned_parts, got))
+    ring_sum = sum([part.astype(f32) for part in got], parts[0].astype(f32))
+    ring_sum = ring_sum.astype(bf16).reshape(group_count, 4, share_rows, 8, 128)
+    ring_sum = ring_sum.reshape(4 * group_count, share_rows, 8, 128)
     over_seq = exchange(owned_parts, SEQ)
     ring_sum, over_seq = lax.optimization_barrier((ring_sum, over_seq))
-    ring_sum = exchange(ring_sum, ("x", "y"))
+    ring_sum = exchange(ring_sum, BATCH + ("y",))
     out, d_latents, grad_query = finish(over_seq, latents[0], d_out[0], w_query, w_out)
     ring_sum, out, d_latents, grad_query = lax.optimization_barrier(
         (ring_sum, out, d_latents, grad_query)
     )
-
-    chip_sum = jnp.sum(ring_sum.astype(f32), axis=0).reshape(2, share_rows, model_width)
-    kept_sum = lax.dynamic_index_in_dim(chip_sum, core, 0, False)
-    got_sum = other_core(lax.dynamic_index_in_dim(chip_sum, 1 - core, 0, False))
-    grad_kv = jnp.where(
-        core == 0,
-        jnp.concatenate([kept_sum, got_sum], axis=1),
-        jnp.concatenate([got_sum, kept_sum], axis=1),
-    )
+    ring_sum = ring_sum.reshape(4, 2, 4, share_rows, 8, 128).astype(f32)
+    halves = jnp.sum(ring_sum, axis=(0, 2)).reshape(2, share_rows, model_width)
+    grad_kv = jnp.concatenate([halves[0], halves[1]], axis=1)
     return (out[None], d_latents[None], grad_query, grad_outproj, grad_kv)
 
 

time: 157 us -> 148 us (0.943)
  waiting for transfers between devices: 40.3 us -> 34.2 us
  starting transfers between devices: 44.2 us -> 40.8 us
  Pallas kernels: 32.2 us -> 34.3 us
  local copies, waits for them, and re-layouts: 9.59 us -> 7.72 us
    ppermute x6, waiting for transfers between devices: 7.1 us -> 3.47 us  [ring_step(): return lax.ppermute(values, axis, [(i, (i + step) % 4) for i in range(4)])]
    pallas_call x1 -> x2, Pallas kernels: 8.53 us -> 11.1 us  [the longest x1 6.75 us: gradients(): pl.pallas_call(grads_kernel, grid=(4 // PER_STEP,), out_shape=(jax.ShapeD...]
    all_to_all x5, waiting for transfers between devices: 31.8 us -> 30.1 us  [exchange(): return lax.all_to_all(values, axes, 0, 0, tiled=True)]
    ppermute x7 -> x6, starting transfers between devices: 6.98 us -> 5.9 us  [other_core(): return lax.ppermute(values, 'core', [(0, 1), (1, 0)])]
    unnamed x40 -> x39, local copies, waits for them, and re-layouts: 5.68 us -> 4.74 us
  transfers between devices with their start and end apart: 18 -> 17, of which waited for: 11 -> 8; matrix products, arithmetic and copies ran while one was open for 8% -> 8% of each run, Pallas kernels for 8% -> 14%
where the time goes in v5:
time: 148 us
  starting transfers between devices  40.8 us (28%)
  Pallas kernels  34.3 us (23%)
  waiting for transfers between devices  34.2 us (23%)
  blocking collectives  19.5 us (13%)
  local copies, waits for them, and re-layouts  7.72 us (5%)
  other arithmetic  5.48 us (4%)
  matrix products  4.78 us (3%)
    all_to_all x5, waiting for transfers between devices, exchange(): return lax.all_to_all(values, axes, 0, 0, tiled=True)  30.1 us
    all_to_all x5, starting transfers between devices, exchange(): return lax.all_to_all(values, axes, 0, 0, tiled=True)  26.2 us
    all_to_all x2, blocking collectives, exchange(): return lax.all_to_all(values, axes, 0, 0, tiled=True)  19.5 us
    ppermute x6, starting transfers between devices, ring_step(): return lax.ppermute(values, axis, [(i, (i + step) % 4) for i in range(4)])  8.76 us
    pallas_call x1, Pallas kernels, attend(): pl.pallas_call(attend_kernel, out_shape=(small, small, jax.ShapeDtypeStru...  7.26 us
    pallas_call x1, Pallas kernels, gradients(): pl.pallas_call(grads_kernel, grid=(4 // PER_STEP,), out_shape=(jax.ShapeD...  6.75 us
    pallas_call x1, Pallas kernels, project_pairs(): pl.pallas_call(pairs_kernel, grid=(width // tile,), out_shape=(jax.ShapeD...  6.43 us
    ppermute x6, starting transfers between devices, other_core(): return lax.ppermute(values, 'core', [(0, 1), (1, 0)])  5.9 us
  transfers between devices with their start and end apart: 17, of which 8 were waited for; matrix products, arithmetic and copies ran while one was open for 8% of the time, Pallas kernels for 14%

profile of v5, /device:TPU:1, one launch (start us, length us, event | category | flops | bytes accessed | tf_op | source)
XLA Modules:
  0.0 147.7 jit_solution(13681200012799450580)
XLA Ops:
  2.5 3.4 %collective-permute-start.2 = (bf16[2,64,1024]{2,1,0:T(8,128)(2,1)S(1)}, bf16[2,64,1024]{2,1,0:T(8,128)(2,1)S(1)}, u32[]{:S(2)}, u32[]{:S(2)}) collective-permute-start(bf16[2,64,1024]{2,1,0:T(8,128)(2,1)S(1)} %constant_dynamic-update-slice_fusion.refs_0_), channel_id=1, source_target_pairs={{0,96},{32,0},{64,32},{96,64},{1,97},{33,1},{65,33},{97,65},{2,98}... | collective-permute-start | bytes 786440 | tf_op jit(solution)/shard_map/ppermute | solution.py:51
  7.0 6.4 %shard_map.119 = (bf16[512,1152]{1,0:T(8,128)(2,1)}, bf16[512,2048]{1,0:T(8,128)(2,1)}) custom-call(bf16[512,1152]{1,0:T(8,128)(2,1)} %bitcast.59, bf16[1152,2048]{1,0:T(8,128)(2,1)} %w_ref.1), custom_call_target="tpu_custom_call" | custom-call | flops 2415919104 | bytes 9437184 | tf_op jit(solution)/shard_map/pallas_call | solution.py:95
  14.9 3.1 %collective-permute-start.6 = (bf16[2,64,1024]{2,1,0:T(8,128)(2,1)S(1)}, bf16[2,64,1024]{2,1,0:T(8,128)(2,1)S(1)}, u32[]{:S(2)}, u32[]{:S(2)}) collective-permute-start(bf16[2,64,1024]{2,1,0:T(8,128)(2,1)S(1)} %collective-permute-done.2.refs_3_), channel_id=1, source_target_pairs={{0,16},{16,0},{1,17},{17,1},{2,18},{18,2},{3,19},{19,3},{4,20},{20... | collective-permute-start | bytes 786440 | tf_op jit(solution)/shard_map/ppermute | solution.py:47
  18.1 3.1 %collective-permute-done.refs_1_ = bf16[2,64,1024]{2,1,0:T(8,128)(2,1)S(1)} collective-permute-done((bf16[2,64,1024]{2,1,0:T(8,128)(2,1)S(1)}, bf16[2,64,1024]{2,1,0:T(8,128)(2,1)S(1)}, u32[]{:S(2)}, u32[]{:S(2)}) %collective-permute-start) | collective-permute-done | bytes 262176 | tf_op jit(solution)/shard_map/ppermute | solution.py:51
  23.9 7.3 %shard_map.120 = (bf16[256,1024]{1,0:T(8,128)(2,1)}, bf16[256,1024]{1,0:T(8,128)(2,1)}, f32[128,1,256]{2,1,0:T(1,128)}) custom-call(s32[4]{0:T(128)} %counts.3, s32[4]{0:T(128)} %groups.3, s32[4]{0:T(128)} %fusion.9.places, bf16[2,64,1024]{2,1,0:T(8,128)(2,1)} %copy-done.5, bf16[2,64,1024]{2,1,0:T(8,128)(2,1)} %copy-done.9, bf16[2,64,1024]{2,1,0:T(8,128)(2,1)} %copy-done.8, ...), custom_call_target="tpu_custom_call" | custom-call | flops 6442450944 | bytes 10485760 | tf_op jit(solution)/shard_map/pallas_call | solution.py:257
  32.0 8.1 %all-to-all-start = ((f32[128,1,256]{2,1,0:T(1,128)}), f32[128,1,256]{2,1,0:T(1,128)S(1)}, u32[]{:S(2)}, u32[]{:S(2)}) async-start(f32[128,1,256]{2,1,0:T(1,128)} %get-tuple-element.62), calls=%async_computation | async-start | bytes 262144 | tf_op jit(solution)/shard_map/all_to_all | solution.py:39
  40.1 4.4 %shard_map.123 = (f32[512,1024]{1,0:T(8,128)}, f32[512,1024]{1,0:T(8,128)}) custom-call(bf16[256,1024]{1,0:T(8,128)(2,1)} %get-tuple-element.68.q_ref, bf16[256,1024]{1,0:T(8,128)(2,1)} %get-tuple-element.69.d_ref, bf16[512,2048]{1,0:T(8,128)(2,1)} %get-tuple-element.54.refs_10_.pairs_ref), custom_call_target="tpu_custom_call" | custom-call | flops 2147483648 | bytes 8388608 | tf_op jit(solution)/shard_map/pallas_call | solution.py:317
  44.5 5.8 %all-to-all-done.in_ref = f32[128,1,256]{2,1,0:T(1,128)S(1)} async-done(((f32[128,1,256]{2,1,0:T(1,128)}), f32[128,1,256]{2,1,0:T(1,128)S(1)}, u32[]{:S(2)}, u32[]{:S(2)}) %all-to-all-start) | async-done | bytes 131104 | tf_op jit(solution)/shard_map/all_to_all | solution.py:39
  51.3 4.9 %all-to-all-start.1 = ((f32[128,1,256]{2,1,0:T(1,128)}), f32[128,1,256]{2,1,0:T(1,128)}, u32[]{:S(2)}, u32[]{:S(2)}) async-start(f32[128,1,256]{2,1,0:T(1,128)} %shard_map.121), calls=%async_computation.1 | async-start | bytes 262144 | tf_op jit(solution)/shard_map/all_to_all | solution.py:39
  56.3 3.3 %shard_map.122 = (bf16[512,1024]{1,0:T(8,128)(2,1)}, bf16[512,1024]{1,0:T(8,128)(2,1)}) custom-call(s32[8]{0:T(128)} %stack.35.owners, bf16[2,64,1024]{2,1,0:T(8,128)(2,1)} %copy-done.5, bf16[2,64,1024]{2,1,0:T(8,128)(2,1)} %copy-done.9, bf16[2,64,1024]{2,1,0:T(8,128)(2,1)} %copy-done.8, bf16[2,64,1024]{2,1,0:T(8,128)(2,1)} %copy-done.7, ...), custom_call_target="tpu_custom_call" | custom-call | flops 4194304 | bytes 4194304 | tf_op jit(solution)/shard_map/pallas_call | solution.py:492
  61.1 5.3 %all-to-all-done.1.reply_ref = f32[128,1,256]{2,1,0:T(1,128)} async-done(((f32[128,1,256]{2,1,0:T(1,128)}), f32[128,1,256]{2,1,0:T(1,128)}, u32[]{:S(2)}, u32[]{:S(2)}) %all-to-all-start.1) | async-done | bytes 131104 | tf_op jit(solution)/shard_map/all_to_all | solution.py:39
  66.3 6.8 %shard_map.124 = (bf16[512,1024]{1,0:T(8,128)(2,1)}, bf16[512,1024]{1,0:T(8,128)(2,1)}, bf16[16,3,64,128]{3,2,1,0:T(8,128)(2,1)}) custom-call(s32[4]{0:T(128)} %counts.3, s32[4]{0:T(128)} %groups.3, s32[1]{0:T(128)} %bitcast.10.core, bf16[256,1024]{1,0:T(8,128)(2,1)} %get-tuple-element.68.q_ref, bf16[256,1024]{1,0:T(8,128)(2,1)} %get-tuple-element.69.d_ref, ...), custom_call_target="tpu_custom_call" | custom-call | flops 8589934592 | bytes 8388608 | tf_op jit(solution)/shard_map/pallas_call | solution.py:455
  73.6 3.6 %all-to-all-start.2 = ((bf16[16,3,64,128]{3,2,1,0:T(8,128)(2,1)}), bf16[16,3,64,128]{3,2,1,0:T(8,128)(2,1)S(1)}, u32[]{:S(2)}, u32[]{:S(2)}) async-start(bf16[16,3,64,128]{3,2,1,0:T(8,128)(2,1)} %get-tuple-element.80), calls=%async_computation.2 | async-start | bytes 1572864 | tf_op jit(solution)/shard_map/all_to_all | solution.py:39
  77.3 4.2 %fusion.3 = bf16[144,8,8,128]{3,1,2,0:T(8,128)(2,1)S(1)} fusion(bf16[1024,1152]{1,0:T(8,128)(2,1)S(1)} %pad_maximum_fusion, bf16[512,1024]{1,0:T(8,128)(2,1)} %collective-permute-done.8, bf16[512,1024]{1,0:T(8,128)(2,1)} %get-tuple-element.76), kind=kOutput, calls=%fused_computation.5 | convolution fusion | flops 2421293056 | bytes 6815744 | tf_op jit(solution)/shard_map/dot_general | solution.py:620
  83.3 2.8 %collective-permute-start.10 = (bf16[8,36,8,128]{3,2,1,0:T(8,128)(2,1)}, bf16[8,36,8,128]{3,2,1,0:T(8,128)(2,1)S(1)}, u32[]{:S(2)}, u32[]{:S(2)}) collective-permute-start(bf16[8,36,8,128]{3,2,1,0:T(8,128)(2,1)} %get-tuple-element.85), channel_id=1, source_target_pairs={{0,8},{4,12},{8,0},{12,4},{1,9},{5,13},{9,1},{13,5},{2,10},{6,14},... | collective-permute-start | bytes 1769480 | tf_op jit(solution)/shard_map/ppermute | solution.py:51
  87.6 4.5 %all-to-all-done.2 = bf16[16,3,64,128]{3,2,1,0:T(8,128)(2,1)S(1)} async-done(((bf16[16,3,64,128]{3,2,1,0:T(8,128)(2,1)}), bf16[16,3,64,128]{3,2,1,0:T(8,128)(2,1)S(1)}, u32[]{:S(2)}, u32[]{:S(2)}) %all-to-all-start.2) | async-done | bytes 786464 | tf_op jit(solution)/shard_map/all_to_all | solution.py:39
  92.7 10.5 %all_to_all.35 = f32[8,64,128]{2,1,0:T(8,128)S(1)} all-to-all(f32[8,64,128]{2,1,0:T(8,128)S(1)} %copy.17), channel_id=1, replica_groups=mesh['x'=4,'core'=2,'z'=4,'y'=4] {'x','core'}, dimensions={0} | all-to-all | bytes 524288 | tf_op jit(solution)/shard_map/all_to_all | solution.py:39
  103.3 9.1 %all_to_all.36 = bf16[8,64,128]{2,1,0:T(8,128)(2,1)} all-to-all(bf16[8,64,128]{2,1,0:T(8,128)(2,1)S(1)} %broadcast_in_dim.20), channel_id=1, replica_groups=mesh['x'=4,'core'=2,'z'=4,'y'=4] {'x','core'}, dimensions={0} | all-to-all | bytes 262144 | tf_op jit(solution)/shard_map/all_to_all | solution.py:39
  112.4 3.1 %shard_map.125 = (f32[64,1024]{1,0:T(8,128)}, bf16[16,96,128]{2,1,0:T(8,128)(2,1)}) custom-call(bf16[512,128]{1,0:T(8,128)(2,1)} %bitcast.53, bf16[64,128]{1,0:T(8,128)(2,1)} %copy-done.14, bf16[512,1024]{1,0:T(8,128)(2,1)} %get-tuple-element.81.latents_ref, bf16[512,1024]{1,0:T(8,128)(2,1)} %get-tuple-element.82.d_out_ref), custom_call_target="tpu_custom_call" | custom-call | flops 536870912 | bytes 4194304 | tf_op jit(solution)/shard_map/pallas_call | solution.py:524
  116.3 4.3 %all-to-all-start.5 = ((bf16[16,96,128]{2,1,0:T(8,128)(2,1)}), bf16[16,96,128]{2,1,0:T(8,128)(2,1)S(1)}, u32[]{:S(2)}, u32[]{:S(2)}) async-start(bf16[16,96,128]{2,1,0:T(8,128)(2,1)} %get-tuple-element.90), calls=%async_computation.5 | async-start | bytes 786432 | tf_op jit(solution)/shard_map/all_to_all | solution.py:39
  120.6 2.7 %add_convert_fusion = bf16[8,36,8,128]{3,2,1,0:T(8,128)(2,1)} fusion(bf16[8,36,8,128]{3,2,1,0:T(8,128)(2,1)} %collective-permute-done.11, bf16[8,36,8,128]{3,2,1,0:T(8,128)(2,1)} %copy-done.6, bf16[8,36,8,128]{3,2,1,0:T(8,128)(2,1)} %collective-permute-done.9, bf16[8,36,8,128]{3,2,1,0:T(8,128)(2,1)S(1)} %get-tuple-element.78), kind=kLoop, calls=%fused_computation.7 | loop fusion | flops 2359296 | bytes 2949120 | tf_op jit(solution)/shard_map/convert_element_type | solution.py:636
  123.4 6.6 %all-to-all-done.5.in_ref = bf16[16,96,128]{2,1,0:T(8,128)(2,1)S(1)} async-done(((bf16[16,96,128]{2,1,0:T(8,128)(2,1)}), bf16[16,96,128]{2,1,0:T(8,128)(2,1)S(1)}, u32[]{:S(2)}, u32[]{:S(2)}) %all-to-all-start.5) | async-done | bytes 393248 | tf_op jit(solution)/shard_map/all_to_all | solution.py:39
  130.0 5.2 %all-to-all-start.6 = ((bf16[32,9,8,128]{3,2,1,0:T(8,128)(2,1)}), bf16[32,9,8,128]{3,2,1,0:T(8,128)(2,1)S(1)}, u32[]{:S(2)}, u32[]{:S(2)}) async-start(bf16[32,9,8,128]{3,2,1,0:T(8,128)(2,1)} %bitcast.52), calls=%async_computation.6 | async-start | bytes 1179648 | tf_op jit(solution)/shard_map/all_to_all | solution.py:39
  139.0 7.8 %all-to-all-done.6 = bf16[32,9,8,128]{3,2,1,0:T(8,128)(2,1)S(1)} async-done(((bf16[32,9,8,128]{3,2,1,0:T(8,128)(2,1)}), bf16[32,9,8,128]{3,2,1,0:T(8,128)(2,1)S(1)}, u32[]{:S(2)}, u32[]{:S(2)}) %all-to-all-start.6) | async-done | bytes 589856 | tf_op jit(solution)/shard_map/all_to_all | solution.py:39
  (75 shorter events, 20.6 us)
Async XLA Ops:
  2.5 11.0 %copy-start.5 = (bf16[2,64,1024]{2,1,0:T(8,128)(2,1)}, bf16[2,64,1024]{2,1,0:T(8,128)(2,1)S(1)}, u32[]{:S(2)}) copy-start(bf16[2,64,1024]{2,1,0:T(8,128)(2,1)S(1)} %constant_dynamic-update-slice_fusion.refs_0_) | copy-start | bytes 786436
  2.5 12.5 %collective-permute-start.2 = (bf16[2,64,1024]{2,1,0:T(8,128)(2,1)S(1)}, bf16[2,64,1024]{2,1,0:T(8,128)(2,1)S(1)}, u32[]{:S(2)}, u32[]{:S(2)}) collective-permute-start(bf16[2,64,1024]{2,1,0:T(8,128)(2,1)S(1)} %constant_dynamic-update-slice_fusion.refs_0_), channel_id=1, source_target_pairs={{0,96},{32,0},{64,32},{96,64},{1,97},{33,1},{65,33},{97,65},{2,98}... | collective-permute-start | bytes 786440 | tf_op jit(solution)/shard_map/ppermute | solution.py:51
  5.9 12.1 %collective-permute-start.1 = (bf16[2,64,1024]{2,1,0:T(8,128)(2,1)S(1)}, bf16[2,64,1024]{2,1,0:T(8,128)(2,1)S(1)}, u32[]{:S(2)}, u32[]{:S(2)}) collective-permute-start(bf16[2,64,1024]{2,1,0:T(8,128)(2,1)S(1)} %constant_dynamic-update-slice_fusion.refs_0_), channel_id=1, source_target_pairs={{0,64},{32,96},{64,0},{96,32},{1,65},{33,97},{65,1},{97,33},{2,66}... | collective-permute-start | bytes 786440 | tf_op jit(solution)/shard_map/ppermute | solution.py:51
  6.4 14.8 %collective-permute-start = (bf16[2,64,1024]{2,1,0:T(8,128)(2,1)S(1)}, bf16[2,64,1024]{2,1,0:T(8,128)(2,1)S(1)}, u32[]{:S(2)}, u32[]{:S(2)}) collective-permute-start(bf16[2,64,1024]{2,1,0:T(8,128)(2,1)S(1)} %constant_dynamic-update-slice_fusion.refs_0_), channel_id=1, source_target_pairs={{0,32},{32,64},{64,96},{96,0},{1,33},{33,65},{65,97},{97,1},{2,34}... | collective-permute-start | bytes 786440 | tf_op jit(solution)/shard_map/ppermute | solution.py:51
  7.0 14.7 %copy-start.15 = (s32[4]{0:T(128)S(1)}, s32[4]{0:T(128)}, u32[]{:S(2)}) copy-start(s32[4]{0:T(128)} %groups.3) | copy-start | bytes 52
  13.4 8.8 %collective-permute-start.3 = (bf16[2,64,1024]{2,1,0:T(8,128)(2,1)S(1)}, bf16[2,64,1024]{2,1,0:T(8,128)(2,1)S(1)}, u32[]{:S(2)}, u32[]{:S(2)}) collective-permute-start(bf16[2,64,1024]{2,1,0:T(8,128)(2,1)S(1)} %constant_dynamic-update-slice_fusion.refs_0_), channel_id=1, source_target_pairs={{0,16},{16,0},{1,17},{17,1},{2,18},{18,2},{3,19},{19,3},{4,20},{20... | collective-permute-start | bytes 786440 | tf_op jit(solution)/shard_map/ppermute | solution.py:47
  14.9 7.3 %collective-permute-start.6 = (bf16[2,64,1024]{2,1,0:T(8,128)(2,1)S(1)}, bf16[2,64,1024]{2,1,0:T(8,128)(2,1)S(1)}, u32[]{:S(2)}, u32[]{:S(2)}) collective-permute-start(bf16[2,64,1024]{2,1,0:T(8,128)(2,1)S(1)} %collective-permute-done.2.refs_3_), channel_id=1, source_target_pairs={{0,16},{16,0},{1,17},{17,1},{2,18},{18,2},{3,19},{19,3},{4,20},{20... | collective-permute-start | bytes 786440 | tf_op jit(solution)/shard_map/ppermute | solution.py:47
  18.0 4.3 %collective-permute-start.5 = (bf16[2,64,1024]{2,1,0:T(8,128)(2,1)S(1)}, bf16[2,64,1024]{2,1,0:T(8,128)(2,1)S(1)}, u32[]{:S(2)}, u32[]{:S(2)}) collective-permute-start(bf16[2,64,1024]{2,1,0:T(8,128)(2,1)S(1)} %collective-permute-done.1.refs_2_), channel_id=1, source_target_pairs={{0,16},{16,0},{1,17},{17,1},{2,18},{18,2},{3,19},{19,3},{4,20},{20... | collective-permute-start | bytes 786440 | tf_op jit(solution)/shard_map/ppermute | solution.py:47
  21.2 1.7 %collective-permute-start.4 = (bf16[2,64,1024]{2,1,0:T(8,128)(2,1)S(1)}, bf16[2,64,1024]{2,1,0:T(8,128)(2,1)S(1)}, u32[]{:S(2)}, u32[]{:S(2)}) collective-permute-start(bf16[2,64,1024]{2,1,0:T(8,128)(2,1)S(1)} %collective-permute-done.refs_1_), channel_id=1, source_target_pairs={{0,16},{16,0},{1,17},{17,1},{2,18},{18,2},{3,19},{19,3},{4,20},{20... | collective-permute-start | bytes 786440 | tf_op jit(solution)/shard_map/ppermute | solution.py:47
  22.2 8.9 %copy-start.4 = (bf16[512,1152]{1,0:T(8,128)(2,1)S(1)}, bf16[512,1152]{1,0:T(8,128)(2,1)}, u32[]{:S(2)}) copy-start(bf16[512,1152]{1,0:T(8,128)(2,1)} %get-tuple-element.67) | copy-start | bytes 3538948
  31.1 28.4 %collective-permute-start.7 = (bf16[512,1152]{1,0:T(8,128)(2,1)S(1)}, bf16[512,1152]{1,0:T(8,128)(2,1)}, u32[]{:S(2)}, u32[]{:S(2)}) collective-permute-start(bf16[512,1152]{1,0:T(8,128)(2,1)S(1)} %copy-done.4), channel_id=1, source_target_pairs={{0,16},{16,0},{1,17},{17,1},{2,18},{18,2},{3,19},{19,3},{4,20},{20... | collective-permute-start | bytes 3538952 | tf_op jit(solution)/shard_map/ppermute | solution.py:47
  32.0 18.4 %all-to-all-start = ((f32[128,1,256]{2,1,0:T(1,128)}), f32[128,1,256]{2,1,0:T(1,128)S(1)}, u32[]{:S(2)}, u32[]{:S(2)}) async-start(f32[128,1,256]{2,1,0:T(1,128)} %get-tuple-element.62), calls=%async_computation | async-start | bytes 262144 | tf_op jit(solution)/shard_map/all_to_all | solution.py:39
  51.3 15.1 %all-to-all-start.1 = ((f32[128,1,256]{2,1,0:T(1,128)}), f32[128,1,256]{2,1,0:T(1,128)}, u32[]{:S(2)}, u32[]{:S(2)}) async-start(f32[128,1,256]{2,1,0:T(1,128)} %shard_map.121), calls=%async_computation.1 | async-start | bytes 262144 | tf_op jit(solution)/shard_map/all_to_all | solution.py:39
  73.1 4.2 %collective-permute-start.8 = (bf16[512,1024]{1,0:T(8,128)(2,1)}, bf16[512,1024]{1,0:T(8,128)(2,1)}, u32[]{:S(2)}, u32[]{:S(2)}) collective-permute-start(bf16[512,1024]{1,0:T(8,128)(2,1)} %get-tuple-element.77), channel_id=1, source_target_pairs={{0,16},{16,0},{1,17},{17,1},{2,18},{18,2},{3,19},{19,3},{4,20},{20... | collective-permute-start | bytes 3145736 | tf_op jit(solution)/shard_map/ppermute | solution.py:47
  73.6 18.5 %all-to-all-start.2 = ((bf16[16,3,64,128]{3,2,1,0:T(8,128)(2,1)}), bf16[16,3,64,128]{3,2,1,0:T(8,128)(2,1)S(1)}, u32[]{:S(2)}, u32[]{:S(2)}) async-start(bf16[16,3,64,128]{3,2,1,0:T(8,128)(2,1)} %get-tuple-element.80), calls=%async_computation.2 | async-start | bytes 1572864 | tf_op jit(solution)/shard_map/all_to_all | solution.py:39
  83.3 32.1 %collective-permute-start.10 = (bf16[8,36,8,128]{3,2,1,0:T(8,128)(2,1)}, bf16[8,36,8,128]{3,2,1,0:T(8,128)(2,1)S(1)}, u32[]{:S(2)}, u32[]{:S(2)}) collective-permute-start(bf16[8,36,8,128]{3,2,1,0:T(8,128)(2,1)} %get-tuple-element.85), channel_id=1, source_target_pairs={{0,8},{4,12},{8,0},{12,4},{1,9},{5,13},{9,1},{13,5},{2,10},{6,14},... | collective-permute-start | bytes 1769480 | tf_op jit(solution)/shard_map/ppermute | solution.py:51
  86.1 29.3 %collective-permute-start.11 = (bf16[8,36,8,128]{3,2,1,0:T(8,128)(2,1)}, bf16[8,36,8,128]{3,2,1,0:T(8,128)(2,1)}, u32[]{:S(2)}, u32[]{:S(2)}) collective-permute-start(bf16[8,36,8,128]{3,2,1,0:T(8,128)(2,1)} %get-tuple-element.86), channel_id=1, source_target_pairs={{0,12},{4,0},{8,4},{12,8},{1,13},{5,1},{9,5},{13,9},{2,14},{6,2},{... | collective-permute-start | bytes 1769480 | tf_op jit(solution)/shard_map/ppermute | solution.py:51
  87.0 28.8 %collective-permute-start.9 = (bf16[8,36,8,128]{3,2,1,0:T(8,128)(2,1)S(1)}, bf16[8,36,8,128]{3,2,1,0:T(8,128)(2,1)}, u32[]{:S(2)}, u32[]{:S(2)}) collective-permute-start(bf16[8,36,8,128]{3,2,1,0:T(8,128)(2,1)S(1)} %get-tuple-element.84), channel_id=1, source_target_pairs={{0,4},{4,8},{8,12},{12,0},{1,5},{5,9},{9,13},{13,1},{2,6},{6,10},{... | collective-permute-start | bytes 1769480 | tf_op jit(solution)/shard_map/ppermute | solution.py:51
  103.2 9.1 %copy-start.14 = (bf16[64,128]{1,0:T(8,128)(2,1)}, bf16[64,128]{1,0:T(8,128)(2,1)S(1)}, u32[]{:S(2)}) copy-start(bf16[64,128]{1,0:T(8,128)(2,1)S(1)} %reduce_sum.18.owned_ref) | copy-start | bytes 49156
  116.3 13.8 %all-to-all-start.5 = ((bf16[16,96,128]{2,1,0:T(8,128)(2,1)}), bf16[16,96,128]{2,1,0:T(8,128)(2,1)S(1)}, u32[]{:S(2)}, u32[]{:S(2)}) async-start(bf16[16,96,128]{2,1,0:T(8,128)(2,1)} %get-tuple-element.90), calls=%async_computation.5 | async-start | bytes 786432 | tf_op jit(solution)/shard_map/all_to_all | solution.py:39
  120.6 14.6 %copy-start = (bf16[1024,1024]{1,0:T(8,128)(2,1)S(1)}, bf16[1024,1024]{1,0:T(8,128)(2,1)}, u32[]{:S(2)}) copy-start(bf16[1024,1024]{1,0:T(8,128)(2,1)} %w_query_ref.1) | copy-start | bytes 6291460
  120.6 14.6 %copy-start.2 = (bf16[1,64,1024]{2,1,0:T(8,128)(2,1)S(1)}, bf16[1,64,1024]{2,1,0:T(8,128)(2,1)}, u32[]{:S(2)}) copy-start(bf16[1,64,1024]{2,1,0:T(8,128)(2,1)} %param.8) | copy-start | bytes 393220
  120.6 14.6 %copy-start.3 = (bf16[1,64,1024]{2,1,0:T(8,128)(2,1)S(1)}, bf16[1,64,1024]{2,1,0:T(8,128)(2,1)}, u32[]{:S(2)}) copy-start(bf16[1,64,1024]{2,1,0:T(8,128)(2,1)} %param.15) | copy-start | bytes 393220
  130.0 16.9 %all-to-all-start.6 = ((bf16[32,9,8,128]{3,2,1,0:T(8,128)(2,1)}), bf16[32,9,8,128]{3,2,1,0:T(8,128)(2,1)S(1)}, u32[]{:S(2)}, u32[]{:S(2)}) async-start(bf16[32,9,8,128]{3,2,1,0:T(8,128)(2,1)} %bitcast.52), calls=%async_computation.6 | async-start | bytes 1179648 | tf_op jit(solution)/shard_map/all_to_all | solution.py:39
  (9 other events, 20.0 us)

commit v6 on v5

--- a/solution.py
+++ b/solution.py
@@ -87,6 +87,21 @@
         normed_ref[...] = normalize(frames_ref[...])
 
     out_ref[...] = jnp.dot(normed_ref[...], w_ref[...], preferred_element_type=f32).astype(bf16)
+
+
+def pair_up_kernel(first_ref, second_ref, out_ref):
+    out_ref[0:1] = first_ref[...]
+    out_ref[1:2] = second_ref[...]
+
+
+def pair_up(first, second):
+    return pl.pallas_call(
+        pair_up_kernel,
+        out_shape=jax.ShapeDtypeStruct((2,) + first.shape[1:], first.dtype),
+        in_specs=[VMEM, VMEM],
+        out_specs=VMEM,
+        cost_estimate=pl.CostEstimate(flops=0, bytes_accessed=512 * 1024, transcendentals=0),
+    )(first, second)
 
 
 def project_pairs(frames, w_kv):
@@ -587,14 +602,16 @@
     core = lax.axis_index("core")
     batch_at = lax.axis_index(BATCH)
 
-    near = along_chips(jnp.concatenate([latents, d_out], axis=0))
+    near = along_chips(pair_up(latents, d_out))
     normed, pairs = project_pairs(frames.reshape(rows, feature), w_kv)
+    sources = jnp.stack([group_at(j) for j in range(8)])
+    places = place_of(groups)
     near = [lax.optimization_barrier((piece, normed, pairs))[0] for piece in near]
+    near[0], sources, places = lax.optimization_barrier((near[0], sources, places))
     pieces = near + [other_core(piece) for piece in near]
     queries, d_mixed, stats = attend(
-        counts, groups, place_of(groups), pieces, w_query, w_out, pairs
-    )
-    sources = jnp.stack([group_at(j) for j in range(8)])
+        counts, groups, places, pieces, w_query, w_out, pairs
+    )
     normed, stats, queries, d_mixed = lax.optimization_barrier((normed, stats, queries, d_mixed))
     scores, d_weights = products(queries, d_mixed, pairs)
     normed = jnp.concatenate([normed, other_core(normed)], axis=0)

time: 148 us -> 148 us (level)
  local copies, waits for them, and re-layouts: 7.72 us -> 5.59 us
  Pallas kernels: 34.3 us -> 35.9 us
    pallas_call x0 -> x1, Pallas kernels: none -> 1.69 us  [pair_up(): pl.pallas_call(pair_up_kernel, out_shape=jax.ShapeDtypeStruct((2,) + firs...]
    unnamed x39 -> x38, local copies, waits for them, and re-layouts: 4.74 us -> 3.53 us
where the time goes in v6:
time: 148 us; the launch traced here: 147 us
  starting transfers between devices  40.2 us (27%)
  Pallas kernels  35.9 us (24%)
  waiting for transfers between devices  34.6 us (23%)
  blocking collectives  19.5 us (13%)
  local copies, waits for them, and re-layouts  5.59 us (4%)
  other arithmetic  5.47 us (4%)
  matrix products  4.78 us (3%)
    all_to_all x5, waiting for transfers between devices, exchange(): return lax.all_to_all(values, axes, 0, 0, tiled=True)  30.1 us
    all_to_all x5, starting transfers between devices, exchange(): return lax.all_to_all(values, axes, 0, 0, tiled=True)  26.2 us
    all_to_all x2, blocking collectives, exchange(): return lax.all_to_all(values, axes, 0, 0, tiled=True)  19.5 us
    ppermute x6, starting transfers between devices, ring_step(): return lax.ppermute(values, axis, [(i, (i + step) % 4) for i in range(4)])  8.69 us
    pallas_call x1, Pallas kernels, attend(): pl.pallas_call(attend_kernel, out_shape=(small, small, jax.ShapeDtypeStru...  7.26 us
    pallas_call x1, Pallas kernels, gradients(): pl.pallas_call(grads_kernel, grid=(4 // PER_STEP,), out_shape=(jax.ShapeD...  6.75 us
    pallas_call x1, Pallas kernels, project_pairs(): pl.pallas_call(pairs_kernel, grid=(width // tile,), out_shape=(jax.ShapeD...  6.47 us
    ppermute x6, starting transfers between devices, other_core(): return lax.ppermute(values, 'core', [(0, 1), (1, 0)])  5.29 us
  transfers between devices with their start and end apart: 17, of which 8 were waited for; matrix products, arithmetic and copies ran while one was open for 8% of the time, Pallas kernels for 14%

profile of v6, /device:TPU:1, one launch (start us, length us, event | category | flops | bytes accessed | tf_op | source)
XLA Modules:
  0.0 147.1 jit_solution(14077824144370912849)
XLA Ops:
  2.3 3.3 %collective-permute-start.2 = (bf16[2,64,1024]{2,1,0:T(8,128)(2,1)}, bf16[2,64,1024]{2,1,0:T(8,128)(2,1)S(1)}, u32[]{:S(2)}, u32[]{:S(2)}) collective-permute-start(bf16[2,64,1024]{2,1,0:T(8,128)(2,1)} %shard_map.120.refs_0_), channel_id=1, source_target_pairs={{0,96},{32,0},{64,32},{96,64},{1,97},{33,1},{65,33},{97,65},{2,98}... | collective-permute-start | bytes 786440 | tf_op jit(solution)/shard_map/ppermute | solution.py:51
  6.8 6.5 %shard_map.119 = (bf16[512,1152]{1,0:T(8,128)(2,1)}, bf16[512,2048]{1,0:T(8,128)(2,1)}) custom-call(bf16[512,1152]{1,0:T(8,128)(2,1)} %bitcast.59, bf16[1152,2048]{1,0:T(8,128)(2,1)} %w_ref.1), custom_call_target="tpu_custom_call" | custom-call | flops 2415919104 | bytes 9437184 | tf_op jit(solution)/shard_map/pallas_call | solution.py:110
  15.9 2.2 %collective-permute-start.6 = (bf16[2,64,1024]{2,1,0:T(8,128)(2,1)S(1)}, bf16[2,64,1024]{2,1,0:T(8,128)(2,1)S(1)}, u32[]{:S(2)}, u32[]{:S(2)}) collective-permute-start(bf16[2,64,1024]{2,1,0:T(8,128)(2,1)S(1)} %collective-permute-done.2.refs_3_), channel_id=1, source_target_pairs={{0,16},{16,0},{1,17},{17,1},{2,18},{18,2},{3,19},{19,3},{4,20},{20... | collective-permute-start | bytes 786440 | tf_op jit(solution)/shard_map/ppermute | solution.py:47
  18.2 3.0 %collective-permute-done.refs_1_ = bf16[2,64,1024]{2,1,0:T(8,128)(2,1)S(1)} collective-permute-done((bf16[2,64,1024]{2,1,0:T(8,128)(2,1)}, bf16[2,64,1024]{2,1,0:T(8,128)(2,1)S(1)}, u32[]{:S(2)}, u32[]{:S(2)}) %collective-permute-start) | collective-permute-done | bytes 262176 | tf_op jit(solution)/shard_map/ppermute | solution.py:51
  23.6 7.3 %shard_map.121 = (bf16[256,1024]{1,0:T(8,128)(2,1)}, bf16[256,1024]{1,0:T(8,128)(2,1)}, f32[128,1,256]{2,1,0:T(1,128)}) custom-call(s32[4]{0:T(128)} %counts.3, s32[4]{0:T(128)} %groups.3, s32[4]{0:T(128)} %fusion.9.places, bf16[2,64,1024]{2,1,0:T(8,128)(2,1)} %shard_map.120.refs_0_, bf16[2,64,1024]{2,1,0:T(8,128)(2,1)} %copy-done.9, ...), custom_call_target="tpu_custom_call" | custom-call | flops 6442450944 | bytes 10485760 | tf_op jit(solution)/shard_map/pallas_call | solution.py:272
  31.3 8.1 %all-to-all-start = ((f32[128,1,256]{2,1,0:T(1,128)}), f32[128,1,256]{2,1,0:T(1,128)S(1)}, u32[]{:S(2)}, u32[]{:S(2)}) async-start(f32[128,1,256]{2,1,0:T(1,128)} %get-tuple-element.67), calls=%async_computation | async-start | bytes 262144 | tf_op jit(solution)/shard_map/all_to_all | solution.py:39
  39.5 4.4 %shard_map.124 = (f32[512,1024]{1,0:T(8,128)}, f32[512,1024]{1,0:T(8,128)}) custom-call(bf16[256,1024]{1,0:T(8,128)(2,1)} %get-tuple-element.74.q_ref, bf16[256,1024]{1,0:T(8,128)(2,1)} %get-tuple-element.75.d_ref, bf16[512,2048]{1,0:T(8,128)(2,1)} %get-tuple-element.57.refs_10_.pairs_ref), custom_call_target="tpu_custom_call" | custom-call | flops 2147483648 | bytes 8388608 | tf_op jit(solution)/shard_map/pallas_call | solution.py:332
  43.9 5.8 %all-to-all-done.in_ref = f32[128,1,256]{2,1,0:T(1,128)S(1)} async-done(((f32[128,1,256]{2,1,0:T(1,128)}), f32[128,1,256]{2,1,0:T(1,128)S(1)}, u32[]{:S(2)}, u32[]{:S(2)}) %all-to-all-start) | async-done | bytes 131104 | tf_op jit(solution)/shard_map/all_to_all | solution.py:39
  50.6 4.9 %all-to-all-start.1 = ((f32[128,1,256]{2,1,0:T(1,128)}), f32[128,1,256]{2,1,0:T(1,128)}, u32[]{:S(2)}, u32[]{:S(2)}) async-start(f32[128,1,256]{2,1,0:T(1,128)} %shard_map.122), calls=%async_computation.1 | async-start | bytes 262144 | tf_op jit(solution)/shard_map/all_to_all | solution.py:39
  55.7 3.2 %shard_map.123 = (bf16[512,1024]{1,0:T(8,128)(2,1)}, bf16[512,1024]{1,0:T(8,128)(2,1)}) custom-call(s32[8]{0:T(128)} %stack.35.owners, bf16[2,64,1024]{2,1,0:T(8,128)(2,1)} %shard_map.120.refs_0_, bf16[2,64,1024]{2,1,0:T(8,128)(2,1)} %copy-done.9, bf16[2,64,1024]{2,1,0:T(8,128)(2,1)} %copy-done.8, bf16[2,64,1024]{2,1,0:T(8,128)(2,1)} %copy-done.7, ...), custom_call_target="tpu_custom_call" | custom-call | flops 4194304 | bytes 4194304 | tf_op jit(solution)/shard_map/pallas_call | solution.py:507
  60.4 5.3 %all-to-all-done.1.reply_ref = f32[128,1,256]{2,1,0:T(1,128)} async-done(((f32[128,1,256]{2,1,0:T(1,128)}), f32[128,1,256]{2,1,0:T(1,128)}, u32[]{:S(2)}, u32[]{:S(2)}) %all-to-all-start.1) | async-done | bytes 131104 | tf_op jit(solution)/shard_map/all_to_all | solution.py:39
  65.7 6.8 %shard_map.125 = (bf16[512,1024]{1,0:T(8,128)(2,1)}, bf16[512,1024]{1,0:T(8,128)(2,1)}, bf16[16,3,64,128]{3,2,1,0:T(8,128)(2,1)}) custom-call(s32[4]{0:T(128)} %counts.3, s32[4]{0:T(128)} %groups.3, s32[1]{0:T(128)} %bitcast.10.core, bf16[256,1024]{1,0:T(8,128)(2,1)} %get-tuple-element.74.q_ref, bf16[256,1024]{1,0:T(8,128)(2,1)} %get-tuple-element.75.d_ref, ...), custom_call_target="tpu_custom_call" | custom-call | flops 8589934592 | bytes 8388608 | tf_op jit(solution)/shard_map/pallas_call | solution.py:470
  73.0 3.6 %all-to-all-start.2 = ((bf16[16,3,64,128]{3,2,1,0:T(8,128)(2,1)}), bf16[16,3,64,128]{3,2,1,0:T(8,128)(2,1)S(1)}, u32[]{:S(2)}, u32[]{:S(2)}) async-start(bf16[16,3,64,128]{3,2,1,0:T(8,128)(2,1)} %get-tuple-element.86), calls=%async_computation.2 | async-start | bytes 1572864 | tf_op jit(solution)/shard_map/all_to_all | solution.py:39
  76.6 4.2 %fusion.3 = bf16[144,8,8,128]{3,1,2,0:T(8,128)(2,1)S(1)} fusion(bf16[1024,1152]{1,0:T(8,128)(2,1)S(1)} %pad_maximum_fusion, bf16[512,1024]{1,0:T(8,128)(2,1)} %collective-permute-done.8, bf16[512,1024]{1,0:T(8,128)(2,1)} %get-tuple-element.82), kind=kOutput, calls=%fused_computation.5 | convolution fusion | flops 2421293056 | bytes 6815744 | tf_op jit(solution)/shard_map/dot_general | solution.py:637
  82.7 2.8 %collective-permute-start.10 = (bf16[8,36,8,128]{3,2,1,0:T(8,128)(2,1)}, bf16[8,36,8,128]{3,2,1,0:T(8,128)(2,1)S(1)}, u32[]{:S(2)}, u32[]{:S(2)}) collective-permute-start(bf16[8,36,8,128]{3,2,1,0:T(8,128)(2,1)} %get-tuple-element.91), channel_id=1, source_target_pairs={{0,8},{4,12},{8,0},{12,4},{1,9},{5,13},{9,1},{13,5},{2,10},{6,14},... | collective-permute-start | bytes 1769480 | tf_op jit(solution)/shard_map/ppermute | solution.py:51
  86.9 4.5 %all-to-all-done.2 = bf16[16,3,64,128]{3,2,1,0:T(8,128)(2,1)S(1)} async-done(((bf16[16,3,64,128]{3,2,1,0:T(8,128)(2,1)}), bf16[16,3,64,128]{3,2,1,0:T(8,128)(2,1)S(1)}, u32[]{:S(2)}, u32[]{:S(2)}) %all-to-all-start.2) | async-done | bytes 786464 | tf_op jit(solution)/shard_map/all_to_all | solution.py:39
  92.1 10.5 %all_to_all.35 = f32[8,64,128]{2,1,0:T(8,128)S(1)} all-to-all(f32[8,64,128]{2,1,0:T(8,128)S(1)} %copy.17), channel_id=1, replica_groups=mesh['x'=4,'core'=2,'z'=4,'y'=4] {'x','core'}, dimensions={0} | all-to-all | bytes 524288 | tf_op jit(solution)/shard_map/all_to_all | solution.py:39
  102.6 9.1 %all_to_all.36 = bf16[8,64,128]{2,1,0:T(8,128)(2,1)} all-to-all(bf16[8,64,128]{2,1,0:T(8,128)(2,1)S(1)} %broadcast_in_dim.20), channel_id=1, replica_groups=mesh['x'=4,'core'=2,'z'=4,'y'=4] {'x','core'}, dimensions={0} | all-to-all | bytes 262144 | tf_op jit(solution)/shard_map/all_to_all | solution.py:39
  111.7 3.1 %shard_map.126 = (f32[64,1024]{1,0:T(8,128)}, bf16[16,96,128]{2,1,0:T(8,128)(2,1)}) custom-call(bf16[512,128]{1,0:T(8,128)(2,1)} %bitcast.53, bf16[64,128]{1,0:T(8,128)(2,1)} %copy-done.14, bf16[512,1024]{1,0:T(8,128)(2,1)} %get-tuple-element.87.latents_ref, bf16[512,1024]{1,0:T(8,128)(2,1)} %get-tuple-element.88.d_out_ref), custom_call_target="tpu_custom_call" | custom-call | flops 536870912 | bytes 4194304 | tf_op jit(solution)/shard_map/pallas_call | solution.py:539
  115.6 4.4 %all-to-all-start.5 = ((bf16[16,96,128]{2,1,0:T(8,128)(2,1)}), bf16[16,96,128]{2,1,0:T(8,128)(2,1)S(1)}, u32[]{:S(2)}, u32[]{:S(2)}) async-start(bf16[16,96,128]{2,1,0:T(8,128)(2,1)} %get-tuple-element.96), calls=%async_computation.5 | async-start | bytes 786432 | tf_op jit(solution)/shard_map/all_to_all | solution.py:39
  120.0 2.7 %add_convert_fusion = bf16[8,36,8,128]{3,2,1,0:T(8,128)(2,1)} fusion(bf16[8,36,8,128]{3,2,1,0:T(8,128)(2,1)} %collective-permute-done.11, bf16[8,36,8,128]{3,2,1,0:T(8,128)(2,1)} %copy-done.6, bf16[8,36,8,128]{3,2,1,0:T(8,128)(2,1)} %collective-permute-done.9, bf16[8,36,8,128]{3,2,1,0:T(8,128)(2,1)S(1)} %get-tuple-element.84), kind=kLoop, calls=%fused_computation.7 | loop fusion | flops 2359296 | bytes 2949120 | tf_op jit(solution)/shard_map/convert_element_type | solution.py:653
  122.7 6.7 %all-to-all-done.5.in_ref = bf16[16,96,128]{2,1,0:T(8,128)(2,1)S(1)} async-done(((bf16[16,96,128]{2,1,0:T(8,128)(2,1)}), bf16[16,96,128]{2,1,0:T(8,128)(2,1)S(1)}, u32[]{:S(2)}, u32[]{:S(2)}) %all-to-all-start.5) | async-done | bytes 393248 | tf_op jit(solution)/shard_map/all_to_all | solution.py:39
  129.4 5.2 %all-to-all-start.6 = ((bf16[32,9,8,128]{3,2,1,0:T(8,128)(2,1)}), bf16[32,9,8,128]{3,2,1,0:T(8,128)(2,1)S(1)}, u32[]{:S(2)}, u32[]{:S(2)}) async-start(bf16[32,9,8,128]{3,2,1,0:T(8,128)(2,1)} %bitcast.52), calls=%async_computation.6 | async-start | bytes 1179648 | tf_op jit(solution)/shard_map/all_to_all | solution.py:39
  138.4 7.8 %all-to-all-done.6 = bf16[32,9,8,128]{3,2,1,0:T(8,128)(2,1)S(1)} async-done(((bf16[32,9,8,128]{3,2,1,0:T(8,128)(2,1)}), bf16[32,9,8,128]{3,2,1,0:T(8,128)(2,1)S(1)}, u32[]{:S(2)}, u32[]{:S(2)}) %all-to-all-start.6) | async-done | bytes 589856 | tf_op jit(solution)/shard_map/all_to_all | solution.py:39
  (74 shorter events, 20.9 us)
Async XLA Ops:
  2.3 13.6 %collective-permute-start.2 = (bf16[2,64,1024]{2,1,0:T(8,128)(2,1)}, bf16[2,64,1024]{2,1,0:T(8,128)(2,1)S(1)}, u32[]{:S(2)}, u32[]{:S(2)}) collective-permute-start(bf16[2,64,1024]{2,1,0:T(8,128)(2,1)} %shard_map.120.refs_0_), channel_id=1, source_target_pairs={{0,96},{32,0},{64,32},{96,64},{1,97},{33,1},{65,33},{97,65},{2,98}... | collective-permute-start | bytes 786440 | tf_op jit(solution)/shard_map/ppermute | solution.py:51
  5.6 12.5 %collective-permute-start.1 = (bf16[2,64,1024]{2,1,0:T(8,128)(2,1)}, bf16[2,64,1024]{2,1,0:T(8,128)(2,1)S(1)}, u32[]{:S(2)}, u32[]{:S(2)}) collective-permute-start(bf16[2,64,1024]{2,1,0:T(8,128)(2,1)} %shard_map.120.refs_0_), channel_id=1, source_target_pairs={{0,64},{32,96},{64,0},{96,32},{1,65},{33,97},{65,1},{97,33},{2,66}... | collective-permute-start | bytes 786440 | tf_op jit(solution)/shard_map/ppermute | solution.py:51
  6.1 15.0 %collective-permute-start = (bf16[2,64,1024]{2,1,0:T(8,128)(2,1)}, bf16[2,64,1024]{2,1,0:T(8,128)(2,1)S(1)}, u32[]{:S(2)}, u32[]{:S(2)}) collective-permute-start(bf16[2,64,1024]{2,1,0:T(8,128)(2,1)} %shard_map.120.refs_0_), channel_id=1, source_target_pairs={{0,32},{32,64},{64,96},{96,0},{1,33},{33,65},{65,97},{97,1},{2,34}... | collective-permute-start | bytes 786440 | tf_op jit(solution)/shard_map/ppermute | solution.py:51
  6.8 7.1 %copy-start.15 = (s32[4]{0:T(128)S(1)}, s32[4]{0:T(128)}, u32[]{:S(2)}) copy-start(s32[4]{0:T(128)} %groups.3) | copy-start | bytes 52
  6.8 7.6 %copy-start.5 = (bf16[2,64,1024]{2,1,0:T(8,128)(2,1)S(1)}, bf16[2,64,1024]{2,1,0:T(8,128)(2,1)}, u32[]{:S(2)}) copy-start(bf16[2,64,1024]{2,1,0:T(8,128)(2,1)} %shard_map.120.refs_0_) | copy-start | bytes 786436
  14.4 16.5 %copy-start.4 = (bf16[512,1152]{1,0:T(8,128)(2,1)S(1)}, bf16[512,1152]{1,0:T(8,128)(2,1)}, u32[]{:S(2)}) copy-start(bf16[512,1152]{1,0:T(8,128)(2,1)} %get-tuple-element.73) | copy-start | bytes 3538948
  14.4 7.3 %collective-permute-start.3 = (bf16[2,64,1024]{2,1,0:T(8,128)(2,1)S(1)}, bf16[2,64,1024]{2,1,0:T(8,128)(2,1)S(1)}, u32[]{:S(2)}, u32[]{:S(2)}) collective-permute-start(bf16[2,64,1024]{2,1,0:T(8,128)(2,1)S(1)} %copy-done.5), channel_id=1, source_target_pairs={{0,16},{16,0},{1,17},{17,1},{2,18},{18,2},{3,19},{19,3},{4,20},{20... | collective-permute-start | bytes 786440 | tf_op jit(solution)/shard_map/ppermute | solution.py:47
  15.9 5.8 %collective-permute-start.6 = (bf16[2,64,1024]{2,1,0:T(8,128)(2,1)S(1)}, bf16[2,64,1024]{2,1,0:T(8,128)(2,1)S(1)}, u32[]{:S(2)}, u32[]{:S(2)}) collective-permute-start(bf16[2,64,1024]{2,1,0:T(8,128)(2,1)S(1)} %collective-permute-done.2.refs_3_), channel_id=1, source_target_pairs={{0,16},{16,0},{1,17},{17,1},{2,18},{18,2},{3,19},{19,3},{4,20},{20... | collective-permute-start | bytes 786440 | tf_op jit(solution)/shard_map/ppermute | solution.py:47
  18.1 3.6 %collective-permute-start.5 = (bf16[2,64,1024]{2,1,0:T(8,128)(2,1)S(1)}, bf16[2,64,1024]{2,1,0:T(8,128)(2,1)S(1)}, u32[]{:S(2)}, u32[]{:S(2)}) collective-permute-start(bf16[2,64,1024]{2,1,0:T(8,128)(2,1)S(1)} %collective-permute-done.1.refs_2_), channel_id=1, source_target_pairs={{0,16},{16,0},{1,17},{17,1},{2,18},{18,2},{3,19},{19,3},{4,20},{20... | collective-permute-start | bytes 786440 | tf_op jit(solution)/shard_map/ppermute | solution.py:47
  21.2 1.7 %collective-permute-start.4 = (bf16[2,64,1024]{2,1,0:T(8,128)(2,1)S(1)}, bf16[2,64,1024]{2,1,0:T(8,128)(2,1)S(1)}, u32[]{:S(2)}, u32[]{:S(2)}) collective-permute-start(bf16[2,64,1024]{2,1,0:T(8,128)(2,1)S(1)} %collective-permute-done.refs_1_), channel_id=1, source_target_pairs={{0,16},{16,0},{1,17},{17,1},{2,18},{18,2},{3,19},{19,3},{4,20},{20... | collective-permute-start | bytes 786440 | tf_op jit(solution)/shard_map/ppermute | solution.py:47
  30.9 28.0 %collective-permute-start.7 = (bf16[512,1152]{1,0:T(8,128)(2,1)S(1)}, bf16[512,1152]{1,0:T(8,128)(2,1)}, u32[]{:S(2)}, u32[]{:S(2)}) collective-permute-start(bf16[512,1152]{1,0:T(8,128)(2,1)S(1)} %copy-done.4), channel_id=1, source_target_pairs={{0,16},{16,0},{1,17},{17,1},{2,18},{18,2},{3,19},{19,3},{4,20},{20... | collective-permute-start | bytes 3538952 | tf_op jit(solution)/shard_map/ppermute | solution.py:47
  31.3 18.4 %all-to-all-start = ((f32[128,1,256]{2,1,0:T(1,128)}), f32[128,1,256]{2,1,0:T(1,128)S(1)}, u32[]{:S(2)}, u32[]{:S(2)}) async-start(f32[128,1,256]{2,1,0:T(1,128)} %get-tuple-element.67), calls=%async_computation | async-start | bytes 262144 | tf_op jit(solution)/shard_map/all_to_all | solution.py:39
  50.6 15.1 %all-to-all-start.1 = ((f32[128,1,256]{2,1,0:T(1,128)}), f32[128,1,256]{2,1,0:T(1,128)}, u32[]{:S(2)}, u32[]{:S(2)}) async-start(f32[128,1,256]{2,1,0:T(1,128)} %shard_map.122), calls=%async_computation.1 | async-start | bytes 262144 | tf_op jit(solution)/shard_map/all_to_all | solution.py:39
  72.4 4.2 %collective-permute-start.8 = (bf16[512,1024]{1,0:T(8,128)(2,1)}, bf16[512,1024]{1,0:T(8,128)(2,1)}, u32[]{:S(2)}, u32[]{:S(2)}) collective-permute-start(bf16[512,1024]{1,0:T(8,128)(2,1)} %get-tuple-element.83), channel_id=1, source_target_pairs={{0,16},{16,0},{1,17},{17,1},{2,18},{18,2},{3,19},{19,3},{4,20},{20... | collective-permute-start | bytes 3145736 | tf_op jit(solution)/shard_map/ppermute | solution.py:47
  73.0 18.5 %all-to-all-start.2 = ((bf16[16,3,64,128]{3,2,1,0:T(8,128)(2,1)}), bf16[16,3,64,128]{3,2,1,0:T(8,128)(2,1)S(1)}, u32[]{:S(2)}, u32[]{:S(2)}) async-start(bf16[16,3,64,128]{3,2,1,0:T(8,128)(2,1)} %get-tuple-element.86), calls=%async_computation.2 | async-start | bytes 1572864 | tf_op jit(solution)/shard_map/all_to_all | solution.py:39
  82.7 32.1 %collective-permute-start.10 = (bf16[8,36,8,128]{3,2,1,0:T(8,128)(2,1)}, bf16[8,36,8,128]{3,2,1,0:T(8,128)(2,1)S(1)}, u32[]{:S(2)}, u32[]{:S(2)}) collective-permute-start(bf16[8,36,8,128]{3,2,1,0:T(8,128)(2,1)} %get-tuple-element.91), channel_id=1, source_target_pairs={{0,8},{4,12},{8,0},{12,4},{1,9},{5,13},{9,1},{13,5},{2,10},{6,14},... | collective-permute-start | bytes 1769480 | tf_op jit(solution)/shard_map/ppermute | solution.py:51
  85.5 29.3 %collective-permute-start.11 = (bf16[8,36,8,128]{3,2,1,0:T(8,128)(2,1)}, bf16[8,36,8,128]{3,2,1,0:T(8,128)(2,1)}, u32[]{:S(2)}, u32[]{:S(2)}) collective-permute-start(bf16[8,36,8,128]{3,2,1,0:T(8,128)(2,1)} %get-tuple-element.92), channel_id=1, source_target_pairs={{0,12},{4,0},{8,4},{12,8},{1,13},{5,1},{9,5},{13,9},{2,14},{6,2},{... | collective-permute-start | bytes 1769480 | tf_op jit(solution)/shard_map/ppermute | solution.py:51
  86.3 28.8 %collective-permute-start.9 = (bf16[8,36,8,128]{3,2,1,0:T(8,128)(2,1)S(1)}, bf16[8,36,8,128]{3,2,1,0:T(8,128)(2,1)}, u32[]{:S(2)}, u32[]{:S(2)}) collective-permute-start(bf16[8,36,8,128]{3,2,1,0:T(8,128)(2,1)S(1)} %get-tuple-element.90), channel_id=1, source_target_pairs={{0,4},{4,8},{8,12},{12,0},{1,5},{5,9},{9,13},{13,1},{2,6},{6,10},{... | collective-permute-start | bytes 1769480 | tf_op jit(solution)/shard_map/ppermute | solution.py:51
  102.6 9.1 %copy-start.14 = (bf16[64,128]{1,0:T(8,128)(2,1)}, bf16[64,128]{1,0:T(8,128)(2,1)S(1)}, u32[]{:S(2)}) copy-start(bf16[64,128]{1,0:T(8,128)(2,1)S(1)} %reduce_sum.18.owned_ref) | copy-start | bytes 49156
  115.6 13.8 %all-to-all-start.5 = ((bf16[16,96,128]{2,1,0:T(8,128)(2,1)}), bf16[16,96,128]{2,1,0:T(8,128)(2,1)S(1)}, u32[]{:S(2)}, u32[]{:S(2)}) async-start(bf16[16,96,128]{2,1,0:T(8,128)(2,1)} %get-tuple-element.96), calls=%async_computation.5 | async-start | bytes 786432 | tf_op jit(solution)/shard_map/all_to_all | solution.py:39
  120.0 14.6 %copy-start = (bf16[1024,1024]{1,0:T(8,128)(2,1)S(1)}, bf16[1024,1024]{1,0:T(8,128)(2,1)}, u32[]{:S(2)}) copy-start(bf16[1024,1024]{1,0:T(8,128)(2,1)} %w_query_ref.1) | copy-start | bytes 6291460
  120.0 14.6 %copy-start.2 = (bf16[1,64,1024]{2,1,0:T(8,128)(2,1)S(1)}, bf16[1,64,1024]{2,1,0:T(8,128)(2,1)}, u32[]{:S(2)}) copy-start(bf16[1,64,1024]{2,1,0:T(8,128)(2,1)} %first_ref.1) | copy-start | bytes 393220
  120.0 14.6 %copy-start.3 = (bf16[1,64,1024]{2,1,0:T(8,128)(2,1)S(1)}, bf16[1,64,1024]{2,1,0:T(8,128)(2,1)}, u32[]{:S(2)}) copy-start(bf16[1,64,1024]{2,1,0:T(8,128)(2,1)} %second_ref.1) | copy-start | bytes 393220
  129.4 16.9 %all-to-all-start.6 = ((bf16[32,9,8,128]{3,2,1,0:T(8,128)(2,1)}), bf16[32,9,8,128]{3,2,1,0:T(8,128)(2,1)S(1)}, u32[]{:S(2)}, u32[]{:S(2)}) async-start(bf16[32,9,8,128]{3,2,1,0:T(8,128)(2,1)} %bitcast.52), calls=%async_computation.6 | async-start | bytes 1179648 | tf_op jit(solution)/shard_map/all_to_all | solution.py:39
  (9 other events, 20.0 us)

commit v7 on v6

--- a/solution.py
+++ b/solution.py
@@ -515,13 +515,11 @@
     )(owners, *pieces)
 
 
-def owners_kernel(heads_ref, owned_ref, latents_ref, d_out_ref, outproj_ref, out_ref):
-    rows = outproj_ref.shape[0]
-    heads = heads_ref[...]
-    outproj_ref[...] = lax.dot_general(
-        heads, d_out_ref[...], FIRST, preferred_element_type=f32
-    )[:rows]
-    query = lax.dot_general(latents_ref[...], heads, FIRST, preferred_element_type=f32)
+def owners_kernel(heads_ref, owned_ref, latents_ref, out_ref):
+    rows = owned_ref.shape[0]
+    query = lax.dot_general(
+        latents_ref[...], heads_ref[...], FIRST, preferred_element_type=f32
+    )
     other = pltpu.roll(query, 64, 1)
     half = rows // 2
     left = low_lanes((half, 128))
@@ -533,21 +531,17 @@
         ).astype(bf16)
 
 
-def owners(heads, owned, normed_latents, d_outs):
+def owners(heads, owned, normed_latents):
     rows = owned.shape[0]
-    width = d_outs.shape[1]
     return pl.pallas_call(
         owners_kernel,
-        out_shape=(
-            jax.ShapeDtypeStruct((rows, width), f32),
-            jax.ShapeDtypeStruct((H, rows + rows // 2, 128), bf16),
-        ),
-        in_specs=[VMEM] * 4,
-        out_specs=(VMEM, VMEM),
+        out_shape=jax.ShapeDtypeStruct((H, rows + rows // 2, 128), bf16),
+        in_specs=[VMEM] * 3,
+        out_specs=VMEM,
         cost_estimate=pl.CostEstimate(
-            flops=512 * 1024 * 1024, bytes_accessed=4 * 1024 * 1024, transcendentals=0
-        ),
-    )(heads, owned, normed_latents, d_outs)
+            flops=256 * 1024 * 1024, bytes_accessed=2 * 1024 * 1024, transcendentals=0
+        ),
+    )(heads, owned, normed_latents)
 
 
 def finish_kernel(in_ref, latent_ref, d_out_ref, w_query_ref, w_out_in, *refs):
@@ -645,19 +639,23 @@
     parts = lax.optimization_barrier([z_part(step) for step in range(4)])
     got = [ring_step(parts[step], "z", step) for step in range(1, 4)]
     by_group = jnp.einsum("gsk,sklc->glc", chosen, slotted, preferred_element_type=f32)
-    owned = jnp.sum(exchange(by_group, BATCH), axis=0).astype(bf16)
+    by_group = exchange(by_group.astype(bf16), BATCH).astype(f32)
+    owned = jnp.sum(by_group, axis=0).astype(bf16)
     heads = share(owned, BATCH, group_count).reshape(group_count * latent_count, 128)
-    grad_outproj, owned_parts = owners(heads, owned, all_latents, all_d_out)
-    owned_parts, got = lax.optimization_barrier((owned_parts, got))
+    owned_parts = owners(heads, owned, all_latents)
+    owned_parts, got[1] = lax.optimization_barrier((owned_parts, got[1]))
     ring_sum = sum([part.astype(f32) for part in got], parts[0].astype(f32))
     ring_sum = ring_sum.astype(bf16).reshape(group_count, 4, share_rows, 8, 128)
     ring_sum = ring_sum.reshape(4 * group_count, share_rows, 8, 128)
     over_seq = exchange(owned_parts, SEQ)
     ring_sum, over_seq = lax.optimization_barrier((ring_sum, over_seq))
     ring_sum = exchange(ring_sum, BATCH + ("y",))
+    grad_outproj = lax.dot_general(
+        heads[:, :head_dim], all_d_out, FIRST, preferred_element_type=f32
+    )
     out, d_latents, grad_query = finish(over_seq, latents[0], d_out[0], w_query, w_out)
-    ring_sum, out, d_latents, grad_query = lax.optimization_barrier(
-        (ring_sum, out, d_latents, grad_query)
+    ring_sum, out, d_latents, grad_query, grad_outproj = lax.optimization_barrier(
+        (ring_sum, out, d_latents, grad_query, grad_outproj)
     )
     ring_sum = ring_sum.reshape(4, 2, 4, share_rows, 8, 128).astype(f32)
     halves = jnp.sum(ring_sum, axis=(0, 2)).reshape(2, share_rows, model_width)

time: 148 us -> 145 us (0.980)
  waiting for transfers between devices: 34.6 us -> 31.6 us
  matrix products: 4.78 us -> 7.02 us
    all_to_all x5, waiting for transfers between devices: 30.1 us -> 27.5 us  [exchange(): return lax.all_to_all(values, axes, 0, 0, tiled=True)]
    dot_general x0 -> x1, matrix products: none -> 2.25 us  [local(): lax.dot_general(heads[:, :head_dim], all_d_out, FIRST, preferred_element_...]
    unnamed x38 -> x40, local copies, waits for them, and re-layouts: 3.53 us -> 3.89 us
  transfers between devices with their start and end apart: 17 -> 17, of which waited for: 8 -> 7; matrix products, arithmetic and copies ran while one was open for 8% -> 10% of each run, Pallas kernels for 14% -> 14%
where the time goes in v7:
time: 145 us
  starting transfers between devices  39.5 us (27%)
  Pallas kernels  35.6 us (25%)
  waiting for transfers between devices  31.6 us (22%)
  blocking collectives  18.1 us (12%)
  matrix products  7.02 us (5%)
  local copies, waits for them, and re-layouts  6.04 us (4%)
  other arithmetic  5.64 us (4%)
    all_to_all x5, waiting for transfers between devices, exchange(): return lax.all_to_all(values, axes, 0, 0, tiled=True)  27.5 us
    all_to_all x5, starting transfers between devices, exchange(): return lax.all_to_all(values, axes, 0, 0, tiled=True)  25.5 us
    all_to_all x2, blocking collectives, exchange(): return lax.all_to_all(values, axes, 0, 0, tiled=True)  18.1 us
    ppermute x6, starting transfers between devices, ring_step(): return lax.ppermute(values, axis, [(i, (i + step) % 4) for i in range(4)])  8.7 us
    pallas_call x1, Pallas kernels, attend(): pl.pallas_call(attend_kernel, out_shape=(small, small, jax.ShapeDtypeStru...  7.26 us
    pallas_call x1, Pallas kernels, gradients(): pl.pallas_call(grads_kernel, grid=(4 // PER_STEP,), out_shape=(jax.ShapeD...  6.75 us
    pallas_call x1, Pallas kernels, project_pairs(): pl.pallas_call(pairs_kernel, grid=(width // tile,), out_shape=(jax.ShapeD...  6.51 us
    ppermute x6, starting transfers between devices, other_core(): return lax.ppermute(values, 'core', [(0, 1), (1, 0)])  5.3 us
  transfers between devices with their start and end apart: 17, of which 7 were waited for; matrix products, arithmetic and copies ran while one was open for 10% of the time, Pallas kernels for 14%

profile of v7, /device:TPU:1, one launch (start us, length us, event | category | flops | bytes accessed | tf_op | source)
XLA Modules:
  0.0 144.5 jit_solution(12151340038728397919)
XLA Ops:
  2.3 3.3 %collective-permute-start.2 = (bf16[2,64,1024]{2,1,0:T(8,128)(2,1)}, bf16[2,64,1024]{2,1,0:T(8,128)(2,1)S(1)}, u32[]{:S(2)}, u32[]{:S(2)}) collective-permute-start(bf16[2,64,1024]{2,1,0:T(8,128)(2,1)} %shard_map.120.refs_0_), channel_id=1, source_target_pairs={{0,96},{32,0},{64,32},{96,64},{1,97},{33,1},{65,33},{97,65},{2,98}... | collective-permute-start | bytes 786440 | tf_op jit(solution)/shard_map/ppermute | solution.py:51
  6.8 6.5 %shard_map.119 = (bf16[512,1152]{1,0:T(8,128)(2,1)}, bf16[512,2048]{1,0:T(8,128)(2,1)}) custom-call(bf16[512,1152]{1,0:T(8,128)(2,1)} %bitcast.63, bf16[1152,2048]{1,0:T(8,128)(2,1)} %w_ref.1), custom_call_target="tpu_custom_call" | custom-call | flops 2415919104 | bytes 9437184 | tf_op jit(solution)/shard_map/pallas_call | solution.py:110
  18.2 3.0 %collective-permute-done.refs_1_ = bf16[2,64,1024]{2,1,0:T(8,128)(2,1)S(1)} collective-permute-done((bf16[2,64,1024]{2,1,0:T(8,128)(2,1)}, bf16[2,64,1024]{2,1,0:T(8,128)(2,1)S(1)}, u32[]{:S(2)}, u32[]{:S(2)}) %collective-permute-start) | collective-permute-done | bytes 262176 | tf_op jit(solution)/shard_map/ppermute | solution.py:51
  23.6 7.3 %shard_map.121 = (bf16[256,1024]{1,0:T(8,128)(2,1)}, bf16[256,1024]{1,0:T(8,128)(2,1)}, f32[128,1,256]{2,1,0:T(1,128)}) custom-call(s32[4]{0:T(128)} %counts.3, s32[4]{0:T(128)} %groups.3, s32[4]{0:T(128)} %fusion.12.places, bf16[2,64,1024]{2,1,0:T(8,128)(2,1)} %shard_map.120.refs_0_, bf16[2,64,1024]{2,1,0:T(8,128)(2,1)} %copy-done.10, ...), custom_call_target="tpu_custom_call" | custom-call | flops 6442450944 | bytes 10485760 | tf_op jit(solution)/shard_map/pallas_call | solution.py:272
  31.3 8.1 %all-to-all-start = ((f32[128,1,256]{2,1,0:T(1,128)}), f32[128,1,256]{2,1,0:T(1,128)S(1)}, u32[]{:S(2)}, u32[]{:S(2)}) async-start(f32[128,1,256]{2,1,0:T(1,128)} %get-tuple-element.64), calls=%async_computation | async-start | bytes 262144 | tf_op jit(solution)/shard_map/all_to_all | solution.py:39
  39.5 4.4 %shard_map.124 = (f32[512,1024]{1,0:T(8,128)}, f32[512,1024]{1,0:T(8,128)}) custom-call(bf16[256,1024]{1,0:T(8,128)(2,1)} %get-tuple-element.71.q_ref, bf16[256,1024]{1,0:T(8,128)(2,1)} %get-tuple-element.72.d_ref, bf16[512,2048]{1,0:T(8,128)(2,1)} %get-tuple-element.54.refs_10_.pairs_ref), custom_call_target="tpu_custom_call" | custom-call | flops 2147483648 | bytes 8388608 | tf_op jit(solution)/shard_map/pallas_call | solution.py:332
  43.9 5.8 %all-to-all-done.in_ref = f32[128,1,256]{2,1,0:T(1,128)S(1)} async-done(((f32[128,1,256]{2,1,0:T(1,128)}), f32[128,1,256]{2,1,0:T(1,128)S(1)}, u32[]{:S(2)}, u32[]{:S(2)}) %all-to-all-start) | async-done | bytes 131104 | tf_op jit(solution)/shard_map/all_to_all | solution.py:39
  50.6 4.9 %all-to-all-start.1 = ((f32[128,1,256]{2,1,0:T(1,128)}), f32[128,1,256]{2,1,0:T(1,128)}, u32[]{:S(2)}, u32[]{:S(2)}) async-start(f32[128,1,256]{2,1,0:T(1,128)} %shard_map.122), calls=%async_computation.1 | async-start | bytes 262144 | tf_op jit(solution)/shard_map/all_to_all | solution.py:39
  55.7 3.3 %shard_map.123 = (bf16[512,1024]{1,0:T(8,128)(2,1)}, bf16[512,1024]{1,0:T(8,128)(2,1)}) custom-call(s32[8]{0:T(128)} %stack.35.owners, bf16[2,64,1024]{2,1,0:T(8,128)(2,1)} %shard_map.120.refs_0_, bf16[2,64,1024]{2,1,0:T(8,128)(2,1)} %copy-done.10, bf16[2,64,1024]{2,1,0:T(8,128)(2,1)} %copy-done.9, bf16[2,64,1024]{2,1,0:T(8,128)(2,1)} %copy-done.8, ...), custom_call_target="tpu_custom_call" | custom-call | flops 4194304 | bytes 4194304 | tf_op jit(solution)/shard_map/pallas_call | solution.py:507
  60.5 5.4 %all-to-all-done.1.reply_ref = f32[128,1,256]{2,1,0:T(1,128)} async-done(((f32[128,1,256]{2,1,0:T(1,128)}), f32[128,1,256]{2,1,0:T(1,128)}, u32[]{:S(2)}, u32[]{:S(2)}) %all-to-all-start.1) | async-done | bytes 131104 | tf_op jit(solution)/shard_map/all_to_all | solution.py:39
  65.8 6.8 %shard_map.125 = (bf16[512,1024]{1,0:T(8,128)(2,1)}, bf16[512,1024]{1,0:T(8,128)(2,1)}, bf16[16,3,64,128]{3,2,1,0:T(8,128)(2,1)}) custom-call(s32[4]{0:T(128)} %counts.3, s32[4]{0:T(128)} %groups.3, s32[1]{0:T(128)} %bitcast.10.core, bf16[256,1024]{1,0:T(8,128)(2,1)} %get-tuple-element.71.q_ref, bf16[256,1024]{1,0:T(8,128)(2,1)} %get-tuple-element.72.d_ref, ...), custom_call_target="tpu_custom_call" | custom-call | flops 8589934592 | bytes 8388608 | tf_op jit(solution)/shard_map/pallas_call | solution.py:470
  73.2 3.6 %all-to-all-start.2 = ((bf16[16,3,64,128]{3,2,1,0:T(8,128)(2,1)}), bf16[16,3,64,128]{3,2,1,0:T(8,128)(2,1)S(1)}, u32[]{:S(2)}, u32[]{:S(2)}) async-start(bf16[16,3,64,128]{3,2,1,0:T(8,128)(2,1)} %get-tuple-element.84), calls=%async_computation.2 | async-start | bytes 1572864 | tf_op jit(solution)/shard_map/all_to_all | solution.py:39
  76.8 4.2 %fusion.3 = bf16[144,8,8,128]{3,1,2,0:T(8,128)(2,1)S(1)} fusion(bf16[1024,1152]{1,0:T(8,128)(2,1)S(1)} %pad_maximum_fusion, bf16[512,1024]{1,0:T(8,128)(2,1)} %collective-permute-done.8, bf16[512,1024]{1,0:T(8,128)(2,1)} %get-tuple-element.79), kind=kOutput, calls=%fused_computation.5 | convolution fusion | flops 2421293056 | bytes 6815744 | tf_op jit(solution)/shard_map/dot_general | solution.py:631
  83.0 2.8 %collective-permute-start.10 = (bf16[8,36,8,128]{3,2,1,0:T(8,128)(2,1)S(1)}, bf16[8,36,8,128]{3,2,1,0:T(8,128)(2,1)S(1)}, u32[]{:S(2)}, u32[]{:S(2)}) collective-permute-start(bf16[8,36,8,128]{3,2,1,0:T(8,128)(2,1)S(1)} %get-tuple-element.86), channel_id=1, source_target_pairs={{0,8},{4,12},{8,0},{12,4},{1,9},{5,13},{9,1},{13,5},{2,10},{6,14},... | collective-permute-start | bytes 1769480 | tf_op jit(solution)/shard_map/ppermute | solution.py:51
  87.2 4.4 %all-to-all-done.2 = bf16[16,3,64,128]{3,2,1,0:T(8,128)(2,1)S(1)} async-done(((bf16[16,3,64,128]{3,2,1,0:T(8,128)(2,1)}), bf16[16,3,64,128]{3,2,1,0:T(8,128)(2,1)S(1)}, u32[]{:S(2)}, u32[]{:S(2)}) %all-to-all-start.2) | async-done | bytes 786464 | tf_op jit(solution)/shard_map/all_to_all | solution.py:39
  92.3 9.2 %all_to_all.35 = bf16[8,64,128]{2,1,0:T(8,128)(2,1)S(1)} all-to-all(bf16[8,64,128]{2,1,0:T(8,128)(2,1)S(1)} %copy.17), channel_id=1, replica_groups=mesh['x'=4,'core'=2,'z'=4,'y'=4] {'x','core'}, dimensions={0} | all-to-all | bytes 262144 | tf_op jit(solution)/shard_map/all_to_all | solution.py:39
  101.5 8.9 %all_to_all.36 = bf16[8,64,128]{2,1,0:T(8,128)(2,1)} all-to-all(bf16[8,64,128]{2,1,0:T(8,128)(2,1)S(1)} %broadcast_in_dim.20), channel_id=1, replica_groups=mesh['x'=4,'core'=2,'z'=4,'y'=4] {'x','core'}, dimensions={0} | all-to-all | bytes 262144 | tf_op jit(solution)/shard_map/all_to_all | solution.py:39
  110.4 2.6 %shard_map.126 = bf16[16,96,128]{2,1,0:T(8,128)(2,1)} custom-call(bf16[512,128]{1,0:T(8,128)(2,1)} %bitcast.56, bf16[64,128]{1,0:T(8,128)(2,1)} %copy-done.15, bf16[512,1024]{1,0:T(8,128)(2,1)} %get-tuple-element.85.latents_ref), custom_call_target="tpu_custom_call" | custom-call | flops 268435456 | bytes 2097152 | tf_op jit(solution)/shard_map/pallas_call | solution.py:536
  113.9 3.6 %all-to-all-start.5 = ((bf16[16,96,128]{2,1,0:T(8,128)(2,1)}), bf16[16,96,128]{2,1,0:T(8,128)(2,1)S(1)}, u32[]{:S(2)}, u32[]{:S(2)}) async-start(bf16[16,96,128]{2,1,0:T(8,128)(2,1)} %shard_map.126), calls=%async_computation.5 | async-start | bytes 786432 | tf_op jit(solution)/shard_map/all_to_all | solution.py:39
  117.5 2.9 %add_convert_fusion = bf16[8,36,8,128]{3,2,1,0:T(8,128)(2,1)} fusion(bf16[8,36,8,128]{3,2,1,0:T(8,128)(2,1)} %collective-permute-done.11, bf16[8,36,8,128]{3,2,1,0:T(8,128)(2,1)} %copy-done.7, bf16[8,36,8,128]{3,2,1,0:T(8,128)(2,1)} %collective-permute-done.9, bf16[8,36,8,128]{3,2,1,0:T(8,128)(2,1)} %get-tuple-element.81), kind=kLoop, calls=%fused_computation.7 | loop fusion | flops 2359296 | bytes 2949120 | tf_op jit(solution)/shard_map/convert_element_type | solution.py:648
  120.4 6.3 %all-to-all-done.5.in_ref = bf16[16,96,128]{2,1,0:T(8,128)(2,1)S(1)} async-done(((bf16[16,96,128]{2,1,0:T(8,128)(2,1)}), bf16[16,96,128]{2,1,0:T(8,128)(2,1)S(1)}, u32[]{:S(2)}, u32[]{:S(2)}) %all-to-all-start.5) | async-done | bytes 393248 | tf_op jit(solution)/shard_map/all_to_all | solution.py:39
  126.7 5.3 %all-to-all-start.6 = ((bf16[32,9,8,128]{3,2,1,0:T(8,128)(2,1)}), bf16[32,9,8,128]{3,2,1,0:T(8,128)(2,1)S(1)}, u32[]{:S(2)}, u32[]{:S(2)}) async-start(bf16[32,9,8,128]{3,2,1,0:T(8,128)(2,1)} %bitcast.55), calls=%async_computation.6 | async-start | bytes 1179648 | tf_op jit(solution)/shard_map/all_to_all | solution.py:39
  132.1 2.2 %fusion.8 = f32[64,1024]{1,0:T(8,128)} fusion(bf16[512,1024]{1,0:T(8,128)(2,1)} %get-tuple-element.95, bf16[512,128]{1,0:T(8,128)(2,1)S(1)} %bitcast.57), kind=kOutput, calls=%fused_computation.15 | convolution fusion | flops 67108864 | bytes 1441792 | tf_op jit(solution)/shard_map/dot_general | solution.py:653
  138.1 5.6 %all-to-all-done.6 = bf16[32,9,8,128]{3,2,1,0:T(8,128)(2,1)S(1)} async-done(((bf16[32,9,8,128]{3,2,1,0:T(8,128)(2,1)}), bf16[32,9,8,128]{3,2,1,0:T(8,128)(2,1)S(1)}, u32[]{:S(2)}, u32[]{:S(2)}) %all-to-all-start.6) | async-done | bytes 589856 | tf_op jit(solution)/shard_map/all_to_all | solution.py:39
  (77 shorter events, 23.2 us)
Async XLA Ops:
  2.3 13.6 %collective-permute-start.2 = (bf16[2,64,1024]{2,1,0:T(8,128)(2,1)}, bf16[2,64,1024]{2,1,0:T(8,128)(2,1)S(1)}, u32[]{:S(2)}, u32[]{:S(2)}) collective-permute-start(bf16[2,64,1024]{2,1,0:T(8,128)(2,1)} %shard_map.120.refs_0_), channel_id=1, source_target_pairs={{0,96},{32,0},{64,32},{96,64},{1,97},{33,1},{65,33},{97,65},{2,98}... | collective-permute-start | bytes 786440 | tf_op jit(solution)/shard_map/ppermute | solution.py:51
  5.6 12.5 %collective-permute-start.1 = (bf16[2,64,1024]{2,1,0:T(8,128)(2,1)}, bf16[2,64,1024]{2,1,0:T(8,128)(2,1)S(1)}, u32[]{:S(2)}, u32[]{:S(2)}) collective-permute-start(bf16[2,64,1024]{2,1,0:T(8,128)(2,1)} %shard_map.120.refs_0_), channel_id=1, source_target_pairs={{0,64},{32,96},{64,0},{96,32},{1,65},{33,97},{65,1},{97,33},{2,66}... | collective-permute-start | bytes 786440 | tf_op jit(solution)/shard_map/ppermute | solution.py:51
  6.1 15.0 %collective-permute-start = (bf16[2,64,1024]{2,1,0:T(8,128)(2,1)}, bf16[2,64,1024]{2,1,0:T(8,128)(2,1)S(1)}, u32[]{:S(2)}, u32[]{:S(2)}) collective-permute-start(bf16[2,64,1024]{2,1,0:T(8,128)(2,1)} %shard_map.120.refs_0_), channel_id=1, source_target_pairs={{0,32},{32,64},{64,96},{96,0},{1,33},{33,65},{65,97},{97,1},{2,34}... | collective-permute-start | bytes 786440 | tf_op jit(solution)/shard_map/ppermute | solution.py:51
  6.8 7.6 %copy-start.6 = (bf16[2,64,1024]{2,1,0:T(8,128)(2,1)S(1)}, bf16[2,64,1024]{2,1,0:T(8,128)(2,1)}, u32[]{:S(2)}) copy-start(bf16[2,64,1024]{2,1,0:T(8,128)(2,1)} %shard_map.120.refs_0_) | copy-start | bytes 786436
  14.4 16.5 %copy-start.4 = (bf16[512,1152]{1,0:T(8,128)(2,1)S(1)}, bf16[512,1152]{1,0:T(8,128)(2,1)}, u32[]{:S(2)}) copy-start(bf16[512,1152]{1,0:T(8,128)(2,1)} %get-tuple-element.70) | copy-start | bytes 3538948
  14.4 7.3 %collective-permute-start.3 = (bf16[2,64,1024]{2,1,0:T(8,128)(2,1)S(1)}, bf16[2,64,1024]{2,1,0:T(8,128)(2,1)S(1)}, u32[]{:S(2)}, u32[]{:S(2)}) collective-permute-start(bf16[2,64,1024]{2,1,0:T(8,128)(2,1)S(1)} %copy-done.6), channel_id=1, source_target_pairs={{0,16},{16,0},{1,17},{17,1},{2,18},{18,2},{3,19},{19,3},{4,20},{20... | collective-permute-start | bytes 786440 | tf_op jit(solution)/shard_map/ppermute | solution.py:47
  15.9 5.8 %collective-permute-start.6 = (bf16[2,64,1024]{2,1,0:T(8,128)(2,1)S(1)}, bf16[2,64,1024]{2,1,0:T(8,128)(2,1)S(1)}, u32[]{:S(2)}, u32[]{:S(2)}) collective-permute-start(bf16[2,64,1024]{2,1,0:T(8,128)(2,1)S(1)} %collective-permute-done.2.refs_3_), channel_id=1, source_target_pairs={{0,16},{16,0},{1,17},{17,1},{2,18},{18,2},{3,19},{19,3},{4,20},{20... | collective-permute-start | bytes 786440 | tf_op jit(solution)/shard_map/ppermute | solution.py:47
  18.1 3.6 %collective-permute-start.5 = (bf16[2,64,1024]{2,1,0:T(8,128)(2,1)S(1)}, bf16[2,64,1024]{2,1,0:T(8,128)(2,1)S(1)}, u32[]{:S(2)}, u32[]{:S(2)}) collective-permute-start(bf16[2,64,1024]{2,1,0:T(8,128)(2,1)S(1)} %collective-permute-done.1.refs_2_), channel_id=1, source_target_pairs={{0,16},{16,0},{1,17},{17,1},{2,18},{18,2},{3,19},{19,3},{4,20},{20... | collective-permute-start | bytes 786440 | tf_op jit(solution)/shard_map/ppermute | solution.py:47
  21.2 1.7 %collective-permute-start.4 = (bf16[2,64,1024]{2,1,0:T(8,128)(2,1)S(1)}, bf16[2,64,1024]{2,1,0:T(8,128)(2,1)S(1)}, u32[]{:S(2)}, u32[]{:S(2)}) collective-permute-start(bf16[2,64,1024]{2,1,0:T(8,128)(2,1)S(1)} %collective-permute-done.refs_1_), channel_id=1, source_target_pairs={{0,16},{16,0},{1,17},{17,1},{2,18},{18,2},{3,19},{19,3},{4,20},{20... | collective-permute-start | bytes 786440 | tf_op jit(solution)/shard_map/ppermute | solution.py:47
  30.9 28.1 %collective-permute-start.7 = (bf16[512,1152]{1,0:T(8,128)(2,1)S(1)}, bf16[512,1152]{1,0:T(8,128)(2,1)}, u32[]{:S(2)}, u32[]{:S(2)}) collective-permute-start(bf16[512,1152]{1,0:T(8,128)(2,1)S(1)} %copy-done.4), channel_id=1, source_target_pairs={{0,16},{16,0},{1,17},{17,1},{2,18},{18,2},{3,19},{19,3},{4,20},{20... | collective-permute-start | bytes 3538952 | tf_op jit(solution)/shard_map/ppermute | solution.py:47
  31.3 18.4 %all-to-all-start = ((f32[128,1,256]{2,1,0:T(1,128)}), f32[128,1,256]{2,1,0:T(1,128)S(1)}, u32[]{:S(2)}, u32[]{:S(2)}) async-start(f32[128,1,256]{2,1,0:T(1,128)} %get-tuple-element.64), calls=%async_computation | async-start | bytes 262144 | tf_op jit(solution)/shard_map/all_to_all | solution.py:39
  50.6 15.2 %all-to-all-start.1 = ((f32[128,1,256]{2,1,0:T(1,128)}), f32[128,1,256]{2,1,0:T(1,128)}, u32[]{:S(2)}, u32[]{:S(2)}) async-start(f32[128,1,256]{2,1,0:T(1,128)} %shard_map.122), calls=%async_computation.1 | async-start | bytes 262144 | tf_op jit(solution)/shard_map/all_to_all | solution.py:39
  72.6 4.2 %collective-permute-start.8 = (bf16[512,1024]{1,0:T(8,128)(2,1)}, bf16[512,1024]{1,0:T(8,128)(2,1)}, u32[]{:S(2)}, u32[]{:S(2)}) collective-permute-start(bf16[512,1024]{1,0:T(8,128)(2,1)} %get-tuple-element.80), channel_id=1, source_target_pairs={{0,16},{16,0},{1,17},{17,1},{2,18},{18,2},{3,19},{19,3},{4,20},{20... | collective-permute-start | bytes 3145736 | tf_op jit(solution)/shard_map/ppermute | solution.py:47
  73.2 18.5 %all-to-all-start.2 = ((bf16[16,3,64,128]{3,2,1,0:T(8,128)(2,1)}), bf16[16,3,64,128]{3,2,1,0:T(8,128)(2,1)S(1)}, u32[]{:S(2)}, u32[]{:S(2)}) async-start(bf16[16,3,64,128]{3,2,1,0:T(8,128)(2,1)} %get-tuple-element.84), calls=%async_computation.2 | async-start | bytes 1572864 | tf_op jit(solution)/shard_map/all_to_all | solution.py:39
  83.0 30.1 %collective-permute-start.10 = (bf16[8,36,8,128]{3,2,1,0:T(8,128)(2,1)S(1)}, bf16[8,36,8,128]{3,2,1,0:T(8,128)(2,1)S(1)}, u32[]{:S(2)}, u32[]{:S(2)}) collective-permute-start(bf16[8,36,8,128]{3,2,1,0:T(8,128)(2,1)S(1)} %get-tuple-element.86), channel_id=1, source_target_pairs={{0,8},{4,12},{8,0},{12,4},{1,9},{5,13},{9,1},{13,5},{2,10},{6,14},... | collective-permute-start | bytes 1769480 | tf_op jit(solution)/shard_map/ppermute | solution.py:51
  85.8 31.7 %collective-permute-start.11 = (bf16[8,36,8,128]{3,2,1,0:T(8,128)(2,1)}, bf16[8,36,8,128]{3,2,1,0:T(8,128)(2,1)}, u32[]{:S(2)}, u32[]{:S(2)}) collective-permute-start(bf16[8,36,8,128]{3,2,1,0:T(8,128)(2,1)} %get-tuple-element.88), channel_id=1, source_target_pairs={{0,12},{4,0},{8,4},{12,8},{1,13},{5,1},{9,5},{13,9},{2,14},{6,2},{... | collective-permute-start | bytes 1769480 | tf_op jit(solution)/shard_map/ppermute | solution.py:51
  86.6 30.9 %collective-permute-start.9 = (bf16[8,36,8,128]{3,2,1,0:T(8,128)(2,1)}, bf16[8,36,8,128]{3,2,1,0:T(8,128)(2,1)}, u32[]{:S(2)}, u32[]{:S(2)}) collective-permute-start(bf16[8,36,8,128]{3,2,1,0:T(8,128)(2,1)} %get-tuple-element.82), channel_id=1, source_target_pairs={{0,4},{4,8},{8,12},{12,0},{1,5},{5,9},{9,13},{13,1},{2,6},{6,10},{... | collective-permute-start | bytes 1769480 | tf_op jit(solution)/shard_map/ppermute | solution.py:51
  101.5 8.9 %copy-start.15 = (bf16[64,128]{1,0:T(8,128)(2,1)}, bf16[64,128]{1,0:T(8,128)(2,1)S(1)}, u32[]{:S(2)}) copy-start(bf16[64,128]{1,0:T(8,128)(2,1)S(1)} %reduce_sum.21.owned_ref) | copy-start | bytes 49156
  113.9 12.8 %all-to-all-start.5 = ((bf16[16,96,128]{2,1,0:T(8,128)(2,1)}), bf16[16,96,128]{2,1,0:T(8,128)(2,1)S(1)}, u32[]{:S(2)}, u32[]{:S(2)}) async-start(bf16[16,96,128]{2,1,0:T(8,128)(2,1)} %shard_map.126), calls=%async_computation.5 | async-start | bytes 786432 | tf_op jit(solution)/shard_map/all_to_all | solution.py:39
  117.5 14.6 %copy-start.5 = (bf16[8,64,128]{2,1,0:T(8,128)(2,1)S(1)}, bf16[8,64,128]{2,1,0:T(8,128)(2,1)}, u32[]{:S(2)}) copy-start(bf16[8,64,128]{2,1,0:T(8,128)(2,1)} %all_to_all.36) | copy-start | bytes 393220
  117.5 16.8 %copy-start = (bf16[1024,1024]{1,0:T(8,128)(2,1)S(1)}, bf16[1024,1024]{1,0:T(8,128)(2,1)}, u32[]{:S(2)}) copy-start(bf16[1024,1024]{1,0:T(8,128)(2,1)} %w_query_ref.1) | copy-start | bytes 6291460
  117.5 16.8 %copy-start.2 = (bf16[1,64,1024]{2,1,0:T(8,128)(2,1)S(1)}, bf16[1,64,1024]{2,1,0:T(8,128)(2,1)}, u32[]{:S(2)}) copy-start(bf16[1,64,1024]{2,1,0:T(8,128)(2,1)} %first_ref.1) | copy-start | bytes 393220
  117.5 16.8 %copy-start.3 = (bf16[1,64,1024]{2,1,0:T(8,128)(2,1)S(1)}, bf16[1,64,1024]{2,1,0:T(8,128)(2,1)}, u32[]{:S(2)}) copy-start(bf16[1,64,1024]{2,1,0:T(8,128)(2,1)} %second_ref.1) | copy-start | bytes 393220
  126.7 17.0 %all-to-all-start.6 = ((bf16[32,9,8,128]{3,2,1,0:T(8,128)(2,1)}), bf16[32,9,8,128]{3,2,1,0:T(8,128)(2,1)S(1)}, u32[]{:S(2)}, u32[]{:S(2)}) async-start(bf16[32,9,8,128]{3,2,1,0:T(8,128)(2,1)} %bitcast.55), calls=%async_computation.6 | async-start | bytes 1179648 | tf_op jit(solution)/shard_map/all_to_all | solution.py:39
  (10 other events, 27.1 us)

commit v8 on v7

--- a/solution.py
+++ b/solution.py
@@ -538,6 +538,7 @@
         out_shape=jax.ShapeDtypeStruct((H, rows + rows // 2, 128), bf16),
         in_specs=[VMEM] * 3,
         out_specs=VMEM,
+        compiler_params=room(12),
         cost_estimate=pl.CostEstimate(
             flops=256 * 1024 * 1024, bytes_accessed=2 * 1024 * 1024, transcendentals=0
         ),

time: 145 us -> 145 us (level)
  transfers between devices with their start and end apart: 17 -> 17, of which waited for: 7 -> 7; matrix products, arithmetic and copies ran while one was open for 10% -> 11% of each run, Pallas kernels for 14% -> 13%
where the time goes in v8:
time: 145 us; the launch traced here: 144 us
  starting transfers between devices  39.2 us (27%)
  Pallas kernels  34.3 us (24%)
  waiting for transfers between devices  31 us (21%)
  blocking collectives  17.5 us (12%)
  matrix products  7.41 us (5%)
  other arithmetic  6.9 us (5%)
  local copies, waits for them, and re-layouts  6.72 us (5%)
    all_to_all x5, waiting for transfers between devices, exchange(): return lax.all_to_all(values, axes, 0, 0, tiled=True)  26.9 us
    all_to_all x5, starting transfers between devices, exchange(): return lax.all_to_all(values, axes, 0, 0, tiled=True)  25.3 us
    all_to_all x2, blocking collectives, exchange(): return lax.all_to_all(values, axes, 0, 0, tiled=True)  17.5 us
    ppermute x6, starting transfers between devices, ring_step(): return lax.ppermute(values, axis, [(i, (i + step) % 4) for i in range(4)])  8.7 us
    pallas_call x1, Pallas kernels, attend(): pl.pallas_call(attend_kernel, out_shape=(small, small, jax.ShapeDtypeStru...  7.26 us
    pallas_call x1, Pallas kernels, gradients(): pl.pallas_call(grads_kernel, grid=(4 // PER_STEP,), out_shape=(jax.ShapeD...  6.77 us
    pallas_call x1, Pallas kernels, project_pairs(): pl.pallas_call(pairs_kernel, grid=(width // tile,), out_shape=(jax.ShapeD...  6.51 us
    ppermute x6, starting transfers between devices, other_core(): return lax.ppermute(values, 'core', [(0, 1), (1, 0)])  5.19 us
  transfers between devices with their start and end apart: 17, of which 7 were waited for; matrix products, arithmetic and copies ran while one was open for 11% of the time, Pallas kernels for 13%

profile of v8, /device:TPU:1, one launch (start us, length us, event | category | flops | bytes accessed | tf_op | source)
XLA Modules:
  0.0 143.9 jit_solution(7580197868181076943)
XLA Ops:
  2.3 3.3 %collective-permute-start.2 = (bf16[2,64,1024]{2,1,0:T(8,128)(2,1)}, bf16[2,64,1024]{2,1,0:T(8,128)(2,1)S(1)}, u32[]{:S(2)}, u32[]{:S(2)}) collective-permute-start(bf16[2,64,1024]{2,1,0:T(8,128)(2,1)} %shard_map.120.refs_0_), channel_id=1, source_target_pairs={{0,96},{32,0},{64,32},{96,64},{1,97},{33,1},{65,33},{97,65},{2,98}... | collective-permute-start | bytes 786440 | tf_op jit(solution)/shard_map/ppermute | solution.py:51
  6.8 6.5 %shard_map.119 = (bf16[512,1152]{1,0:T(8,128)(2,1)}, bf16[512,2048]{1,0:T(8,128)(2,1)}) custom-call(bf16[512,1152]{1,0:T(8,128)(2,1)} %bitcast.62, bf16[1152,2048]{1,0:T(8,128)(2,1)} %w_ref.1), custom_call_target="tpu_custom_call" | custom-call | flops 2415919104 | bytes 9437184 | tf_op jit(solution)/shard_map/pallas_call | solution.py:110
  18.2 3.0 %collective-permute-done.refs_1_ = bf16[2,64,1024]{2,1,0:T(8,128)(2,1)S(1)} collective-permute-done((bf16[2,64,1024]{2,1,0:T(8,128)(2,1)}, bf16[2,64,1024]{2,1,0:T(8,128)(2,1)S(1)}, u32[]{:S(2)}, u32[]{:S(2)}) %collective-permute-start) | collective-permute-done | bytes 262176 | tf_op jit(solution)/shard_map/ppermute | solution.py:51
  23.6 7.3 %shard_map.121 = (bf16[256,1024]{1,0:T(8,128)(2,1)}, bf16[256,1024]{1,0:T(8,128)(2,1)}, f32[128,1,256]{2,1,0:T(1,128)}) custom-call(s32[4]{0:T(128)} %counts.3, s32[4]{0:T(128)} %groups.3, s32[4]{0:T(128)} %fusion.12.places, bf16[2,64,1024]{2,1,0:T(8,128)(2,1)} %shard_map.120.refs_0_, bf16[2,64,1024]{2,1,0:T(8,128)(2,1)} %copy-done.10, ...), custom_call_target="tpu_custom_call" | custom-call | flops 6442450944 | bytes 10485760 | tf_op jit(solution)/shard_map/pallas_call | solution.py:272
  31.3 8.1 %all-to-all-start = ((f32[128,1,256]{2,1,0:T(1,128)}), f32[128,1,256]{2,1,0:T(1,128)S(1)}, u32[]{:S(2)}, u32[]{:S(2)}) async-start(f32[128,1,256]{2,1,0:T(1,128)} %get-tuple-element.64), calls=%async_computation | async-start | bytes 262144 | tf_op jit(solution)/shard_map/all_to_all | solution.py:39
  39.5 4.4 %shard_map.124 = (f32[512,1024]{1,0:T(8,128)}, f32[512,1024]{1,0:T(8,128)}) custom-call(bf16[256,1024]{1,0:T(8,128)(2,1)} %get-tuple-element.71.q_ref, bf16[256,1024]{1,0:T(8,128)(2,1)} %get-tuple-element.72.d_ref, bf16[512,2048]{1,0:T(8,128)(2,1)} %get-tuple-element.54.refs_10_.pairs_ref), custom_call_target="tpu_custom_call" | custom-call | flops 2147483648 | bytes 8388608 | tf_op jit(solution)/shard_map/pallas_call | solution.py:332
  43.9 5.8 %all-to-all-done.in_ref = f32[128,1,256]{2,1,0:T(1,128)S(1)} async-done(((f32[128,1,256]{2,1,0:T(1,128)}), f32[128,1,256]{2,1,0:T(1,128)S(1)}, u32[]{:S(2)}, u32[]{:S(2)}) %all-to-all-start) | async-done | bytes 131104 | tf_op jit(solution)/shard_map/all_to_all | solution.py:39
  50.6 4.0 %all-to-all-start.1 = ((f32[128,1,256]{2,1,0:T(1,128)}), f32[128,1,256]{2,1,0:T(1,128)S(1)}, u32[]{:S(2)}, u32[]{:S(2)}) async-start(f32[128,1,256]{2,1,0:T(1,128)} %shard_map.122), calls=%async_computation.1 | async-start | bytes 262144 | tf_op jit(solution)/shard_map/all_to_all | solution.py:39
  54.8 3.2 %shard_map.123 = (bf16[512,1024]{1,0:T(8,128)(2,1)}, bf16[512,1024]{1,0:T(8,128)(2,1)}) custom-call(s32[8]{0:T(128)} %stack.35.owners, bf16[2,64,1024]{2,1,0:T(8,128)(2,1)} %shard_map.120.refs_0_, bf16[2,64,1024]{2,1,0:T(8,128)(2,1)} %copy-done.10, bf16[2,64,1024]{2,1,0:T(8,128)(2,1)} %copy-done.9, bf16[2,64,1024]{2,1,0:T(8,128)(2,1)} %copy-done.8, ...), custom_call_target="tpu_custom_call" | custom-call | flops 4194304 | bytes 4194304 | tf_op jit(solution)/shard_map/pallas_call | solution.py:507
  59.6 5.2 %all-to-all-done.1.reply_ref = f32[128,1,256]{2,1,0:T(1,128)S(1)} async-done(((f32[128,1,256]{2,1,0:T(1,128)}), f32[128,1,256]{2,1,0:T(1,128)S(1)}, u32[]{:S(2)}, u32[]{:S(2)}) %all-to-all-start.1) | async-done | bytes 131104 | tf_op jit(solution)/shard_map/all_to_all | solution.py:39
  65.5 6.8 %shard_map.125 = (bf16[512,1024]{1,0:T(8,128)(2,1)}, bf16[512,1024]{1,0:T(8,128)(2,1)}, bf16[16,3,64,128]{3,2,1,0:T(8,128)(2,1)}) custom-call(s32[4]{0:T(128)} %counts.3, s32[4]{0:T(128)} %groups.3, s32[1]{0:T(128)} %bitcast.10.core, bf16[256,1024]{1,0:T(8,128)(2,1)} %get-tuple-element.71.q_ref, bf16[256,1024]{1,0:T(8,128)(2,1)} %get-tuple-element.72.d_ref, ...), custom_call_target="tpu_custom_call" | custom-call | flops 8589934592 | bytes 8388608 | tf_op jit(solution)/shard_map/pallas_call | solution.py:470
  72.8 3.6 %all-to-all-start.2 = ((bf16[16,3,64,128]{3,2,1,0:T(8,128)(2,1)}), bf16[16,3,64,128]{3,2,1,0:T(8,128)(2,1)S(1)}, u32[]{:S(2)}, u32[]{:S(2)}) async-start(bf16[16,3,64,128]{3,2,1,0:T(8,128)(2,1)} %get-tuple-element.84), calls=%async_computation.2 | async-start | bytes 1572864 | tf_op jit(solution)/shard_map/all_to_all | solution.py:39
  76.4 4.6 %fusion.3 = bf16[144,8,8,128]{3,1,2,0:T(8,128)(2,1)S(1)} fusion(bf16[1024,1152]{1,0:T(8,128)(2,1)} %pad_maximum_fusion, bf16[512,1024]{1,0:T(8,128)(2,1)S(1)} %collective-permute-done.8, bf16[512,1024]{1,0:T(8,128)(2,1)} %get-tuple-element.79), kind=kOutput, calls=%fused_computation.5 | convolution fusion | flops 2421293056 | bytes 6815744 | tf_op jit(solution)/shard_map/dot_general | solution.py:632
  83.0 2.8 %collective-permute-start.10 = (bf16[8,36,8,128]{3,2,1,0:T(8,128)(2,1)S(1)}, bf16[8,36,8,128]{3,2,1,0:T(8,128)(2,1)S(1)}, u32[]{:S(2)}, u32[]{:S(2)}) collective-permute-start(bf16[8,36,8,128]{3,2,1,0:T(8,128)(2,1)S(1)} %get-tuple-element.86), channel_id=1, source_target_pairs={{0,8},{4,12},{8,0},{12,4},{1,9},{5,13},{9,1},{13,5},{2,10},{6,14},... | collective-permute-start | bytes 1769480 | tf_op jit(solution)/shard_map/ppermute | solution.py:51
  87.2 4.0 %all-to-all-done.2 = bf16[16,3,64,128]{3,2,1,0:T(8,128)(2,1)S(1)} async-done(((bf16[16,3,64,128]{3,2,1,0:T(8,128)(2,1)}), bf16[16,3,64,128]{3,2,1,0:T(8,128)(2,1)S(1)}, u32[]{:S(2)}, u32[]{:S(2)}) %all-to-all-start.2) | async-done | bytes 786464 | tf_op jit(solution)/shard_map/all_to_all | solution.py:39
  91.8 9.3 %all_to_all.35 = bf16[8,64,128]{2,1,0:T(8,128)(2,1)S(1)} all-to-all(bf16[8,64,128]{2,1,0:T(8,128)(2,1)S(1)} %copy.17), channel_id=1, replica_groups=mesh['x'=4,'core'=2,'z'=4,'y'=4] {'x','core'}, dimensions={0} | all-to-all | bytes 262144 | tf_op jit(solution)/shard_map/all_to_all | solution.py:39
  101.1 8.2 %all_to_all.36 = bf16[8,64,128]{2,1,0:T(8,128)(2,1)S(1)} all-to-all(bf16[8,64,128]{2,1,0:T(8,128)(2,1)S(1)} %broadcast_in_dim.20), channel_id=1, replica_groups=mesh['x'=4,'core'=2,'z'=4,'y'=4] {'x','core'}, dimensions={0} | all-to-all | bytes 262144 | tf_op jit(solution)/shard_map/all_to_all | solution.py:39
  111.5 3.6 %all-to-all-start.5 = ((bf16[16,96,128]{2,1,0:T(8,128)(2,1)}), bf16[16,96,128]{2,1,0:T(8,128)(2,1)S(1)}, u32[]{:S(2)}, u32[]{:S(2)}) async-start(bf16[16,96,128]{2,1,0:T(8,128)(2,1)} %shard_map.126), calls=%async_computation.5 | async-start | bytes 786432 | tf_op jit(solution)/shard_map/all_to_all | solution.py:39
  115.2 2.9 %add_convert_fusion = bf16[8,36,8,128]{3,2,1,0:T(8,128)(2,1)} fusion(bf16[8,36,8,128]{3,2,1,0:T(8,128)(2,1)} %collective-permute-done.11, bf16[8,36,8,128]{3,2,1,0:T(8,128)(2,1)} %copy-done.7, bf16[8,36,8,128]{3,2,1,0:T(8,128)(2,1)} %collective-permute-done.9, bf16[8,36,8,128]{3,2,1,0:T(8,128)(2,1)} %get-tuple-element.81), kind=kLoop, calls=%fused_computation.7 | loop fusion | flops 2359296 | bytes 2949120 | tf_op jit(solution)/shard_map/convert_element_type | solution.py:649
  118.1 6.3 %all-to-all-done.5.in_ref = bf16[16,96,128]{2,1,0:T(8,128)(2,1)S(1)} async-done(((bf16[16,96,128]{2,1,0:T(8,128)(2,1)}), bf16[16,96,128]{2,1,0:T(8,128)(2,1)S(1)}, u32[]{:S(2)}, u32[]{:S(2)}) %all-to-all-start.5) | async-done | bytes 393248 | tf_op jit(solution)/shard_map/all_to_all | solution.py:39
  124.3 6.0 %all-to-all-start.6 = ((bf16[32,9,8,128]{3,2,1,0:T(8,128)(2,1)}), bf16[32,9,8,128]{3,2,1,0:T(8,128)(2,1)}, u32[]{:S(2)}, u32[]{:S(2)}) async-start(bf16[32,9,8,128]{3,2,1,0:T(8,128)(2,1)} %bitcast.56), calls=%async_computation.6 | async-start | bytes 1179648 | tf_op jit(solution)/shard_map/all_to_all | solution.py:39
  130.3 2.2 %fusion.8 = f32[64,1024]{1,0:T(8,128)} fusion(bf16[512,1024]{1,0:T(8,128)(2,1)} %get-tuple-element.95, bf16[512,128]{1,0:T(8,128)(2,1)S(1)} %bitcast.52), kind=kOutput, calls=%fused_computation.15 | convolution fusion | flops 67108864 | bytes 1441792 | tf_op jit(solution)/shard_map/dot_general | solution.py:654
  134.2 2.2 %shard_map.127 = (bf16[64,1024]{1,0:T(8,128)(2,1)}, bf16[64,1024]{1,0:T(8,128)(2,1)}, f32[64,1024]{1,0:T(8,128)}) custom-call(bf16[16,96,128]{2,1,0:T(8,128)(2,1)S(1)} %all-to-all-done.5.in_ref, bf16[64,1024]{1,0:T(8,128)(2,1)S(1)} %bitcast.53, bf16[64,1024]{1,0:T(8,128)(2,1)S(1)} %bitcast.54, bf16[1024,1024]{1,0:T(8,128)(2,1)S(1)} %copy-done, ...), custom_call_target="tpu_custom_call" | custom-call | tf_op jit(solution)/shard_map/pallas_call | solution.py:580
  136.4 5.7 %all-to-all-done.6 = bf16[32,9,8,128]{3,2,1,0:T(8,128)(2,1)} async-done(((bf16[32,9,8,128]{3,2,1,0:T(8,128)(2,1)}), bf16[32,9,8,128]{3,2,1,0:T(8,128)(2,1)}, u32[]{:S(2)}, u32[]{:S(2)}) %all-to-all-start.6) | async-done | bytes 589856 | tf_op jit(solution)/shard_map/all_to_all | solution.py:39
  (77 shorter events, 24.2 us)
Async XLA Ops:
  2.3 13.7 %collective-permute-start.2 = (bf16[2,64,1024]{2,1,0:T(8,128)(2,1)}, bf16[2,64,1024]{2,1,0:T(8,128)(2,1)S(1)}, u32[]{:S(2)}, u32[]{:S(2)}) collective-permute-start(bf16[2,64,1024]{2,1,0:T(8,128)(2,1)} %shard_map.120.refs_0_), channel_id=1, source_target_pairs={{0,96},{32,0},{64,32},{96,64},{1,97},{33,1},{65,33},{97,65},{2,98}... | collective-permute-start | bytes 786440 | tf_op jit(solution)/shard_map/ppermute | solution.py:51
  5.6 12.5 %collective-permute-start.1 = (bf16[2,64,1024]{2,1,0:T(8,128)(2,1)}, bf16[2,64,1024]{2,1,0:T(8,128)(2,1)S(1)}, u32[]{:S(2)}, u32[]{:S(2)}) collective-permute-start(bf16[2,64,1024]{2,1,0:T(8,128)(2,1)} %shard_map.120.refs_0_), channel_id=1, source_target_pairs={{0,64},{32,96},{64,0},{96,32},{1,65},{33,97},{65,1},{97,33},{2,66}... | collective-permute-start | bytes 786440 | tf_op jit(solution)/shard_map/ppermute | solution.py:51
  6.1 15.0 %collective-permute-start = (bf16[2,64,1024]{2,1,0:T(8,128)(2,1)}, bf16[2,64,1024]{2,1,0:T(8,128)(2,1)S(1)}, u32[]{:S(2)}, u32[]{:S(2)}) collective-permute-start(bf16[2,64,1024]{2,1,0:T(8,128)(2,1)} %shard_map.120.refs_0_), channel_id=1, source_target_pairs={{0,32},{32,64},{64,96},{96,0},{1,33},{33,65},{65,97},{97,1},{2,34}... | collective-permute-start | bytes 786440 | tf_op jit(solution)/shard_map/ppermute | solution.py:51
  6.8 7.2 %copy-start.16 = (s32[4]{0:T(128)S(1)}, s32[4]{0:T(128)}, u32[]{:S(2)}) copy-start(s32[4]{0:T(128)} %groups.3) | copy-start | bytes 52
  6.8 7.7 %copy-start.6 = (bf16[2,64,1024]{2,1,0:T(8,128)(2,1)S(1)}, bf16[2,64,1024]{2,1,0:T(8,128)(2,1)}, u32[]{:S(2)}) copy-start(bf16[2,64,1024]{2,1,0:T(8,128)(2,1)} %shard_map.120.refs_0_) | copy-start | bytes 786436
  14.5 16.4 %copy-start.5 = (bf16[512,1152]{1,0:T(8,128)(2,1)S(1)}, bf16[512,1152]{1,0:T(8,128)(2,1)}, u32[]{:S(2)}) copy-start(bf16[512,1152]{1,0:T(8,128)(2,1)} %get-tuple-element.70) | copy-start | bytes 3538948
  14.5 7.2 %collective-permute-start.3 = (bf16[2,64,1024]{2,1,0:T(8,128)(2,1)S(1)}, bf16[2,64,1024]{2,1,0:T(8,128)(2,1)S(1)}, u32[]{:S(2)}, u32[]{:S(2)}) collective-permute-start(bf16[2,64,1024]{2,1,0:T(8,128)(2,1)S(1)} %copy-done.6), channel_id=1, source_target_pairs={{0,16},{16,0},{1,17},{17,1},{2,18},{18,2},{3,19},{19,3},{4,20},{20... | collective-permute-start | bytes 786440 | tf_op jit(solution)/shard_map/ppermute | solution.py:47
  16.0 5.7 %collective-permute-start.6 = (bf16[2,64,1024]{2,1,0:T(8,128)(2,1)S(1)}, bf16[2,64,1024]{2,1,0:T(8,128)(2,1)S(1)}, u32[]{:S(2)}, u32[]{:S(2)}) collective-permute-start(bf16[2,64,1024]{2,1,0:T(8,128)(2,1)S(1)} %collective-permute-done.2.refs_3_), channel_id=1, source_target_pairs={{0,16},{16,0},{1,17},{17,1},{2,18},{18,2},{3,19},{19,3},{4,20},{20... | collective-permute-start | bytes 786440 | tf_op jit(solution)/shard_map/ppermute | solution.py:47
  18.1 3.6 %collective-permute-start.5 = (bf16[2,64,1024]{2,1,0:T(8,128)(2,1)S(1)}, bf16[2,64,1024]{2,1,0:T(8,128)(2,1)S(1)}, u32[]{:S(2)}, u32[]{:S(2)}) collective-permute-start(bf16[2,64,1024]{2,1,0:T(8,128)(2,1)S(1)} %collective-permute-done.1.refs_2_), channel_id=1, source_target_pairs={{0,16},{16,0},{1,17},{17,1},{2,18},{18,2},{3,19},{19,3},{4,20},{20... | collective-permute-start | bytes 786440 | tf_op jit(solution)/shard_map/ppermute | solution.py:47
  21.2 1.7 %collective-permute-start.4 = (bf16[2,64,1024]{2,1,0:T(8,128)(2,1)S(1)}, bf16[2,64,1024]{2,1,0:T(8,128)(2,1)S(1)}, u32[]{:S(2)}, u32[]{:S(2)}) collective-permute-start(bf16[2,64,1024]{2,1,0:T(8,128)(2,1)S(1)} %collective-permute-done.refs_1_), channel_id=1, source_target_pairs={{0,16},{16,0},{1,17},{17,1},{2,18},{18,2},{3,19},{19,3},{4,20},{20... | collective-permute-start | bytes 786440 | tf_op jit(solution)/shard_map/ppermute | solution.py:47
  30.9 27.1 %collective-permute-start.7 = (bf16[512,1152]{1,0:T(8,128)(2,1)S(1)}, bf16[512,1152]{1,0:T(8,128)(2,1)S(1)}, u32[]{:S(2)}, u32[]{:S(2)}) collective-permute-start(bf16[512,1152]{1,0:T(8,128)(2,1)S(1)} %copy-done.5), channel_id=1, source_target_pairs={{0,16},{16,0},{1,17},{17,1},{2,18},{18,2},{3,19},{19,3},{4,20},{20... | collective-permute-start | bytes 3538952 | tf_op jit(solution)/shard_map/ppermute | solution.py:47
  31.3 18.3 %all-to-all-start = ((f32[128,1,256]{2,1,0:T(1,128)}), f32[128,1,256]{2,1,0:T(1,128)S(1)}, u32[]{:S(2)}, u32[]{:S(2)}) async-start(f32[128,1,256]{2,1,0:T(1,128)} %get-tuple-element.64), calls=%async_computation | async-start | bytes 262144 | tf_op jit(solution)/shard_map/all_to_all | solution.py:39
  50.6 14.2 %all-to-all-start.1 = ((f32[128,1,256]{2,1,0:T(1,128)}), f32[128,1,256]{2,1,0:T(1,128)S(1)}, u32[]{:S(2)}, u32[]{:S(2)}) async-start(f32[128,1,256]{2,1,0:T(1,128)} %shard_map.122), calls=%async_computation.1 | async-start | bytes 262144 | tf_op jit(solution)/shard_map/all_to_all | solution.py:39
  72.2 4.2 %collective-permute-start.8 = (bf16[512,1024]{1,0:T(8,128)(2,1)}, bf16[512,1024]{1,0:T(8,128)(2,1)S(1)}, u32[]{:S(2)}, u32[]{:S(2)}) collective-permute-start(bf16[512,1024]{1,0:T(8,128)(2,1)} %get-tuple-element.80), channel_id=1, source_target_pairs={{0,16},{16,0},{1,17},{17,1},{2,18},{18,2},{3,19},{19,3},{4,20},{20... | collective-permute-start | bytes 3145736 | tf_op jit(solution)/shard_map/ppermute | solution.py:47
  72.8 18.4 %all-to-all-start.2 = ((bf16[16,3,64,128]{3,2,1,0:T(8,128)(2,1)}), bf16[16,3,64,128]{3,2,1,0:T(8,128)(2,1)S(1)}, u32[]{:S(2)}, u32[]{:S(2)}) async-start(bf16[16,3,64,128]{3,2,1,0:T(8,128)(2,1)} %get-tuple-element.84), calls=%async_computation.2 | async-start | bytes 1572864 | tf_op jit(solution)/shard_map/all_to_all | solution.py:39
  83.0 26.4 %copy-start.2 = (bf16[512,1024]{1,0:T(8,128)(2,1)S(1)}, bf16[512,1024]{1,0:T(8,128)(2,1)}, u32[]{:S(2)}) copy-start(bf16[512,1024]{1,0:T(8,128)(2,1)} %get-tuple-element.85.latents_ref) | copy-start | bytes 3145732
  83.0 27.7 %collective-permute-start.10 = (bf16[8,36,8,128]{3,2,1,0:T(8,128)(2,1)S(1)}, bf16[8,36,8,128]{3,2,1,0:T(8,128)(2,1)S(1)}, u32[]{:S(2)}, u32[]{:S(2)}) collective-permute-start(bf16[8,36,8,128]{3,2,1,0:T(8,128)(2,1)S(1)} %get-tuple-element.86), channel_id=1, source_target_pairs={{0,8},{4,12},{8,0},{12,4},{1,9},{5,13},{9,1},{13,5},{2,10},{6,14},... | collective-permute-start | bytes 1769480 | tf_op jit(solution)/shard_map/ppermute | solution.py:51
  85.8 29.4 %collective-permute-start.11 = (bf16[8,36,8,128]{3,2,1,0:T(8,128)(2,1)}, bf16[8,36,8,128]{3,2,1,0:T(8,128)(2,1)}, u32[]{:S(2)}, u32[]{:S(2)}) collective-permute-start(bf16[8,36,8,128]{3,2,1,0:T(8,128)(2,1)} %get-tuple-element.88), channel_id=1, source_target_pairs={{0,12},{4,0},{8,4},{12,8},{1,13},{5,1},{9,5},{13,9},{2,14},{6,2},{... | collective-permute-start | bytes 1769480 | tf_op jit(solution)/shard_map/ppermute | solution.py:51
  86.6 28.5 %collective-permute-start.9 = (bf16[8,36,8,128]{3,2,1,0:T(8,128)(2,1)}, bf16[8,36,8,128]{3,2,1,0:T(8,128)(2,1)}, u32[]{:S(2)}, u32[]{:S(2)}) collective-permute-start(bf16[8,36,8,128]{3,2,1,0:T(8,128)(2,1)} %get-tuple-element.82), channel_id=1, source_target_pairs={{0,4},{4,8},{8,12},{12,0},{1,5},{5,9},{9,13},{13,1},{2,6},{6,10},{... | collective-permute-start | bytes 1769480 | tf_op jit(solution)/shard_map/ppermute | solution.py:51
  111.5 12.8 %all-to-all-start.5 = ((bf16[16,96,128]{2,1,0:T(8,128)(2,1)}), bf16[16,96,128]{2,1,0:T(8,128)(2,1)S(1)}, u32[]{:S(2)}, u32[]{:S(2)}) async-start(bf16[16,96,128]{2,1,0:T(8,128)(2,1)} %shard_map.126), calls=%async_computation.5 | async-start | bytes 786432 | tf_op jit(solution)/shard_map/all_to_all | solution.py:39
  115.1 17.5 %copy-start = (bf16[1024,1024]{1,0:T(8,128)(2,1)S(1)}, bf16[1024,1024]{1,0:T(8,128)(2,1)}, u32[]{:S(2)}) copy-start(bf16[1024,1024]{1,0:T(8,128)(2,1)} %w_query_ref.1) | copy-start | bytes 6291460
  115.1 17.5 %copy-start.3 = (bf16[1,64,1024]{2,1,0:T(8,128)(2,1)S(1)}, bf16[1,64,1024]{2,1,0:T(8,128)(2,1)}, u32[]{:S(2)}) copy-start(bf16[1,64,1024]{2,1,0:T(8,128)(2,1)} %first_ref.1) | copy-start | bytes 393220
  115.1 17.5 %copy-start.4 = (bf16[1,64,1024]{2,1,0:T(8,128)(2,1)S(1)}, bf16[1,64,1024]{2,1,0:T(8,128)(2,1)}, u32[]{:S(2)}) copy-start(bf16[1,64,1024]{2,1,0:T(8,128)(2,1)} %second_ref.1) | copy-start | bytes 393220
  124.3 17.7 %all-to-all-start.6 = ((bf16[32,9,8,128]{3,2,1,0:T(8,128)(2,1)}), bf16[32,9,8,128]{3,2,1,0:T(8,128)(2,1)}, u32[]{:S(2)}, u32[]{:S(2)}) async-start(bf16[32,9,8,128]{3,2,1,0:T(8,128)(2,1)} %bitcast.56), calls=%async_computation.6 | async-start | bytes 1179648 | tf_op jit(solution)/shard_map/all_to_all | solution.py:39
  (10 other events, 20.6 us)

commit v9 on v8

--- a/solution.py
+++ b/solution.py
@@ -233,7 +233,7 @@
                 moment_ref[block, p : p + 1, :] = moment[:, part : part + 128]
         return carry
 
-    lax.fori_loop(0, blocks, one_block, 0, unroll=2)
+    lax.fori_loop(0, blocks, one_block, 0, unroll=4)
     own = [groups[i] for i in range(blocks)]
     slots = slots_of(own)
     left = low_lanes((8, 128))

time: 145 us -> 144 us (level)
  no operation moved by 1% of the time
where the time goes in v9:
time: 144 us
  starting transfers between devices  39.2 us (27%)
  Pallas kernels  34 us (24%)
  waiting for transfers between devices  31.1 us (22%)
  blocking collectives  17.5 us (12%)
  matrix products  7.41 us (5%)
  other arithmetic  6.9 us (5%)
  local copies, waits for them, and re-layouts  6.72 us (5%)
    all_to_all x5, waiting for transfers between devices, exchange(): return lax.all_to_all(values, axes, 0, 0, tiled=True)  26.9 us
    all_to_all x5, starting transfers between devices, exchange(): return lax.all_to_all(values, axes, 0, 0, tiled=True)  25.3 us
    all_to_all x2, blocking collectives, exchange(): return lax.all_to_all(values, axes, 0, 0, tiled=True)  17.5 us
    ppermute x6, starting transfers between devices, ring_step(): return lax.ppermute(values, axis, [(i, (i + step) % 4) for i in range(4)])  8.7 us
    pallas_call x1, Pallas kernels, attend(): pl.pallas_call(attend_kernel, out_shape=(small, small, jax.ShapeDtypeStru...  6.99 us
    pallas_call x1, Pallas kernels, gradients(): pl.pallas_call(grads_kernel, grid=(4 // PER_STEP,), out_shape=(jax.ShapeD...  6.77 us
    pallas_call x1, Pallas kernels, project_pairs(): pl.pallas_call(pairs_kernel, grid=(width // tile,), out_shape=(jax.ShapeD...  6.51 us
    ppermute x6, starting transfers between devices, other_core(): return lax.ppermute(values, 'core', [(0, 1), (1, 0)])  5.19 us
  transfers between devices with their start and end apart: 17, of which 7 were waited for; matrix products, arithmetic and copies ran while one was open for 11% of the time, Pallas kernels for 13%

profile of v9, /device:TPU:1, one launch (start us, length us, event | category | flops | bytes accessed | tf_op | source)
XLA Modules:
  0.0 143.7 jit_solution(12827698559539032211)
XLA Ops:
  2.3 3.3 %collective-permute-start.2 = (bf16[2,64,1024]{2,1,0:T(8,128)(2,1)}, bf16[2,64,1024]{2,1,0:T(8,128)(2,1)S(1)}, u32[]{:S(2)}, u32[]{:S(2)}) collective-permute-start(bf16[2,64,1024]{2,1,0:T(8,128)(2,1)} %shard_map.120.refs_0_), channel_id=1, source_target_pairs={{0,96},{32,0},{64,32},{96,64},{1,97},{33,1},{65,33},{97,65},{2,98}... | collective-permute-start | bytes 786440 | tf_op jit(solution)/shard_map/ppermute | solution.py:51
  6.8 6.5 %shard_map.119 = (bf16[512,1152]{1,0:T(8,128)(2,1)}, bf16[512,2048]{1,0:T(8,128)(2,1)}) custom-call(bf16[512,1152]{1,0:T(8,128)(2,1)} %bitcast.62, bf16[1152,2048]{1,0:T(8,128)(2,1)} %w_ref.1), custom_call_target="tpu_custom_call" | custom-call | flops 2415919104 | bytes 9437184 | tf_op jit(solution)/shard_map/pallas_call | solution.py:110
  18.2 3.0 %collective-permute-done.refs_1_ = bf16[2,64,1024]{2,1,0:T(8,128)(2,1)S(1)} collective-permute-done((bf16[2,64,1024]{2,1,0:T(8,128)(2,1)}, bf16[2,64,1024]{2,1,0:T(8,128)(2,1)S(1)}, u32[]{:S(2)}, u32[]{:S(2)}) %collective-permute-start) | collective-permute-done | bytes 262176 | tf_op jit(solution)/shard_map/ppermute | solution.py:51
  23.6 7.0 %shard_map.121 = (bf16[256,1024]{1,0:T(8,128)(2,1)}, bf16[256,1024]{1,0:T(8,128)(2,1)}, f32[128,1,256]{2,1,0:T(1,128)}) custom-call(s32[4]{0:T(128)} %counts.3, s32[4]{0:T(128)} %groups.3, s32[4]{0:T(128)} %fusion.12.places, bf16[2,64,1024]{2,1,0:T(8,128)(2,1)} %shard_map.120.refs_0_, bf16[2,64,1024]{2,1,0:T(8,128)(2,1)} %copy-done.10, ...), custom_call_target="tpu_custom_call" | custom-call | flops 6442450944 | bytes 10485760 | tf_op jit(solution)/shard_map/pallas_call | solution.py:272
  31.1 8.1 %all-to-all-start = ((f32[128,1,256]{2,1,0:T(1,128)}), f32[128,1,256]{2,1,0:T(1,128)S(1)}, u32[]{:S(2)}, u32[]{:S(2)}) async-start(f32[128,1,256]{2,1,0:T(1,128)} %get-tuple-element.64), calls=%async_computation | async-start | bytes 262144 | tf_op jit(solution)/shard_map/all_to_all | solution.py:39
  39.2 4.4 %shard_map.124 = (f32[512,1024]{1,0:T(8,128)}, f32[512,1024]{1,0:T(8,128)}) custom-call(bf16[256,1024]{1,0:T(8,128)(2,1)} %get-tuple-element.71.q_ref, bf16[256,1024]{1,0:T(8,128)(2,1)} %get-tuple-element.72.d_ref, bf16[512,2048]{1,0:T(8,128)(2,1)} %get-tuple-element.54.refs_10_.pairs_ref), custom_call_target="tpu_custom_call" | custom-call | flops 2147483648 | bytes 8388608 | tf_op jit(solution)/shard_map/pallas_call | solution.py:332
  43.6 5.8 %all-to-all-done.in_ref = f32[128,1,256]{2,1,0:T(1,128)S(1)} async-done(((f32[128,1,256]{2,1,0:T(1,128)}), f32[128,1,256]{2,1,0:T(1,128)S(1)}, u32[]{:S(2)}, u32[]{:S(2)}) %all-to-all-start) | async-done | bytes 131104 | tf_op jit(solution)/shard_map/all_to_all | solution.py:39
  50.3 4.0 %all-to-all-start.1 = ((f32[128,1,256]{2,1,0:T(1,128)}), f32[128,1,256]{2,1,0:T(1,128)S(1)}, u32[]{:S(2)}, u32[]{:S(2)}) async-start(f32[128,1,256]{2,1,0:T(1,128)} %shard_map.122), calls=%async_computation.1 | async-start | bytes 262144 | tf_op jit(solution)/shard_map/all_to_all | solution.py:39
  54.5 3.2 %shard_map.123 = (bf16[512,1024]{1,0:T(8,128)(2,1)}, bf16[512,1024]{1,0:T(8,128)(2,1)}) custom-call(s32[8]{0:T(128)} %stack.35.owners, bf16[2,64,1024]{2,1,0:T(8,128)(2,1)} %shard_map.120.refs_0_, bf16[2,64,1024]{2,1,0:T(8,128)(2,1)} %copy-done.10, bf16[2,64,1024]{2,1,0:T(8,128)(2,1)} %copy-done.9, bf16[2,64,1024]{2,1,0:T(8,128)(2,1)} %copy-done.8, ...), custom_call_target="tpu_custom_call" | custom-call | flops 4194304 | bytes 4194304 | tf_op jit(solution)/shard_map/pallas_call | solution.py:507
  59.4 5.2 %all-to-all-done.1.reply_ref = f32[128,1,256]{2,1,0:T(1,128)S(1)} async-done(((f32[128,1,256]{2,1,0:T(1,128)}), f32[128,1,256]{2,1,0:T(1,128)S(1)}, u32[]{:S(2)}, u32[]{:S(2)}) %all-to-all-start.1) | async-done | bytes 131104 | tf_op jit(solution)/shard_map/all_to_all | solution.py:39
  65.2 6.8 %shard_map.125 = (bf16[512,1024]{1,0:T(8,128)(2,1)}, bf16[512,1024]{1,0:T(8,128)(2,1)}, bf16[16,3,64,128]{3,2,1,0:T(8,128)(2,1)}) custom-call(s32[4]{0:T(128)} %counts.3, s32[4]{0:T(128)} %groups.3, s32[1]{0:T(128)} %bitcast.10.core, bf16[256,1024]{1,0:T(8,128)(2,1)} %get-tuple-element.71.q_ref, bf16[256,1024]{1,0:T(8,128)(2,1)} %get-tuple-element.72.d_ref, ...), custom_call_target="tpu_custom_call" | custom-call | flops 8589934592 | bytes 8388608 | tf_op jit(solution)/shard_map/pallas_call | solution.py:470
  72.5 3.6 %all-to-all-start.2 = ((bf16[16,3,64,128]{3,2,1,0:T(8,128)(2,1)}), bf16[16,3,64,128]{3,2,1,0:T(8,128)(2,1)S(1)}, u32[]{:S(2)}, u32[]{:S(2)}) async-start(bf16[16,3,64,128]{3,2,1,0:T(8,128)(2,1)} %get-tuple-element.84), calls=%async_computation.2 | async-start | bytes 1572864 | tf_op jit(solution)/shard_map/all_to_all | solution.py:39
  76.1 4.6 %fusion.3 = bf16[144,8,8,128]{3,1,2,0:T(8,128)(2,1)S(1)} fusion(bf16[1024,1152]{1,0:T(8,128)(2,1)} %pad_maximum_fusion, bf16[512,1024]{1,0:T(8,128)(2,1)S(1)} %collective-permute-done.8, bf16[512,1024]{1,0:T(8,128)(2,1)} %get-tuple-element.79), kind=kOutput, calls=%fused_computation.5 | convolution fusion | flops 2421293056 | bytes 6815744 | tf_op jit(solution)/shard_map/dot_general | solution.py:632
  82.7 2.8 %collective-permute-start.10 = (bf16[8,36,8,128]{3,2,1,0:T(8,128)(2,1)S(1)}, bf16[8,36,8,128]{3,2,1,0:T(8,128)(2,1)S(1)}, u32[]{:S(2)}, u32[]{:S(2)}) collective-permute-start(bf16[8,36,8,128]{3,2,1,0:T(8,128)(2,1)S(1)} %get-tuple-element.86), channel_id=1, source_target_pairs={{0,8},{4,12},{8,0},{12,4},{1,9},{5,13},{9,1},{13,5},{2,10},{6,14},... | collective-permute-start | bytes 1769480 | tf_op jit(solution)/shard_map/ppermute | solution.py:51
  87.0 4.0 %all-to-all-done.2 = bf16[16,3,64,128]{3,2,1,0:T(8,128)(2,1)S(1)} async-done(((bf16[16,3,64,128]{3,2,1,0:T(8,128)(2,1)}), bf16[16,3,64,128]{3,2,1,0:T(8,128)(2,1)S(1)}, u32[]{:S(2)}, u32[]{:S(2)}) %all-to-all-start.2) | async-done | bytes 786464 | tf_op jit(solution)/shard_map/all_to_all | solution.py:39
  91.6 9.2 %all_to_all.35 = bf16[8,64,128]{2,1,0:T(8,128)(2,1)S(1)} all-to-all(bf16[8,64,128]{2,1,0:T(8,128)(2,1)S(1)} %copy.17), channel_id=1, replica_groups=mesh['x'=4,'core'=2,'z'=4,'y'=4] {'x','core'}, dimensions={0} | all-to-all | bytes 262144 | tf_op jit(solution)/shard_map/all_to_all | solution.py:39
  100.9 8.2 %all_to_all.36 = bf16[8,64,128]{2,1,0:T(8,128)(2,1)S(1)} all-to-all(bf16[8,64,128]{2,1,0:T(8,128)(2,1)S(1)} %broadcast_in_dim.20), channel_id=1, replica_groups=mesh['x'=4,'core'=2,'z'=4,'y'=4] {'x','core'}, dimensions={0} | all-to-all | bytes 262144 | tf_op jit(solution)/shard_map/all_to_all | solution.py:39
  111.3 3.6 %all-to-all-start.5 = ((bf16[16,96,128]{2,1,0:T(8,128)(2,1)}), bf16[16,96,128]{2,1,0:T(8,128)(2,1)S(1)}, u32[]{:S(2)}, u32[]{:S(2)}) async-start(bf16[16,96,128]{2,1,0:T(8,128)(2,1)} %shard_map.126), calls=%async_computation.5 | async-start | bytes 786432 | tf_op jit(solution)/shard_map/all_to_all | solution.py:39
  114.9 2.9 %add_convert_fusion = bf16[8,36,8,128]{3,2,1,0:T(8,128)(2,1)} fusion(bf16[8,36,8,128]{3,2,1,0:T(8,128)(2,1)} %collective-permute-done.11, bf16[8,36,8,128]{3,2,1,0:T(8,128)(2,1)} %copy-done.7, bf16[8,36,8,128]{3,2,1,0:T(8,128)(2,1)} %collective-permute-done.9, bf16[8,36,8,128]{3,2,1,0:T(8,128)(2,1)} %get-tuple-element.81), kind=kLoop, calls=%fused_computation.7 | loop fusion | flops 2359296 | bytes 2949120 | tf_op jit(solution)/shard_map/convert_element_type | solution.py:649
  117.8 6.3 %all-to-all-done.5.in_ref = bf16[16,96,128]{2,1,0:T(8,128)(2,1)S(1)} async-done(((bf16[16,96,128]{2,1,0:T(8,128)(2,1)}), bf16[16,96,128]{2,1,0:T(8,128)(2,1)S(1)}, u32[]{:S(2)}, u32[]{:S(2)}) %all-to-all-start.5) | async-done | bytes 393248 | tf_op jit(solution)/shard_map/all_to_all | solution.py:39
  124.1 6.0 %all-to-all-start.6 = ((bf16[32,9,8,128]{3,2,1,0:T(8,128)(2,1)}), bf16[32,9,8,128]{3,2,1,0:T(8,128)(2,1)}, u32[]{:S(2)}, u32[]{:S(2)}) async-start(bf16[32,9,8,128]{3,2,1,0:T(8,128)(2,1)} %bitcast.56), calls=%async_computation.6 | async-start | bytes 1179648 | tf_op jit(solution)/shard_map/all_to_all | solution.py:39
  130.1 2.2 %fusion.8 = f32[64,1024]{1,0:T(8,128)} fusion(bf16[512,1024]{1,0:T(8,128)(2,1)} %get-tuple-element.95, bf16[512,128]{1,0:T(8,128)(2,1)S(1)} %bitcast.52), kind=kOutput, calls=%fused_computation.15 | convolution fusion | flops 67108864 | bytes 1441792 | tf_op jit(solution)/shard_map/dot_general | solution.py:654
  133.9 2.2 %shard_map.127 = (bf16[64,1024]{1,0:T(8,128)(2,1)}, bf16[64,1024]{1,0:T(8,128)(2,1)}, f32[64,1024]{1,0:T(8,128)}) custom-call(bf16[16,96,128]{2,1,0:T(8,128)(2,1)S(1)} %all-to-all-done.5.in_ref, bf16[64,1024]{1,0:T(8,128)(2,1)S(1)} %bitcast.53, bf16[64,1024]{1,0:T(8,128)(2,1)S(1)} %bitcast.54, bf16[1024,1024]{1,0:T(8,128)(2,1)S(1)} %copy-done, ...), custom_call_target="tpu_custom_call" | custom-call | tf_op jit(solution)/shard_map/pallas_call | solution.py:580
  136.1 5.7 %all-to-all-done.6 = bf16[32,9,8,128]{3,2,1,0:T(8,128)(2,1)} async-done(((bf16[32,9,8,128]{3,2,1,0:T(8,128)(2,1)}), bf16[32,9,8,128]{3,2,1,0:T(8,128)(2,1)}, u32[]{:S(2)}, u32[]{:S(2)}) %all-to-all-start.6) | async-done | bytes 589856 | tf_op jit(solution)/shard_map/all_to_all | solution.py:39
  (77 shorter events, 24.2 us)
Async XLA Ops:
  2.3 13.7 %collective-permute-start.2 = (bf16[2,64,1024]{2,1,0:T(8,128)(2,1)}, bf16[2,64,1024]{2,1,0:T(8,128)(2,1)S(1)}, u32[]{:S(2)}, u32[]{:S(2)}) collective-permute-start(bf16[2,64,1024]{2,1,0:T(8,128)(2,1)} %shard_map.120.refs_0_), channel_id=1, source_target_pairs={{0,96},{32,0},{64,32},{96,64},{1,97},{33,1},{65,33},{97,65},{2,98}... | collective-permute-start | bytes 786440 | tf_op jit(solution)/shard_map/ppermute | solution.py:51
  5.6 12.5 %collective-permute-start.1 = (bf16[2,64,1024]{2,1,0:T(8,128)(2,1)}, bf16[2,64,1024]{2,1,0:T(8,128)(2,1)S(1)}, u32[]{:S(2)}, u32[]{:S(2)}) collective-permute-start(bf16[2,64,1024]{2,1,0:T(8,128)(2,1)} %shard_map.120.refs_0_), channel_id=1, source_target_pairs={{0,64},{32,96},{64,0},{96,32},{1,65},{33,97},{65,1},{97,33},{2,66}... | collective-permute-start | bytes 786440 | tf_op jit(solution)/shard_map/ppermute | solution.py:51
  6.1 15.0 %collective-permute-start = (bf16[2,64,1024]{2,1,0:T(8,128)(2,1)}, bf16[2,64,1024]{2,1,0:T(8,128)(2,1)S(1)}, u32[]{:S(2)}, u32[]{:S(2)}) collective-permute-start(bf16[2,64,1024]{2,1,0:T(8,128)(2,1)} %shard_map.120.refs_0_), channel_id=1, source_target_pairs={{0,32},{32,64},{64,96},{96,0},{1,33},{33,65},{65,97},{97,1},{2,34}... | collective-permute-start | bytes 786440 | tf_op jit(solution)/shard_map/ppermute | solution.py:51
  6.8 7.2 %copy-start.16 = (s32[4]{0:T(128)S(1)}, s32[4]{0:T(128)}, u32[]{:S(2)}) copy-start(s32[4]{0:T(128)} %groups.3) | copy-start | bytes 52
  6.8 7.7 %copy-start.6 = (bf16[2,64,1024]{2,1,0:T(8,128)(2,1)S(1)}, bf16[2,64,1024]{2,1,0:T(8,128)(2,1)}, u32[]{:S(2)}) copy-start(bf16[2,64,1024]{2,1,0:T(8,128)(2,1)} %shard_map.120.refs_0_) | copy-start | bytes 786436
  14.5 16.1 %copy-start.5 = (bf16[512,1152]{1,0:T(8,128)(2,1)S(1)}, bf16[512,1152]{1,0:T(8,128)(2,1)}, u32[]{:S(2)}) copy-start(bf16[512,1152]{1,0:T(8,128)(2,1)} %get-tuple-element.70) | copy-start | bytes 3538948
  14.5 7.2 %collective-permute-start.3 = (bf16[2,64,1024]{2,1,0:T(8,128)(2,1)S(1)}, bf16[2,64,1024]{2,1,0:T(8,128)(2,1)S(1)}, u32[]{:S(2)}, u32[]{:S(2)}) collective-permute-start(bf16[2,64,1024]{2,1,0:T(8,128)(2,1)S(1)} %copy-done.6), channel_id=1, source_target_pairs={{0,16},{16,0},{1,17},{17,1},{2,18},{18,2},{3,19},{19,3},{4,20},{20... | collective-permute-start | bytes 786440 | tf_op jit(solution)/shard_map/ppermute | solution.py:47
  16.0 5.7 %collective-permute-start.6 = (bf16[2,64,1024]{2,1,0:T(8,128)(2,1)S(1)}, bf16[2,64,1024]{2,1,0:T(8,128)(2,1)S(1)}, u32[]{:S(2)}, u32[]{:S(2)}) collective-permute-start(bf16[2,64,1024]{2,1,0:T(8,128)(2,1)S(1)} %collective-permute-done.2.refs_3_), channel_id=1, source_target_pairs={{0,16},{16,0},{1,17},{17,1},{2,18},{18,2},{3,19},{19,3},{4,20},{20... | collective-permute-start | bytes 786440 | tf_op jit(solution)/shard_map/ppermute | solution.py:47
  18.1 3.6 %collective-permute-start.5 = (bf16[2,64,1024]{2,1,0:T(8,128)(2,1)S(1)}, bf16[2,64,1024]{2,1,0:T(8,128)(2,1)S(1)}, u32[]{:S(2)}, u32[]{:S(2)}) collective-permute-start(bf16[2,64,1024]{2,1,0:T(8,128)(2,1)S(1)} %collective-permute-done.1.refs_2_), channel_id=1, source_target_pairs={{0,16},{16,0},{1,17},{17,1},{2,18},{18,2},{3,19},{19,3},{4,20},{20... | collective-permute-start | bytes 786440 | tf_op jit(solution)/shard_map/ppermute | solution.py:47
  21.2 1.7 %collective-permute-start.4 = (bf16[2,64,1024]{2,1,0:T(8,128)(2,1)S(1)}, bf16[2,64,1024]{2,1,0:T(8,128)(2,1)S(1)}, u32[]{:S(2)}, u32[]{:S(2)}) collective-permute-start(bf16[2,64,1024]{2,1,0:T(8,128)(2,1)S(1)} %collective-permute-done.refs_1_), channel_id=1, source_target_pairs={{0,16},{16,0},{1,17},{17,1},{2,18},{18,2},{3,19},{19,3},{4,20},{20... | collective-permute-start | bytes 786440 | tf_op jit(solution)/shard_map/ppermute | solution.py:47
  30.6 27.1 %collective-permute-start.7 = (bf16[512,1152]{1,0:T(8,128)(2,1)S(1)}, bf16[512,1152]{1,0:T(8,128)(2,1)S(1)}, u32[]{:S(2)}, u32[]{:S(2)}) collective-permute-start(bf16[512,1152]{1,0:T(8,128)(2,1)S(1)} %copy-done.5), channel_id=1, source_target_pairs={{0,16},{16,0},{1,17},{17,1},{2,18},{18,2},{3,19},{19,3},{4,20},{20... | collective-permute-start | bytes 3538952 | tf_op jit(solution)/shard_map/ppermute | solution.py:47
  31.1 18.3 %all-to-all-start = ((f32[128,1,256]{2,1,0:T(1,128)}), f32[128,1,256]{2,1,0:T(1,128)S(1)}, u32[]{:S(2)}, u32[]{:S(2)}) async-start(f32[128,1,256]{2,1,0:T(1,128)} %get-tuple-element.64), calls=%async_computation | async-start | bytes 262144 | tf_op jit(solution)/shard_map/all_to_all | solution.py:39
  50.3 14.2 %all-to-all-start.1 = ((f32[128,1,256]{2,1,0:T(1,128)}), f32[128,1,256]{2,1,0:T(1,128)S(1)}, u32[]{:S(2)}, u32[]{:S(2)}) async-start(f32[128,1,256]{2,1,0:T(1,128)} %shard_map.122), calls=%async_computation.1 | async-start | bytes 262144 | tf_op jit(solution)/shard_map/all_to_all | solution.py:39
  72.0 4.2 %collective-permute-start.8 = (bf16[512,1024]{1,0:T(8,128)(2,1)}, bf16[512,1024]{1,0:T(8,128)(2,1)S(1)}, u32[]{:S(2)}, u32[]{:S(2)}) collective-permute-start(bf16[512,1024]{1,0:T(8,128)(2,1)} %get-tuple-element.80), channel_id=1, source_target_pairs={{0,16},{16,0},{1,17},{17,1},{2,18},{18,2},{3,19},{19,3},{4,20},{20... | collective-permute-start | bytes 3145736 | tf_op jit(solution)/shard_map/ppermute | solution.py:47
  72.5 18.4 %all-to-all-start.2 = ((bf16[16,3,64,128]{3,2,1,0:T(8,128)(2,1)}), bf16[16,3,64,128]{3,2,1,0:T(8,128)(2,1)S(1)}, u32[]{:S(2)}, u32[]{:S(2)}) async-start(bf16[16,3,64,128]{3,2,1,0:T(8,128)(2,1)} %get-tuple-element.84), calls=%async_computation.2 | async-start | bytes 1572864 | tf_op jit(solution)/shard_map/all_to_all | solution.py:39
  82.7 26.4 %copy-start.2 = (bf16[512,1024]{1,0:T(8,128)(2,1)S(1)}, bf16[512,1024]{1,0:T(8,128)(2,1)}, u32[]{:S(2)}) copy-start(bf16[512,1024]{1,0:T(8,128)(2,1)} %get-tuple-element.85.latents_ref) | copy-start | bytes 3145732
  82.7 27.7 %collective-permute-start.10 = (bf16[8,36,8,128]{3,2,1,0:T(8,128)(2,1)S(1)}, bf16[8,36,8,128]{3,2,1,0:T(8,128)(2,1)S(1)}, u32[]{:S(2)}, u32[]{:S(2)}) collective-permute-start(bf16[8,36,8,128]{3,2,1,0:T(8,128)(2,1)S(1)} %get-tuple-element.86), channel_id=1, source_target_pairs={{0,8},{4,12},{8,0},{12,4},{1,9},{5,13},{9,1},{13,5},{2,10},{6,14},... | collective-permute-start | bytes 1769480 | tf_op jit(solution)/shard_map/ppermute | solution.py:51
  85.5 29.4 %collective-permute-start.11 = (bf16[8,36,8,128]{3,2,1,0:T(8,128)(2,1)}, bf16[8,36,8,128]{3,2,1,0:T(8,128)(2,1)}, u32[]{:S(2)}, u32[]{:S(2)}) collective-permute-start(bf16[8,36,8,128]{3,2,1,0:T(8,128)(2,1)} %get-tuple-element.88), channel_id=1, source_target_pairs={{0,12},{4,0},{8,4},{12,8},{1,13},{5,1},{9,5},{13,9},{2,14},{6,2},{... | collective-permute-start | bytes 1769480 | tf_op jit(solution)/shard_map/ppermute | solution.py:51
  86.4 28.5 %collective-permute-start.9 = (bf16[8,36,8,128]{3,2,1,0:T(8,128)(2,1)}, bf16[8,36,8,128]{3,2,1,0:T(8,128)(2,1)}, u32[]{:S(2)}, u32[]{:S(2)}) collective-permute-start(bf16[8,36,8,128]{3,2,1,0:T(8,128)(2,1)} %get-tuple-element.82), channel_id=1, source_target_pairs={{0,4},{4,8},{8,12},{12,0},{1,5},{5,9},{9,13},{13,1},{2,6},{6,10},{... | collective-permute-start | bytes 1769480 | tf_op jit(solution)/shard_map/ppermute | solution.py:51
  111.3 12.8 %all-to-all-start.5 = ((bf16[16,96,128]{2,1,0:T(8,128)(2,1)}), bf16[16,96,128]{2,1,0:T(8,128)(2,1)S(1)}, u32[]{:S(2)}, u32[]{:S(2)}) async-start(bf16[16,96,128]{2,1,0:T(8,128)(2,1)} %shard_map.126), calls=%async_computation.5 | async-start | bytes 786432 | tf_op jit(solution)/shard_map/all_to_all | solution.py:39
  114.8 17.5 %copy-start = (bf16[1024,1024]{1,0:T(8,128)(2,1)S(1)}, bf16[1024,1024]{1,0:T(8,128)(2,1)}, u32[]{:S(2)}) copy-start(bf16[1024,1024]{1,0:T(8,128)(2,1)} %w_query_ref.1) | copy-start | bytes 6291460
  114.9 17.5 %copy-start.3 = (bf16[1,64,1024]{2,1,0:T(8,128)(2,1)S(1)}, bf16[1,64,1024]{2,1,0:T(8,128)(2,1)}, u32[]{:S(2)}) copy-start(bf16[1,64,1024]{2,1,0:T(8,128)(2,1)} %first_ref.1) | copy-start | bytes 393220
  114.9 17.5 %copy-start.4 = (bf16[1,64,1024]{2,1,0:T(8,128)(2,1)S(1)}, bf16[1,64,1024]{2,1,0:T(8,128)(2,1)}, u32[]{:S(2)}) copy-start(bf16[1,64,1024]{2,1,0:T(8,128)(2,1)} %second_ref.1) | copy-start | bytes 393220
  124.1 17.7 %all-to-all-start.6 = ((bf16[32,9,8,128]{3,2,1,0:T(8,128)(2,1)}), bf16[32,9,8,128]{3,2,1,0:T(8,128)(2,1)}, u32[]{:S(2)}, u32[]{:S(2)}) async-start(bf16[32,9,8,128]{3,2,1,0:T(8,128)(2,1)} %bitcast.56), calls=%async_computation.6 | async-start | bytes 1179648 | tf_op jit(solution)/shard_map/all_to_all | solution.py:39
  (10 other events, 20.6 us)
